TPU v7x, 128 devices: a whole 4x4x4 slice. The times are simulated.
128 devices in a mesh: band: 4 (over z_hi, core), mem: 32 (over y, x, z_lo).
Axes of the slice: x: 4, y: 4, z: 4 (z_hi: 2, z_lo: 2; z = z_hi * 2 + z_lo), core: 2. Of those that a mesh axis runs over, the one named last changes fastest.
Arguments:
- members: bfloat16 [64, 16, 32768], P('band', None, 'mem'), may hold values from -6 to 6
- eigvecs: bfloat16 [112, 16, 32768], P('band', None, 'mem'), may hold values from -6 to 6
- control: float32 [112, 64], replicated, may hold values from -6 to 6
- columns: int32 [2048, 16], P('mem'), may hold values from 0 to 1023
- interpolation: bfloat16 [2048, 256, 512], P('mem'), may hold values from -0.375 to 0.375
- owners: int32 [2048], replicated, may hold values from 0 to 31, as said below
- innovation: float32 [32, 256, 512], P('mem'), may hold values from -6 to 6
- obs_weight: float32 [32, 256, 512], P('mem'), may hold values from 0.25 to 4
Outputs:
- gradient: float32 [112, 64], P(None, 'band')
- departures: float32 [32, 256, 512], P('mem', None, 'band')
Inputs may be any that keep to these rules, and one draw needn't show every extreme that they name: `owners`: one tile sends at most 8 of its blocks to one owner, and some owner holds exactly 8 blocks from every tile.
All inputs are finite; a program needn't handle non-finite values.
Results may differ from a plain program's by a relative error of at most 0.0032.
Values may be sent and summed in bfloat16 or wider, within the bound.
No kernel may reach another device: no remote copies, remote signals or barrier semaphores. Data moves between devices by JAX's collectives and lax.ppermute only.
A program may use at most 64 MiB of HBM per device.

v0:
```python
import math

import jax
import jax.numpy as jnp
from jax import lax
from jax.sharding import PartitionSpec as P


def per_device(members, eigvecs, control, columns, interpolation, owners, innovation, obs_weight):
    nband = lax.axis_size("band")
    tiles = lax.axis_size("mem")
    band_idx = lax.axis_index("band")
    tile_idx = lax.axis_index("mem")
    mem_dev, levels, tile_cols = members.shape
    blocks, patch = columns.shape
    obs_block = interpolation.shape[2]
    capacity = innovation.shape[1] // tiles
    modes, total_members = control.shape
    scale = 1.0 / math.sqrt(modes * total_members)
    control_b = control.astype(jnp.bfloat16)
    contract_first = (((0,), (0,)), ((), ()))
    contract_second = (((1,), (1,)), ((), ()))
    all_modes = lax.all_gather(eigvecs, "band", axis=0, tiled=True).reshape(modes, -1)
    weight_cols = lax.dynamic_slice_in_dim(control_b, band_idx * mem_dev, mem_dev, 1)
    mixed = lax.dot_general(
        weight_cols, all_modes, contract_first, preferred_element_type=jnp.float32
    )
    partial_field = scale * jnp.sum(members.reshape(mem_dev, -1) * mixed, axis=0)
    increment = lax.psum(partial_field, "band")
    increment_b = increment.reshape(levels, tile_cols).astype(jnp.bfloat16)
    picked = jnp.take(increment_b, columns.reshape(-1), axis=1).reshape(levels, blocks, patch)
    picked = jnp.transpose(picked, (1, 0, 2)).reshape(blocks, levels * patch)
    quarter = obs_block // nband
    innov_part = innovation[0]
    weight_part = obs_weight[0]
    image = jnp.einsum("jr,jro->jo", picked, interpolation, preferred_element_type=jnp.float32)
    local_owner = lax.dynamic_slice_in_dim(owners, tile_idx * blocks, blocks, 0)
    order = jnp.arange(blocks, dtype=jnp.int32)
    earlier = order[None, :] < order[:, None]
    same = local_owner[:, None] == local_owner[None, :]
    rank = jnp.sum(jnp.logical_and(same, earlier), axis=1)
    target = local_owner * capacity + rank
    placing = jnp.arange(tiles * capacity, dtype=jnp.int32)[:, None] == target[None, :]
    send = jnp.dot(placing.astype(jnp.float32), image, precision=lax.Precision.HIGHEST)
    arrived = lax.all_to_all(
        send.reshape(tiles, capacity, obs_block), "mem", split_axis=0, concat_axis=0, tiled=True
    )
    arrived = arrived.reshape(tiles * capacity, obs_block)
    counts = jnp.sum(owners.reshape(tiles, blocks) == tile_idx, axis=1)
    live = (jnp.arange(capacity)[None, :] < counts[:, None]).reshape(-1).astype(jnp.float32)
    departure = live[:, None] * weight_part * (innov_part - arrived)
    departure_b = departure.astype(jnp.bfloat16).reshape(tiles, capacity, obs_block)
    returned = lax.all_to_all(departure_b, "mem", split_axis=0, concat_axis=0, tiled=True).reshape(
        tiles * capacity, obs_block
    )
    own_back = jnp.dot(
        placing.T.astype(jnp.bfloat16), returned, preferred_element_type=jnp.float32
    ).astype(jnp.bfloat16)
    spread = jnp.einsum("jro,jo->jr", interpolation, own_back, preferred_element_type=jnp.float32)
    spread = jnp.transpose(spread.reshape(blocks, levels, patch), (1, 0, 2)).reshape(
        levels, blocks * patch
    )
    selector = (
        columns.reshape(-1)[:, None] == jnp.arange(tile_cols, dtype=jnp.int32)[None, :]
    ).astype(jnp.float32)
    adjoint = jnp.dot(spread, selector, precision=lax.Precision.HIGHEST)
    out_departure = lax.dynamic_slice_in_dim(departure, band_idx * quarter, quarter, 1)
    adjoint_flat = adjoint.reshape(-1)
    weighted = (members.reshape(mem_dev, -1) * adjoint_flat).astype(jnp.bfloat16)
    local_grad = lax.dot_general(
        all_modes, weighted, contract_second, preferred_element_type=jnp.float32
    )
    summed = lax.psum(local_grad, "mem")
    own_control = lax.dynamic_slice_in_dim(control, band_idx * mem_dev, mem_dev, 1)
    gradient = own_control - scale * summed
    return (gradient, out_departure[None])


def solution(mesh):
    return jax.shard_map(
        per_device,
        mesh=mesh,
        in_specs=(
            P("band", None, "mem"),
            P("band", None, "mem"),
            P(),
            P("mem", None),
            P("mem", None, None),
            P(),
            P("mem", None, None),
            P("mem", None, None),
        ),
        out_specs=(P(None, "band"), P("mem", None, "band")),
        check_vma=False,
    )
```

profile of v0, /device:TPU:0, one launch (start us, length us, event | category | flops | bytes accessed | tf_op | source)
XLA Modules:
  0.0 221.5 jit_solution(8201161495989091202)
XLA Ops:
  7.2 0.7 all-gather.2.cloned.1.call-update
  7.9 1.4 copy.39
  9.3 0.8 copy.28
  10.1 0.8 dynamic_slice.13
  11.1 0.8 multiply_add_fusion
  11.9 0.7 compare_and_fusion
  12.6 35.3 %all-gather.2.cloned.1.call-done = bf16[112,16,1024]{2,1,0:T(8,128)(2,1)} async-done(((bf16[28,16,1024]{2,1,0:T(8,128)(2,1)}), bf16[112,16,1024]{2,1,0:T(8,128)(2,1)}) %all-gather.2.cloned.1.call-update) | async-done | bytes 3670032 | tf_op jit(solution)/shard_map/all_gather | solution.py:23
  47.9 4.4 %copy.40 = bf16[14,8,16,1024]{3,1,2,0:T(8,128)(2,1)S(1)} copy(bf16[14,8,16,1024]{3,2,1,0:T(8,128)(2,1)} %bitcast.55) | data formatting | bytes 7340032
  52.3 1.3 fusion.4
  53.6 13.9 %psum.14 = bf16[16384]{0:T(1024)(128)(2,1)S(1)} all-reduce(f32[16384]{0:T(1024)S(1)} %broadcast_multiply_fusion), channel_id=1, replica_groups=mesh['band'=4,'mem'=32] {'band'}, use_global_device_ids=true, to_apply=%region_3.4 | all-reduce | flops 16384 | bytes 98304 | tf_op jit(solution)/shard_map/psum | solution.py:29
  67.7 3.2 %gather_fusion = bf16[1024,16]{1,0:T(8,128)(2,1)S(1)} fusion(bf16[16,1024]{0,1:T(8,128)(2,1)S(1)} %copy.29, s32[1024]{0:T(1024)S(1)} %broadcast_clamp_fusion), kind=kCustom, calls=%fused_computation | custom fusion | bytes 69632 | tf_op jit(solution)/shard_map/jit(_take)/gather | solution.py:31
  71.4 8.1 %fusion.24 = f32[64,1,512]{2,1,0:T(1,128)S(1)} fusion(bf16[64,256,1]{1,2,0:T(2,128)(2,1)S(1)} %copy.35, bf16[64,256,512]{2,1,0:T(8,128)(2,1)} %param.12), kind=kOutput, calls=%fused_computation.46 | convolution fusion | flops 16777216 | bytes 16941056 | tf_op jit(solution)/shard_map/jr,jro->jo/dot_general | solution.py:36
  79.5 1.2 convolution_bitcast_fusion
  80.7 8.1 %all-to-all-start = ((f32[32,8,512]{2,1,0:T(8,128)}), f32[32,8,512]{2,1,0:T(8,128)S(1)}, u32[]{:S(2)}, u32[]{:S(2)}) async-start(f32[32,8,512]{2,1,0:T(8,128)} %convolution_bitcast_fusion), calls=%async_computation | async-start | bytes 1048576 | tf_op jit(solution)/shard_map/all_to_all | solution.py:45
  89.0 11.2 %all-to-all-done = f32[32,8,512]{2,1,0:T(8,128)S(1)} async-done(((f32[32,8,512]{2,1,0:T(8,128)}), f32[32,8,512]{2,1,0:T(8,128)S(1)}, u32[]{:S(2)}, u32[]{:S(2)}) %all-to-all-start) | async-done | bytes 524320 | tf_op jit(solution)/shard_map/all_to_all | solution.py:45
  100.3 0.8 fusion.10
  101.1 4.0 %all-to-all-start.1 = ((bf16[32,8,512]{2,1,0:T(8,128)(2,1)}), bf16[32,8,512]{2,1,0:T(8,128)(2,1)S(1)}, u32[]{:S(2)}, u32[]{:S(2)}) async-start(bf16[32,8,512]{2,1,0:T(8,128)(2,1)} %fusion.10), calls=%async_computation.1 | async-start | bytes 524288 | tf_op jit(solution)/shard_map/all_to_all | solution.py:53
  105.3 0.8 fusion.14
  106.1 8.3 %all-to-all-done.1 = bf16[32,8,512]{2,1,0:T(8,128)(2,1)S(1)} async-done(((bf16[32,8,512]{2,1,0:T(8,128)(2,1)}), bf16[32,8,512]{2,1,0:T(8,128)(2,1)S(1)}, u32[]{:S(2)}, u32[]{:S(2)}) %all-to-all-start.1) | async-done | bytes 262176 | tf_op jit(solution)/shard_map/all_to_all | solution.py:53
  114.6 10.2 %fusion.16 = f32[64,1,256]{2,1,0:T(1,128)S(1)} fusion(bf16[64,256,512]{2,1,0:T(8,128)(2,1)} %param.12, bf16[64,512,1]{1,0,2:T(8,128)(2,1)S(1)} %fusion.5), kind=kOutput, calls=%fused_computation.24 | convolution fusion | flops 16777216 | bytes 16908288 | tf_op jit(solution)/shard_map/jro,jo->jr/dot_general | solution.py:59
  125.5 1.5 fusion
  127.1 6.5 %fusion.6 = f32[112,16]{0,1:T(8,128)S(1)} fusion(bf16[112,16,1024]{2,1,0:T(8,128)(2,1)} %all-gather.2.cloned.1.call-done, bf16[16,16,1024]{2,1,0:T(8,128)(2,1)S(1)} %multiply_convert_fusion), kind=kOutput, calls=%fused_computation.11 | convolution fusion | flops 58720256 | bytes 4201472 | tf_op jit(solution)/shard_map/dot_general | solution.py:70
  133.5 79.8 %psum.15 = f32[112,16]{0,1:T(8,128)S(1)} all-reduce(f32[112,16]{0,1:T(8,128)S(1)} %fusion.6), channel_id=1, replica_groups=mesh['band'=4,'mem'=32] {'mem'}, use_global_device_ids=true, to_apply=%region_4.5 | all-reduce | flops 1792 | bytes 14336 | tf_op jit(solution)/shard_map/psum | solution.py:73
  213.3 1.3 multiply_subtract_fusion
  (30 shorter events, 2.3 us)
Async XLA Ops:
  7.2 40.7 %all-gather.2.cloned.1.call-start = ((), (), s32[]{:S(2)}) async-start(), calls=%async_computation.2 | async-start | bytes 4587520 | tf_op jit(solution)/shard_map/all_gather | solution.py:23
  71.3 17.4 %copy-start.3 = (s32[2048]{0:T(1024)S(1)}, s32[2048]{0:T(1024)}, u32[]{:S(2)}) copy-start(s32[2048]{0:T(1024)} %param.13) | copy-start | bytes 24580
  71.3 28.9 %copy-start.1 = (f32[1,256,512]{2,1,0:T(8,128)S(1)}, f32[1,256,512]{2,1,0:T(8,128)}, u32[]{:S(2)}) copy-start(f32[1,256,512]{2,1,0:T(8,128)} %param.14) | copy-start | bytes 1572868
  71.3 28.9 %copy-start.2 = (f32[1,256,512]{2,1,0:T(8,128)S(1)}, f32[1,256,512]{2,1,0:T(8,128)}, u32[]{:S(2)}) copy-start(f32[1,256,512]{2,1,0:T(8,128)} %param.15) | copy-start | bytes 1572868
  80.7 19.6 %all-to-all-start = ((f32[32,8,512]{2,1,0:T(8,128)}), f32[32,8,512]{2,1,0:T(8,128)S(1)}, u32[]{:S(2)}, u32[]{:S(2)}) async-start(f32[32,8,512]{2,1,0:T(8,128)} %convolution_bitcast_fusion), calls=%async_computation | async-start | bytes 1048576 | tf_op jit(solution)/shard_map/all_to_all | solution.py:45
  101.1 13.3 %all-to-all-start.1 = ((bf16[32,8,512]{2,1,0:T(8,128)(2,1)}), bf16[32,8,512]{2,1,0:T(8,128)(2,1)S(1)}, u32[]{:S(2)}, u32[]{:S(2)}) async-start(bf16[32,8,512]{2,1,0:T(8,128)(2,1)} %fusion.10), calls=%async_computation.1 | async-start | bytes 524288 | tf_op jit(solution)/shard_map/all_to_all | solution.py:53
  114.6 12.3 %copy-start = (bf16[16,16,1024]{2,1,0:T(8,128)(2,1)S(1)}, bf16[16,16,1024]{2,1,0:T(8,128)(2,1)}, u32[]{:S(2)}) copy-start(bf16[16,16,1024]{2,1,0:T(8,128)(2,1)} %param.8) | copy-start | bytes 1572868
Sparse Core Ops, SparseCore 0:
  9.7 38.1 all-gather.1
where the time goes:
time: 222 us; the launch traced here: 221 us
  blocking collectives  93.7 us (42%)
  waiting for transfers between devices  55.5 us (25%)
  matrix products  29 us (13%)
  between operations  14.2 us (6%)
  starting transfers between devices  12.2 us (5%)
  local copies, waits for them, and re-layouts  12 us (5%)
  other arithmetic  4.9 us (2%)
    psum x1, blocking collectives, per_device(): summed = lax.psum(local_grad, 'mem')  79.8 us
    all_gather x1, waiting for transfers between devices, per_device(): lax.all_gather(eigvecs, 'band', axis=0, tiled=True).reshape(modes, -1)  35.3 us
    psum x1, blocking collectives, per_device(): increment = lax.psum(partial_field, 'band')  13.9 us
    all_to_all x1, waiting for transfers between devices, per_device(): lax.all_to_all(send.reshape(tiles, capacity, obs_block), 'mem', split_axi...  11.2 us
    dot_general x1, matrix products, per_device(): jnp.einsum('jro,jo->jr', interpolation, own_back, preferred_element_type=...  10.2 us
    all_to_all x1, waiting for transfers between devices, per_device(): lax.all_to_all(departure_b, 'mem', split_axis=0, concat_axis=0, tiled=True)  8.31 us
    dot_general x1, matrix products, per_device(): jnp.einsum('jr,jro->jo', picked, interpolation, preferred_element_type=jn...  8.12 us
    all_to_all x1, starting transfers between devices, per_device(): lax.all_to_all(send.reshape(tiles, capacity, obs_block), 'mem', split_axi...  8.07 us
  transfers between devices with their start and end apart: 3, of which 3 were waited for; matrix products, arithmetic and copies ran while one was open for 3% of the time, Pallas kernels for 0%

commit v1 on v0

v1 whole, which is shorter than its diff:
```python
import math

import jax
import jax.numpy as jnp
from jax import lax
from jax.experimental import pallas as pl
from jax.experimental.pallas import tpu as pltpu
from jax.sharding import PartitionSpec as P

BF = jnp.bfloat16
F32 = jnp.float32
NN = (((1,), (0,)), ((), ()))
NT = (((1,), (1,)), ((), ()))
TN = (((0,), (0,)), ((), ()))
MIB = 1024 * 1024


def dot(a, b, dims=NN):
    return lax.dot_general(a, b, dims, preferred_element_type=F32)


def parts3(x):
    hi = x.astype(BF)
    rest = x - hi.astype(F32)
    mid = rest.astype(BF)
    lo = (rest - mid.astype(F32)).astype(BF)
    return hi, mid, lo


def iota(shape, dim):
    return lax.broadcasted_iota(jnp.int32, shape, dim)


def call(body, outs, n_smem, n_vmem, flops, nbytes, scratch=(), vmem=16):
    return pl.pallas_call(
        body,
        out_shape=outs,
        in_specs=[pl.BlockSpec(memory_space=pltpu.SMEM)] * n_smem
        + [pl.BlockSpec(memory_space=pltpu.VMEM)] * n_vmem,
        out_specs=jax.tree.map(lambda _: pl.BlockSpec(memory_space=pltpu.VMEM), outs),
        scratch_shapes=list(scratch),
        compiler_params=pltpu.CompilerParams(vmem_limit_bytes=vmem * MIB),
        cost_estimate=pl.CostEstimate(flops=flops, bytes_accessed=nbytes, transcendentals=0),
    )


def shape(dims, dtype):
    return jax.ShapeDtypeStruct(dims, dtype)


def prep_body(meta, control, columns, owners, kron, onehot, place):
    band = meta[0]
    tile = meta[1]
    row = iota((448, 112), 0)
    second = (row >= 224).astype(jnp.int32)
    mode = (band ^ second) * 28 + ((row - 224 * second) >> 3)
    pick_rows = (mode == iota((448, 112), 1)).astype(F32).astype(BF)
    col = iota((64, 512), 1)
    member = (band ^ (col >> 7)) * 16 + ((col & 127) >> 3)
    pick_cols = (member == iota((64, 512), 0)).astype(F32).astype(BF)
    rows = dot(pick_rows, control[...].astype(BF)).astype(BF)
    full = dot(rows, pick_cols)
    same = (iota((448, 512), 0) & 7) == (iota((448, 512), 1) & 7)
    kron[...] = jnp.where(same, full, 0.0).astype(BF)
    t = iota((64, 1024), 1)
    cols = columns[...]
    for c in range(16):
        onehot[c * 64:(c + 1) * 64, :] = (cols[:, c:c + 1] == t).astype(F32).astype(BF)
    own_row = jnp.broadcast_to(owners[pl.ds(tile, 1), :].astype(F32), (64, 64))
    own_col = own_row.T
    earlier = iota((64, 64), 1) < iota((64, 64), 0)
    rank = jnp.sum(jnp.where((own_row == own_col) & earlier, 1.0, 0.0), axis=1, keepdims=True)
    target = (own_col[:, :1] * 8.0 + rank).astype(jnp.int32)
    place[...] = (target == iota((64, 256), 1)).astype(F32).astype(BF)


def select_body(place, got, innov, weight):
    x = got[...]
    sel = place[...]
    for out, a in ((innov, x[:, :8].reshape(256, 128)), (weight, x[:, 8:].reshape(256, 128))):
        hi, mid, lo = parts3(a)
        out[...] = dot(sel, hi) + dot(sel, mid) + dot(sel, lo)


def increment_body(scale, kron, m0, m1, m2, m3, e0, e1, out):
    for g in range(0, 1024, 256):
        cut = slice(g, g + 256)
        mixed = None
        for p, m in enumerate((m0, m1, m2, m3)):
            term = dot(kron[:, p * 128:(p + 1) * 128], m[:, cut])
            mixed = term if mixed is None else mixed + term
        total = jnp.sum((mixed[:224] * e0[:, cut].astype(F32)).reshape(28, 8, 256), axis=0)
        total = total + jnp.sum((mixed[224:] * e1[:, cut].astype(F32)).reshape(28, 8, 256), axis=0)
        out[:, cut] = total * scale


def obs_body(meta, inc_my, inc_mt, onehot, place, innov, weight, interp, adj_my, adj_mt, slots, picked, depb, spread):
    first = (meta[0] & 1) == 0
    mine = inc_my[...].astype(F32)
    mate = inc_mt[...].astype(F32)
    inc = jnp.concatenate([jnp.where(first, mine, mate), jnp.where(first, mate, mine)], axis=0).astype(BF)
    picks = dot(onehot[...], inc, NT)
    by_col = jnp.concatenate([picks[c * 64:(c + 1) * 64] for c in range(16)], axis=1).astype(BF)
    r0 = iota((256, 256), 0)
    r1 = iota((256, 256), 1)
    swap = (((r0 & 15) * 16 + (r0 >> 4)) == r1).astype(F32).astype(BF)
    picked[...] = dot(by_col, swap).astype(BF)
    rows = iota((16, 128), 0)
    rows2 = iota((16, 256), 0)
    image = []
    for b in range(4):
        lhs = picked[b * 16:(b + 1) * 16, :]
        acc = jnp.zeros((16, 128), F32)
        for i in range(16):
            acc = jnp.where(rows == i, dot(lhs, interp[b * 16 + i]), acc)
        image.append(acc)
    image = jnp.concatenate(image, axis=0)
    dep = weight[...] * (innov[...] - image)
    depb[...] = dep.astype(BF)
    for b in range(4):
        lhs = depb[b * 16:(b + 1) * 16, :]
        acc = jnp.zeros((16, 256), F32)
        for i in range(16):
            acc = jnp.where(rows2 == i, dot(lhs, interp[b * 16 + i], NT), acc)
        spread[b * 16:(b + 1) * 16, :] = acc
    x = spread[...]
    hi = x.astype(BF)
    lo = (x - hi.astype(F32)).astype(BF)
    terms = []
    for part in (hi, lo):
        turned = dot(swap, part, NT)
        terms.append(jnp.concatenate([turned[c * 16:(c + 1) * 16] for c in range(16)], axis=1))
    both = dot(jnp.concatenate(terms, axis=0).astype(BF), onehot[...])
    adj = both[:16] + both[16:]
    adj_my[...] = jnp.where(first, adj[:8], adj[8:])
    adj_mt[...] = jnp.where(first, adj[8:], adj[:8])
    sel = place[...]
    hi, mid, lo = parts3(dep)
    slots[...] = dot(sel, hi, TN) + dot(sel, mid, TN) + dot(sel, lo, TN)


def gradient_body(a0, a1, m0, m1, m2, m3, e0, e1, out_my, out_mt):
    adj = a0[...] + a1[...]
    wide = jnp.broadcast_to(adj[None], (16, 8, 1024)).reshape(128, 1024)
    same = (iota((224, 128), 0) & 7) == (iota((224, 128), 1) & 7)
    tops, lows = [], []
    for m in (m0, m1, m2, m3):
        weighted = (m[...].astype(F32) * wide).astype(BF)
        for e, side in ((e0, tops), (e1, lows)):
            full = jnp.where(same, dot(e[...], weighted, NT), 0.0)
            side.append(jnp.sum(full.reshape(28, 8, 128), axis=1))
    sel = ((iota((256, 32), 0) >> 3) == iota((256, 32), 1)).astype(F32).astype(BF)
    for out, p, q in ((out_my, 0, 2), (out_mt, 1, 3)):
        x = jnp.concatenate([
            jnp.concatenate([tops[p], tops[q]], axis=1),
            jnp.concatenate([lows[p], lows[q]], axis=1),
        ], axis=0)
        hi, mid, lo = parts3(x)
        out[...] = dot(hi, sel) + dot(mid, sel) + dot(lo, sel)


def pack_body(keep, came, slots, out):
    full = jnp.concatenate([keep[...], came[...]], axis=0)
    flat = jnp.concatenate(
        [full[i * 16:(i + 1) * 16] for i in range(7)] + [jnp.zeros((16, 16), F32)], axis=1
    )
    out[:, :8, :] = slots[...].reshape(32, 8, 128)
    out[:, 8:, :] = jnp.broadcast_to(flat[None], (32, 16, 128))


def final_body(scale, meta, got, control, gradient, departures):
    band = meta[0]
    departures[...] = got[:, :8, :].reshape(1, 256, 128)
    flat = jnp.sum(got[:, 8:, :], axis=0)
    total = jnp.concatenate([flat[:, i * 16:(i + 1) * 16] for i in range(7)], axis=0)
    r = iota((112, 112), 0)
    block = (r >= 28).astype(jnp.int32) + (r >= 56).astype(jnp.int32) + (r >= 84).astype(jnp.int32)
    source = (band ^ block) * 28 + (r - 28 * block)
    order = (source == iota((112, 112), 1)).astype(F32).astype(BF)
    hi, mid, lo = parts3(total)
    total = dot(order, hi) + dot(order, mid) + dot(order, lo)
    own = (iota((64, 16), 0) == band * 16 + iota((64, 16), 1)).astype(F32).astype(BF)
    hi, mid, lo = parts3(control[...])
    mine = dot(hi, own) + dot(mid, own) + dot(lo, own)
    gradient[...] = mine - scale * total


def per_device(members, eigvecs, control, columns, interpolation, owners, innovation, obs_weight):
    band = lax.axis_index("band")
    tile = lax.axis_index("mem")
    core = band & 1
    scale = 1.0 / math.sqrt(112 * 64)
    meta = jnp.stack([band, tile]).astype(jnp.int32)

    def over(x, bit):
        return lax.ppermute(x, "band", [(i, i ^ bit) for i in range(4)])

    def half(x, which):
        return lax.dynamic_slice_in_dim(x, which * 8, 8, 1).reshape(-1, 1024)

    m_mt = half(members, 1 - core)
    m_my = half(members, core)
    m3 = over(m_mt, 3)
    m2 = over(m_my, 2)
    e_mt = half(eigvecs, 1 - core)
    m1 = over(m_mt, 1)
    e1 = over(e_mt, 1)
    e0 = half(eigvecs, core)

    quarter = lambda x, d: lax.dynamic_slice_in_dim(x, band * 128, 128, d)
    sent = jnp.concatenate(
        [quarter(innovation[0], 1).reshape(32, 8, 128), quarter(obs_weight[0], 1).reshape(32, 8, 128)], axis=1
    )
    got = lax.all_to_all(sent, "mem", split_axis=0, concat_axis=0, tiled=True)
    interp = quarter(interpolation, 2)

    kron, onehot, place = call(
        prep_body,
        (shape((448, 512), BF), shape((1024, 1024), BF), shape((64, 256), BF)),
        1, 3, 10 ** 8, 3 * 10 ** 6,
    )(meta, control, columns, owners.reshape(32, 64))
    innov, weight = call(
        select_body, (shape((64, 128), F32), shape((64, 128), F32)), 0, 2, 10 ** 7, 4 * 10 ** 5
    )(place, got)

    part = call(
        lambda *refs: increment_body(scale, *refs), shape((8, 1024), F32), 0, 7, 5 * 10 ** 8, 2 * 10 ** 6
    )(kron, m_my, m1, m2, m3, e0, e1)
    inc_my = (part + over(part, 2)).astype(BF)
    inc_mt = over(inc_my, 1)

    adj_my, adj_mt, slots = call(
        obs_body,
        (shape((8, 1024), F32), shape((8, 1024), F32), shape((256, 128), F32)),
        1, 7, 10 ** 9, 8 * 10 ** 6,
        scratch=(pltpu.VMEM((64, 256), BF), pltpu.VMEM((64, 128), BF), pltpu.VMEM((64, 256), F32)),
    )(meta, inc_my, inc_mt, onehot, place, innov, weight, interp)
    adj = adj_my + over(adj_mt, 1)

    g_my, g_mt = call(
        gradient_body, (shape((56, 32), F32), shape((56, 32), F32)), 0, 8, 5 * 10 ** 8, 2 * 10 ** 6
    )(adj, over(adj, 2), m_my, m1, m2, m3, e0, e1)
    came = over(g_mt, 1)
    both = g_my + jnp.concatenate([came[28:], came[:28]], axis=0)
    other = over(both[:, 16:], 2)

    payload = call(pack_body, shape((32, 24, 128), F32), 0, 3, 10 ** 5, 6 * 10 ** 5)(both[:, :16], other, slots)
    arrived = lax.all_to_all(payload, "mem", split_axis=0, concat_axis=0, tiled=True)
    gradient, departures = call(
        lambda *refs: final_body(scale, *refs), (shape((112, 16), F32), shape((1, 256, 128), F32)),
        1, 2, 10 ** 6, 6 * 10 ** 5,
    )(meta, arrived, control)
    return (gradient, departures)


def solution(mesh):
    return jax.shard_map(
        per_device,
        mesh=mesh,
        in_specs=(
            P("band", None, "mem"),
            P("band", None, "mem"),
            P(),
            P("mem", None),
            P("mem", None, None),
            P(),
            P("mem", None, None),
            P("mem", None, None),
        ),
        out_specs=(P(None, "band"), P("mem", None, "band")),
        check_vma=False,
    )
```

time: 222 us -> 88.1 us (0.40)
  blocking collectives: 93.7 us -> 14.4 us
  waiting for transfers between devices: 55.5 us -> 19.7 us
  matrix products: 29 us -> 0 us
  between operations: 14.2 us -> 0.79 us
  Pallas kernels: 0 us -> 13 us
  local copies, waits for them, and re-layouts: 12 us -> 19.8 us
  starting transfers between devices: 12.2 us -> 17.9 us
  other arithmetic: 4.9 us -> 1.62 us
    psum x2 -> x0, blocking collectives: 93.7 us -> none  [the longest x1 79.8 us: per_device(): summed = lax.psum(local_grad, 'mem')]
    all_gather x1 -> x0, waiting for transfers between devices: 35.3 us -> none  [per_device(): lax.all_gather(eigvecs, 'band', axis=0, tiled=True).reshape(modes, -1)]
    dot_general x7 -> x0, matrix products: 29 us -> none  [the longest x1 10.2 us: per_device(): jnp.einsum('jro,jo->jr', interpolation, own_back, preferred_element_type=...]
    ppermute x0 -> x10, waiting for transfers between devices: none -> 15.8 us  [over(): return lax.ppermute(x, 'band', [(i, i ^ bit) for i in range(4)])]
    all_to_all x2 -> x1, waiting for transfers between devices: 19.5 us -> 3.97 us  [per_device(): got = lax.all_to_all(sent, 'mem', split_axis=0, concat_axis=0, tiled=True)]
    all_to_all x0 -> x1, blocking collectives: none -> 14.4 us  [per_device(): lax.all_to_all(payload, 'mem', split_axis=0, concat_axis=0, tiled=True)]
    pallas_call x0 -> x7, Pallas kernels: none -> 13 us  [the longest x1 5.07 us: per_device(): call(obs_body, (shape((8, 1024), F32), shape((8, 1024), F32), shape((256,...]
    ppermute x0 -> x10, starting transfers between devices: none -> 10.1 us  [over(): return lax.ppermute(x, 'band', [(i, i ^ bit) for i in range(4)])]
  transfers between devices with their start and end apart: 3 -> 11, of which waited for: 3 -> 6; matrix products, arithmetic and copies ran while one was open for 3% -> 15% of each run, Pallas kernels for 0% -> 2%
where the time goes in v1:
time: 88.1 us; the launch traced here: 87.2 us
  local copies, waits for them, and re-layouts  19.8 us (22%)
  waiting for transfers between devices  19.7 us (22%)
  starting transfers between devices  17.9 us (20%)
  blocking collectives  14.4 us (16%)
  Pallas kernels  13 us (15%)
  other arithmetic  1.62 us (2%)
    ppermute x10, waiting for transfers between devices, over(): return lax.ppermute(x, 'band', [(i, i ^ bit) for i in range(4)])  15.8 us
    all_to_all x1, blocking collectives, per_device(): lax.all_to_all(payload, 'mem', split_axis=0, concat_axis=0, tiled=True)  14.4 us
    ppermute x10, starting transfers between devices, over(): return lax.ppermute(x, 'band', [(i, i ^ bit) for i in range(4)])  10.1 us
    unnamed x26, local copies, waits for them, and re-layouts  8.86 us
    all_to_all x1, starting transfers between devices, per_device(): got = lax.all_to_all(sent, 'mem', split_axis=0, concat_axis=0, tiled=True)  7.77 us
    pallas_call x1, Pallas kernels, per_device(): call(obs_body, (shape((8, 1024), F32), shape((8, 1024), F32), shape((256,...  5.07 us
    dynamic_slice x1, local copies, waits for them, and re-layouts, per_device(): quarter = lambda x, d: lax.dynamic_slice_in_dim(x, band * 128, 128, d)  4.65 us
    all_to_all x1, waiting for transfers between devices, per_device(): got = lax.all_to_all(sent, 'mem', split_axis=0, concat_axis=0, tiled=True)  3.97 us
  transfers between devices with their start and end apart: 11, of which 6 were waited for; matrix products, arithmetic and copies ran while one was open for 15% of the time, Pallas kernels for 2%

profile of v1, /device:TPU:0, one launch (start us, length us, event | category | flops | bytes accessed | tf_op | source)
XLA Modules:
  0.0 87.2 jit_solution(2762426168774550792)
XLA Ops:
  0.6 2.0 %dynamic-slice_bitcast_fusion = (bf16[224,1024]{1,0:T(8,128)(2,1)}, bf16[224,1024]{1,0:T(8,128)(2,1)S(1)}) fusion(bf16[28,16,1024]{2,1,0:T(8,128)(2,1)} %param.9, s32[]{:T(128)S(6)} %select_n.14, s32[]{:T(128)S(6)} %select_n.6), kind=kLoop, calls=%fused_computation | loop fusion | bytes 1835016 | tf_op jit(solution)/shard_map/reshape | solution.py:199
  2.6 1.8 %dynamic-slice_bitcast_fusion.2 = (bf16[128,1024]{1,0:T(8,128)(2,1)}, bf16[128,1024]{1,0:T(8,128)(2,1)S(1)}) fusion(bf16[16,16,1024]{2,1,0:T(8,128)(2,1)} %param.8, s32[]{:T(128)S(6)} %select_n.14, s32[]{:T(128)S(6)} %select_n.6), kind=kLoop, calls=%fused_computation.3 | loop fusion | bytes 1048584 | tf_op jit(solution)/shard_map/reshape | solution.py:199
  4.4 4.1 %collective-permute-start.2 = (bf16[128,1024]{1,0:T(8,128)(2,1)}, bf16[128,1024]{1,0:T(8,128)(2,1)S(1)}, u32[]{:S(2)}, u32[]{:S(2)}) collective-permute-start(bf16[128,1024]{1,0:T(8,128)(2,1)} %get-tuple-element.26), channel_id=1, source_target_pairs={{0,96},{32,64},{64,32},{96,0},{1,97},{33,65},{65,33},{97,1},{2,98}... | collective-permute-start | bytes 786440 | tf_op jit(solution)/shard_map/ppermute | solution.py:196
  9.6 1.4 %copy.11.columns = s32[64,16]{1,0:T(8,128)} copy(s32[64,16]{0,1:T(8,128)} %param.11) | data formatting | bytes 8192 | tf_op args[3]
  11.0 1.5 %copy.10.control.refs_2_ = f32[112,64]{1,0:T(8,128)} copy(f32[112,64]{0,1:T(8,128)} %param.10) | data formatting | bytes 57344 | tf_op args[2]
  14.2 1.2 %shard_map.95 = (bf16[448,512]{1,0:T(8,128)(2,1)S(1)}, bf16[1024,1024]{1,0:T(8,128)(2,1)S(1)}, bf16[64,256]{1,0:T(8,128)(2,1)S(1)}) custom-call(s32[2]{0:T(128)S(1)} %pad_add_fusion.meta.refs_0_, f32[112,64]{1,0:T(8,128)S(1)} %copy-done.3, s32[64,16]{1,0:T(8,128)S(1)} %copy-done.8, s32[32,64]{1,0:T(8,128)S(1)} %reshape.29.owners), custom_call_target="tpu_custom_call" | custom-call | flops 100000000 | bytes 3000000 | tf_op jit(solution)/shard_map/pallas_call | solution.py:217
  15.3 1.0 %dynamic-slice_bitcast_fusion.4 = (f32[32,8,128]{2,1,0:T(8,128)S(1)}, f32[32,8,128]{2,1,0:T(8,128)S(1)}) fusion(f32[1,256,512]{2,1,0:T(8,128)} %param.15, s32[]{:T(128)S(6)} %select_n.15, f32[1,256,512]{2,1,0:T(8,128)} %param.14), kind=kLoop, calls=%fused_computation.5 | loop fusion | bytes 524292 | tf_op jit(solution)/shard_map/reshape | solution.py:212
  16.4 4.9 %collective-permute-done.1.refs_3_.m2 = bf16[128,1024]{1,0:T(8,128)(2,1)} collective-permute-done((bf16[128,1024]{1,0:T(8,128)(2,1)S(1)}, bf16[128,1024]{1,0:T(8,128)(2,1)}, u32[]{:S(2)}, u32[]{:S(2)}) %collective-permute-start.1) | collective-permute-done | bytes 262176 | tf_op jit(solution)/shard_map/ppermute | solution.py:196
  21.3 2.8 %shard_map.96 = f32[8,1024]{1,0:T(8,128)} custom-call(bf16[448,512]{1,0:T(8,128)(2,1)S(1)} %get-tuple-element.12.refs_0_, bf16[128,1024]{1,0:T(8,128)(2,1)S(1)} %get-tuple-element.27.refs_1_.m0, bf16[128,1024]{1,0:T(8,128)(2,1)} %collective-permute-done.refs_2_.m1, bf16[128,1024]{1,0:T(8,128)(2,1)} %collective-permute-done.1.refs_3_.m2, ...), custom_call_target="tpu_custom_call" | custom-call | flops 500000000 | bytes 2000000 | tf_op jit(solution)/shard_map/pallas_call | solution.py:226
  24.0 3.1 %collective-permute-start.4 = (f32[8,1024]{1,0:T(8,128)}, f32[8,1024]{1,0:T(8,128)}, u32[]{:S(2)}, u32[]{:S(2)}) collective-permute-start(f32[8,1024]{1,0:T(8,128)} %shard_map.96), channel_id=1, source_target_pairs={{0,64},{32,96},{64,0},{96,32},{1,65},{33,97},{65,1},{97,33},{2,66}... | collective-permute-start | bytes 98312 | tf_op jit(solution)/shard_map/ppermute | solution.py:196
  27.9 7.8 %all-to-all-start = ((f32[32,16,128]{2,1,0:T(8,128)}), f32[32,16,128]{2,1,0:T(8,128)S(1)}, u32[]{:S(2)}, u32[]{:S(2)}) async-start(f32[32,16,128]{2,1,0:T(8,128)} %pad_maximum_fusion), calls=%async_computation | async-start | bytes 524288 | tf_op jit(solution)/shard_map/all_to_all | solution.py:214
  36.5 4.7 %constant_dynamic-slice_fusion.interp = bf16[64,256,128]{2,1,0:T(8,128)(2,1)} fusion(bf16[64,256,512]{2,1,0:T(8,128)(2,1)} %param.12, s32[]{:T(128)S(6)} %select_n.15), kind=kLoop, calls=%fused_computation.9 | loop fusion | bytes 8388612 | tf_op jit(solution)/shard_map/dynamic_slice | solution.py:210
  41.2 4.0 %all-to-all-done.got = f32[32,16,128]{2,1,0:T(8,128)S(1)} async-done(((f32[32,16,128]{2,1,0:T(8,128)}), f32[32,16,128]{2,1,0:T(8,128)S(1)}, u32[]{:S(2)}, u32[]{:S(2)}) %all-to-all-start) | async-done | bytes 262176 | tf_op jit(solution)/shard_map/all_to_all | solution.py:214
  46.2 2.2 %copy-done = bf16[64,256,128]{2,1,0:T(8,128)(2,1)S(1)} copy-done((bf16[64,256,128]{2,1,0:T(8,128)(2,1)S(1)}, bf16[64,256,128]{2,1,0:T(8,128)(2,1)}, u32[]{:S(2)}) %copy-start) | copy-done | bytes 4194328
  49.8 5.1 %shard_map.98 = (f32[8,1024]{1,0:T(8,128)S(1)}, f32[8,1024]{1,0:T(8,128)S(1)}, f32[256,128]{1,0:T(8,128)S(1)}) custom-call(s32[2]{0:T(128)S(1)} %copy-done.10, bf16[8,1024]{1,0:T(8,128)(2,1)S(1)} %add_convert_fusion.inc_my, bf16[8,1024]{1,0:T(8,128)(2,1)} %collective-permute-done.5.inc_mt, bf16[1024,1024]{1,0:T(8,128)(2,1)S(1)} %get-tuple-element.13.onehot, ...), custom_call_target="tpu_custom_call" | custom-call | flops 1000000000 | bytes 8000000 | tf_op jit(solution)/shard_map/pallas_call | solution.py:232
  54.9 1.2 %collective-permute-done.6 = f32[8,1024]{1,0:T(8,128)S(1)} collective-permute-done((f32[8,1024]{1,0:T(8,128)S(1)}, f32[8,1024]{1,0:T(8,128)S(1)}, u32[]{:S(2)}, u32[]{:S(2)}) %collective-permute-start.6) | collective-permute-done | bytes 32800 | tf_op jit(solution)/shard_map/ppermute | solution.py:196
  56.1 1.2 %collective-permute-start.7 = (f32[8,1024]{1,0:T(8,128)S(1)}, f32[8,1024]{1,0:T(8,128)S(1)}, u32[]{:S(2)}, u32[]{:S(2)}) collective-permute-start(f32[8,1024]{1,0:T(8,128)S(1)} %add.26.a0), channel_id=1, source_target_pairs={{0,64},{32,96},{64,0},{96,32},{1,65},{33,97},{65,1},{97,33},{2,66}... | collective-permute-start | bytes 98312 | tf_op jit(solution)/shard_map/ppermute | solution.py:196
  57.3 4.3 %collective-permute-done.7.a1 = f32[8,1024]{1,0:T(8,128)S(1)} collective-permute-done((f32[8,1024]{1,0:T(8,128)S(1)}, f32[8,1024]{1,0:T(8,128)S(1)}, u32[]{:S(2)}, u32[]{:S(2)}) %collective-permute-start.7) | collective-permute-done | bytes 32800 | tf_op jit(solution)/shard_map/ppermute | solution.py:196
  61.6 2.3 %shard_map.99 = (f32[56,32]{1,0:T(8,128)S(1)}, f32[56,32]{1,0:T(8,128)S(1)}) custom-call(f32[8,1024]{1,0:T(8,128)S(1)} %add.26.a0, f32[8,1024]{1,0:T(8,128)S(1)} %collective-permute-done.7.a1, bf16[128,1024]{1,0:T(8,128)(2,1)S(1)} %get-tuple-element.27.refs_1_.m0, bf16[128,1024]{1,0:T(8,128)(2,1)} %collective-permute-done.refs_2_.m1, ...), custom_call_target="tpu_custom_call" | custom-call | flops 500000000 | bytes 2000000 | tf_op jit(solution)/shard_map/pallas_call | solution.py:240
  64.0 1.2 %collective-permute-done.8 = f32[56,32]{1,0:T(8,128)S(1)} collective-permute-done((f32[56,32]{1,0:T(8,128)S(1)}, f32[56,32]{1,0:T(8,128)S(1)}, u32[]{:S(2)}, u32[]{:S(2)}) %collective-permute-start.8) | collective-permute-done | bytes 7200 | tf_op jit(solution)/shard_map/ppermute | solution.py:196
  65.3 1.2 %collective-permute-start.9 = (f32[56,16]{1,0:T(8,128)S(1)}, f32[56,16]{1,0:T(8,128)S(1)}, u32[]{:S(2)}, u32[]{:S(2)}) collective-permute-start(f32[56,16]{1,0:T(8,128)S(1)} %get-tuple-element.28), channel_id=1, source_target_pairs={{0,64},{32,96},{64,0},{96,32},{1,65},{33,97},{65,1},{97,33},{2,66}... | collective-permute-start | bytes 10760 | tf_op jit(solution)/shard_map/ppermute | solution.py:196
  66.5 4.2 %collective-permute-done.9.came = f32[56,16]{1,0:T(8,128)S(1)} collective-permute-done((f32[56,16]{1,0:T(8,128)S(1)}, f32[56,16]{1,0:T(8,128)S(1)}, u32[]{:S(2)}, u32[]{:S(2)}) %collective-permute-start.9) | collective-permute-done | bytes 3616 | tf_op jit(solution)/shard_map/ppermute | solution.py:196
  70.8 14.4 %all_to_all.10.refs_1_ = f32[32,24,128]{2,1,0:T(8,128)S(1)} all-to-all(f32[32,24,128]{2,1,0:T(8,128)S(1)} %shard_map.100), channel_id=1, replica_groups=mesh['band'=4,'mem'=32] {'mem'}, dimensions={0} | all-to-all | bytes 786432 | tf_op jit(solution)/shard_map/all_to_all | solution.py:248
  85.2 1.4 %shard_map.101 = (f32[112,16]{1,0:T(8,128)S(1)}, f32[1,256,128]{2,1,0:T(8,128)}) custom-call(s32[2]{0:T(128)S(1)} %copy-done.11, f32[32,24,128]{2,1,0:T(8,128)S(1)} %all_to_all.10.refs_1_, f32[112,64]{1,0:T(8,128)S(1)} %copy-done.4), custom_call_target="tpu_custom_call" | custom-call | flops 1000000 | bytes 600000 | tf_op jit(solution)/shard_map/pallas_call | solution.py:249
  (45 shorter events, 7.8 us)
Async XLA Ops:
  2.6 18.6 %collective-permute-start.3 = (bf16[224,1024]{1,0:T(8,128)(2,1)}, bf16[224,1024]{1,0:T(8,128)(2,1)S(1)}, u32[]{:S(2)}, u32[]{:S(2)}) collective-permute-start(bf16[224,1024]{1,0:T(8,128)(2,1)} %get-tuple-element.24), channel_id=1, source_target_pairs={{0,32},{32,0},{64,96},{96,64},{1,33},{33,1},{65,97},{97,65},{2,34}... | collective-permute-start | bytes 1376264 | tf_op jit(solution)/shard_map/ppermute | solution.py:196
  4.4 11.9 %collective-permute-start.2 = (bf16[128,1024]{1,0:T(8,128)(2,1)}, bf16[128,1024]{1,0:T(8,128)(2,1)S(1)}, u32[]{:S(2)}, u32[]{:S(2)}) collective-permute-start(bf16[128,1024]{1,0:T(8,128)(2,1)} %get-tuple-element.26), channel_id=1, source_target_pairs={{0,96},{32,64},{64,32},{96,0},{1,97},{33,65},{65,33},{97,1},{2,98}... | collective-permute-start | bytes 786440 | tf_op jit(solution)/shard_map/ppermute | solution.py:196
  8.5 7.9 %collective-permute-start = (bf16[128,1024]{1,0:T(8,128)(2,1)}, bf16[128,1024]{1,0:T(8,128)(2,1)}, u32[]{:S(2)}, u32[]{:S(2)}) collective-permute-start(bf16[128,1024]{1,0:T(8,128)(2,1)} %get-tuple-element.26), channel_id=1, source_target_pairs={{0,32},{32,0},{64,96},{96,64},{1,33},{33,1},{65,97},{97,65},{2,34}... | collective-permute-start | bytes 786440 | tf_op jit(solution)/shard_map/ppermute | solution.py:196
  8.5 12.8 %collective-permute-start.1 = (bf16[128,1024]{1,0:T(8,128)(2,1)S(1)}, bf16[128,1024]{1,0:T(8,128)(2,1)}, u32[]{:S(2)}, u32[]{:S(2)}) collective-permute-start(bf16[128,1024]{1,0:T(8,128)(2,1)S(1)} %get-tuple-element.27.refs_1_.m0), channel_id=1, source_target_pairs={{0,64},{32,96},{64,0},{96,32},{1,65},{33,97},{65,1},{97,33},{2,66}... | collective-permute-start | bytes 786440 | tf_op jit(solution)/shard_map/ppermute | solution.py:196
  12.6 0.8 copy-start.3
  13.4 0.8 copy-start.8
  14.2 13.0 %copy-start.9 = (s32[2]{0:T(128)}, s32[2]{0:T(128)S(1)}, u32[]{:S(2)}) copy-start(s32[2]{0:T(128)S(1)} %pad_add_fusion.meta.refs_0_) | copy-start | bytes 28
  15.3 8.7 %copy-start.5 = (bf16[64,256]{1,0:T(8,128)(2,1)}, bf16[64,256]{1,0:T(8,128)(2,1)S(1)}, u32[]{:S(2)}) copy-start(bf16[64,256]{1,0:T(8,128)(2,1)S(1)} %get-tuple-element.14.place) | copy-start | bytes 98308
  16.4 11.6 %copy-start.1 = (bf16[128,1024]{1,0:T(8,128)(2,1)}, bf16[128,1024]{1,0:T(8,128)(2,1)S(1)}, u32[]{:S(2)}) copy-start(bf16[128,1024]{1,0:T(8,128)(2,1)S(1)} %collective-permute-done.2.refs_4_.m3) | copy-start | bytes 786436
  24.0 11.7 %collective-permute-start.4 = (f32[8,1024]{1,0:T(8,128)}, f32[8,1024]{1,0:T(8,128)}, u32[]{:S(2)}, u32[]{:S(2)}) collective-permute-start(f32[8,1024]{1,0:T(8,128)} %shard_map.96), channel_id=1, source_target_pairs={{0,64},{32,96},{64,0},{96,32},{1,65},{33,97},{65,1},{97,33},{2,66}... | collective-permute-start | bytes 98312 | tf_op jit(solution)/shard_map/ppermute | solution.py:196
  27.9 17.2 %all-to-all-start = ((f32[32,16,128]{2,1,0:T(8,128)}), f32[32,16,128]{2,1,0:T(8,128)S(1)}, u32[]{:S(2)}, u32[]{:S(2)}) async-start(f32[32,16,128]{2,1,0:T(8,128)} %pad_maximum_fusion), calls=%async_computation | async-start | bytes 524288 | tf_op jit(solution)/shard_map/all_to_all | solution.py:214
  36.5 9.6 %collective-permute-start.5 = (bf16[8,1024]{1,0:T(8,128)(2,1)S(1)}, bf16[8,1024]{1,0:T(8,128)(2,1)}, u32[]{:S(2)}, u32[]{:S(2)}) collective-permute-start(bf16[8,1024]{1,0:T(8,128)(2,1)S(1)} %add_convert_fusion.inc_my), channel_id=1, source_target_pairs={{0,32},{32,0},{64,96},{96,64},{1,33},{33,1},{65,97},{97,65},{2,34}... | collective-permute-start | bytes 49160 | tf_op jit(solution)/shard_map/ppermute | solution.py:196
  45.1 16.4 %copy-start.2 = (bf16[128,1024]{1,0:T(8,128)(2,1)S(1)}, bf16[128,1024]{1,0:T(8,128)(2,1)}, u32[]{:S(2)}) copy-start(bf16[128,1024]{1,0:T(8,128)(2,1)} %copy-done.1) | copy-start | bytes 786436
  45.1 0.8 copy-start.6
  46.2 2.2 %copy-start = (bf16[64,256,128]{2,1,0:T(8,128)(2,1)S(1)}, bf16[64,256,128]{2,1,0:T(8,128)(2,1)}, u32[]{:S(2)}) copy-start(bf16[64,256,128]{2,1,0:T(8,128)(2,1)} %constant_dynamic-slice_fusion.interp) | copy-start | bytes 12582916
  48.3 0.8 copy-start.7
  49.1 0.7 copy-start.10
  49.8 35.4 %copy-start.4 = (f32[112,64]{1,0:T(8,128)S(1)}, f32[112,64]{1,0:T(8,128)}, u32[]{:S(2)}) copy-start(f32[112,64]{1,0:T(8,128)} %copy.10.control.refs_2_) | copy-start | bytes 86020
  49.8 35.4 %copy-start.11 = (s32[2]{0:T(128)S(1)}, s32[2]{0:T(128)}, u32[]{:S(2)}) copy-start(s32[2]{0:T(128)} %copy-done.9) | copy-start | bytes 28
  54.8 1.3 %collective-permute-start.6 = (f32[8,1024]{1,0:T(8,128)S(1)}, f32[8,1024]{1,0:T(8,128)S(1)}, u32[]{:S(2)}, u32[]{:S(2)}) collective-permute-start(f32[8,1024]{1,0:T(8,128)S(1)} %get-tuple-element.18), channel_id=1, source_target_pairs={{0,32},{32,0},{64,96},{96,64},{1,33},{33,1},{65,97},{97,65},{2,34}... | collective-permute-start | bytes 98312 | tf_op jit(solution)/shard_map/ppermute | solution.py:196
  56.1 5.4 %collective-permute-start.7 = (f32[8,1024]{1,0:T(8,128)S(1)}, f32[8,1024]{1,0:T(8,128)S(1)}, u32[]{:S(2)}, u32[]{:S(2)}) collective-permute-start(f32[8,1024]{1,0:T(8,128)S(1)} %add.26.a0), channel_id=1, source_target_pairs={{0,64},{32,96},{64,0},{96,32},{1,65},{33,97},{65,1},{97,33},{2,66}... | collective-permute-start | bytes 98312 | tf_op jit(solution)/shard_map/ppermute | solution.py:196
  63.9 1.3 %collective-permute-start.8 = (f32[56,32]{1,0:T(8,128)S(1)}, f32[56,32]{1,0:T(8,128)S(1)}, u32[]{:S(2)}, u32[]{:S(2)}) collective-permute-start(f32[56,32]{1,0:T(8,128)S(1)} %get-tuple-element.20), channel_id=1, source_target_pairs={{0,32},{32,0},{64,96},{96,64},{1,33},{33,1},{65,97},{97,65},{2,34}... | collective-permute-start | bytes 21512 | tf_op jit(solution)/shard_map/ppermute | solution.py:196
  65.3 5.4 %collective-permute-start.9 = (f32[56,16]{1,0:T(8,128)S(1)}, f32[56,16]{1,0:T(8,128)S(1)}, u32[]{:S(2)}, u32[]{:S(2)}) collective-permute-start(f32[56,16]{1,0:T(8,128)S(1)} %get-tuple-element.28), channel_id=1, source_target_pairs={{0,64},{32,96},{64,0},{96,32},{1,65},{33,97},{65,1},{97,33},{2,66}... | collective-permute-start | bytes 10760 | tf_op jit(solution)/shard_map/ppermute | solution.py:196

commit v2 on v1

v2 whole, which is shorter than its diff:
```python
import math

import jax
import jax.numpy as jnp
from jax import lax
from jax.experimental import pallas as pl
from jax.experimental.pallas import tpu as pltpu
from jax.sharding import PartitionSpec as P

BF = jnp.bfloat16
F32 = jnp.float32
NN = (((1,), (0,)), ((), ()))
NT = (((1,), (1,)), ((), ()))
TN = (((0,), (0,)), ((), ()))
MIB = 1024 * 1024
VM = pl.BlockSpec(memory_space=pltpu.VMEM)
ANY = pl.BlockSpec(memory_space=pl.ANY)


def dot(a, b, dims=NN):
    return lax.dot_general(a, b, dims, preferred_element_type=F32)


def parts3(x):
    hi = x.astype(BF)
    rest = x - hi.astype(F32)
    mid = rest.astype(BF)
    lo = (rest - mid.astype(F32)).astype(BF)
    return hi, mid, lo


def iota(dims, dim):
    return lax.broadcasted_iota(jnp.int32, dims, dim)


def ones_where(cond):
    return cond.astype(F32).astype(BF)


def shape(dims, dtype):
    return jax.ShapeDtypeStruct(dims, dtype)


def call(body, ins, outs, flops, nbytes, scratch=(), vmem=16):
    return pl.pallas_call(
        body,
        out_shape=tuple(o for o, _ in outs),
        in_specs=list(ins),
        out_specs=tuple(s for _, s in outs),
        scratch_shapes=list(scratch),
        compiler_params=pltpu.CompilerParams(vmem_limit_bytes=vmem * MIB),
        cost_estimate=pl.CostEstimate(flops=flops, bytes_accessed=nbytes, transcendentals=0),
    )


def start_all(copies):
    for c in copies:
        c.start()
    return copies


def wait_all(copies):
    for c in copies:
        c.wait()


def halves_copies(src, mine, mate, sem, at):
    core = lax.axis_index("band") & 1
    lo = pl.multiple_of(core * 8, 8)
    hi = pl.multiple_of(8 - core * 8, 8)
    return [
        pltpu.make_async_copy(src.at[:, pl.ds(hi, 8), :], mate, sem.at[at]),
        pltpu.make_async_copy(src.at[:, pl.ds(lo, 8), :], mine, sem.at[at + 1]),
    ]


def split_body(src, mine, mate, sem):
    wait_all(start_all(halves_copies(src, mine, mate, sem, 0)))


def quarter_at(side):
    core = lax.axis_index("band") & 1
    return pl.ds(pl.multiple_of((core + 2 * side) * 128, 128), 128)


def load_body(eig, innovation, obs_weight, owners, mine, mate, payload, innov_own, live_own, iv, sem):
    copies = []
    for n, a in enumerate((innovation, obs_weight)):
        for side in range(2):
            copies.append(pltpu.make_async_copy(
                a.at[0, :, quarter_at(side)], iv.at[n, :, side * 128:(side + 1) * 128], sem.at[2 + 2 * n + side]))
    slices = halves_copies(eig, mine, mate, sem, 0)
    start_all(slices)
    start_all(copies)
    tile = lax.axis_index("mem")
    own = owners[...].astype(F32)
    wait_all(copies)
    for n in range(2):
        payload[:, n * 8:(n + 1) * 8, :] = iv[n].reshape(32, 8, 256).astype(BF)
    hit = jnp.where(own == tile.astype(F32), 1.0, 0.0)
    r = iota((256, 16), 0)
    pair = ones_where((r >> 4) == iota((256, 16), 1))
    both = dot(pair, hit.astype(BF))
    odd = (iota((256, 128), 0) >> 3) & 1
    side = jnp.where((iota((256, 128), 1) >> 6) == odd, both, 0.0)
    count = jnp.sum(side, axis=1, keepdims=True)
    live = jnp.where((iota((256, 1), 0) & 7).astype(F32) < count, 1.0, 0.0)
    high = (lax.axis_index("band") >> 1) == 1
    innov_own[...] = jnp.where(high, iv[0, :, 128:], iv[0, :, :128])
    live_own[...] = live * jnp.where(high, iv[1, :, 128:], iv[1, :, :128])
    wait_all(slices)


def prep_body(control_t, columns_t, owners, interpolation, kron, onehot, place, interp, sem):
    copies = start_all([
        pltpu.make_async_copy(
            interpolation.at[:, :, quarter_at(side)], interp.at[:, :, side * 128:(side + 1) * 128], sem.at[side])
        for side in range(2)
    ])
    band = lax.axis_index("band")
    tile = lax.axis_index("mem")
    row = iota((448, 112), 0)
    second = (row >= 224).astype(jnp.int32)
    mode = (band ^ second) * 28 + ((row - 224 * second) >> 3)
    pick_rows = ones_where(mode == iota((448, 112), 1))
    col = iota((64, 512), 1)
    member = (band ^ (col >> 7)) * 16 + ((col & 127) >> 3)
    pick_cols = ones_where(member == iota((64, 512), 0))
    rows = dot(pick_rows, control_t[...].astype(BF), NT).astype(BF)
    full = dot(rows, pick_cols)
    same = (iota((448, 512), 0) & 7) == (iota((448, 512), 1) & 7)
    kron[...] = jnp.where(same, full, 0.0).astype(BF)
    t = iota((64, 1024), 1)
    cols = columns_t[...].astype(F32).T.astype(jnp.int32)
    for c in range(16):
        onehot[c * 64:(c + 1) * 64, :] = ones_where(cols[:, c:c + 1] == t)
    pair = owners[pl.ds(tile >> 1, 1), :].astype(F32)
    own = jnp.where((tile & 1) == 1, pair[:, 64:], pair[:, :64])
    own_row = jnp.broadcast_to(own, (64, 64))
    own_col = own_row.T
    earlier = iota((64, 64), 1) < iota((64, 64), 0)
    rank = jnp.sum(jnp.where((own_row == own_col) & earlier, 1.0, 0.0), axis=1, keepdims=True)
    target = (own_col[:, :1] * 8.0 + rank).astype(jnp.int32)
    place[...] = ones_where(target == iota((64, 256), 1))
    wait_all(copies)


def select_body(place, got, innov, weight):
    x = got[...].astype(F32)
    sel = place[...]
    innov[...] = dot(sel, x[:, :8].reshape(256, 256).astype(BF))
    weight[...] = dot(sel, x[:, 8:].reshape(256, 256).astype(BF))


def increment_body(scale, kron, m0, m1, m2, m3, e0, e1, _, out):
    for g in range(0, 1024, 256):
        cut = slice(g, g + 256)
        mixed = None
        for p, m in enumerate((m0, m1, m2, m3)):
            term = dot(kron[:, p * 128:(p + 1) * 128], m[:, cut])
            mixed = term if mixed is None else mixed + term
        total = jnp.sum((mixed[:224] * e0[:, cut].astype(F32)).reshape(28, 8, 256), axis=0)
        total = total + jnp.sum((mixed[224:] * e1[:, cut].astype(F32)).reshape(28, 8, 256), axis=0)
        out[:, cut] = total * scale


def obs_body(p0, p1, p2, p3, onehot, place, innov, weight, interp, adj_my, adj_mt, slots, picked, depb, spread):
    band = lax.axis_index("band")
    first = (band & 1) == 0
    mine = p0[...] + p2[...]
    mate = p1[...] + p3[...]
    inc = jnp.concatenate([jnp.where(first, mine, mate), jnp.where(first, mate, mine)], axis=0).astype(BF)
    picks = dot(onehot[...], inc, NT)
    by_col = jnp.concatenate([picks[c * 64:(c + 1) * 64] for c in range(16)], axis=1).astype(BF)
    r0 = iota((256, 256), 0)
    r1 = iota((256, 256), 1)
    swap = ones_where(((r0 & 15) * 16 + (r0 >> 4)) == r1)
    picked[...] = dot(by_col, swap).astype(BF)
    rows = iota((16, 256), 0)
    image = []
    for b in range(4):
        lhs = picked[b * 16:(b + 1) * 16, :]
        acc = jnp.zeros((16, 256), F32)
        for i in range(16):
            acc = jnp.where(rows == i, dot(lhs, interp[b * 16 + i]), acc)
        image.append(acc)
    image = jnp.concatenate(image, axis=0)
    depb[...] = (weight[...] * (innov[...] - image)).astype(BF)
    for b in range(4):
        lhs = depb[b * 16:(b + 1) * 16, :]
        acc = jnp.zeros((16, 256), F32)
        for i in range(16):
            acc = jnp.where(rows == i, dot(lhs, interp[b * 16 + i], NT), acc)
        spread[b * 16:(b + 1) * 16, :] = acc
    x = spread[...]
    hi = x.astype(BF)
    lo = (x - hi.astype(F32)).astype(BF)
    terms = []
    for part in (hi, lo):
        turned = dot(swap, part, NT)
        terms.append(jnp.concatenate([turned[c * 16:(c + 1) * 16] for c in range(16)], axis=1))
    both = dot(jnp.concatenate(terms, axis=0).astype(BF), onehot[...])
    adj = both[:16] + both[16:]
    adj_my[...] = jnp.where(first, adj[:8], adj[8:])
    adj_mt[...] = jnp.where(first, adj[8:], adj[:8])
    sel = place[...]
    hi, mid, lo = parts3(jnp.where((band >> 1) == 0, image[:, :128], image[:, 128:]))
    slots[...] = dot(sel, hi, TN) + dot(sel, mid, TN) + dot(sel, lo, TN)


def gradient_body(a0, a1, m0, m1, m2, m3, e0, e1, g0, g1, g2, g3):
    band = lax.axis_index("band")
    adj = a0[...] + a1[...]
    wide = jnp.broadcast_to(adj[None], (16, 8, 1024)).reshape(128, 1024)
    same = (iota((128, 224), 0) & 7) == (iota((128, 224), 1) & 7)
    mode = iota((224, 128), 0) >> 3
    lane = iota((224, 128), 1)
    sel0 = ones_where(mode + band * 28 == lane)
    sel1 = ones_where(mode + (band ^ 1) * 28 == lane)
    for m, g in ((m3, g3), (m2, g2), (m1, g1), (m0, g0)):
        weighted = (m[...].astype(F32) * wide).astype(BF)
        total = None
        for e, sel in ((e0, sel0), (e1, sel1)):
            full = jnp.where(same, dot(weighted, e[...], NT), 0.0)
            hi, mid, lo = parts3(jnp.sum(full.reshape(16, 8, 224), axis=1))
            term = dot(hi, sel) + dot(mid, sel) + dot(lo, sel)
            total = term if total is None else total + term
        g[...] = total


def pack_body(g0, g1, g2, g3, slots, out):
    total = (g0[...] + g1[...]) + (g2[...] + g3[...])
    out[:, :8, :] = slots[...].reshape(32, 8, 128)
    out[:, 8:, :] = jnp.broadcast_to(total[None], (32, 16, 128))


def final_body(scale, got, control_t, innov, live, gradient_t, departures):
    band = lax.axis_index("band")
    image = got[:, :8, :].reshape(256, 128)
    departures[...] = (live[...] * (innov[...] - image)).reshape(1, 256, 128)
    total = jnp.sum(got[:, 8:, :], axis=0)[:, :112]
    own = ones_where(iota((16, 64), 1) == band * 16 + iota((16, 64), 0))
    hi, mid, lo = parts3(control_t[...])
    gradient_t[...] = dot(own, hi) + dot(own, mid) + dot(own, lo) - scale * total


def per_device(members, eigvecs, control, columns, interpolation, owners, innovation, obs_weight):
    scale = 1.0 / math.sqrt(112 * 64)
    owners = owners.reshape(16, 128)

    def over(x, bit):
        return lax.ppermute(x, "band", [(i, i ^ bit) for i in range(4)])

    dma = pltpu.SemaphoreType.DMA
    m_my, m_mt = call(
        split_body, [ANY], [(shape((16, 8, 1024), BF), ANY)] * 2, 0, 10 ** 6, [dma((2,))]
    )(members)
    m_my, m_mt = m_my.reshape(128, 1024), m_mt.reshape(128, 1024)
    m3 = over(m_mt, 3)
    m2 = over(m_my, 2)
    m1 = over(m_mt, 1)

    e_my, e_mt, payload, innov_own, live_own = call(
        load_body,
        [ANY, ANY, ANY, VM],
        [(shape((28, 8, 1024), BF), ANY)] * 2 + [(shape((32, 16, 256), BF), VM)] + [(shape((256, 128), F32), VM)] * 2,
        10 ** 6, 5 * 10 ** 6,
        [pltpu.VMEM((2, 256, 256), F32), dma((6,))],
    )(eigvecs, innovation, obs_weight, owners)
    e0, e_mt = e_my.reshape(224, 1024), e_mt.reshape(224, 1024)
    e1 = over(e_mt, 1)
    got = lax.all_to_all(payload, "mem", split_axis=0, concat_axis=0, tiled=True)

    kron, onehot, place, interp = call(
        prep_body,
        [VM, VM, VM, ANY],
        [(shape((448, 512), BF), VM), (shape((1024, 1024), BF), VM), (shape((64, 256), BF), VM),
         (shape((64, 256, 256), BF), VM)],
        10 ** 8, 20 * 10 ** 6, [dma((2,))],
    )(control.T, columns.T, owners, interpolation)
    innov, weight = call(
        select_body, [VM] * 2, [(shape((64, 256), F32), VM)] * 2, 10 ** 7, 4 * 10 ** 5
    )(place, got)

    (part,) = call(
        lambda *refs: increment_body(scale, *refs), [VM] * 7 + [ANY], [(shape((8, 1024), F32), VM)],
        5 * 10 ** 8, 2 * 10 ** 6,
    )(kron, m_my, m1, m2, m3, e0, e1, innov)
    p3 = over(part, 3)
    p2 = over(part, 2)
    p1 = over(part, 1)

    adj_my, adj_mt, slots = call(
        obs_body, [VM] * 9,
        [(shape((8, 1024), F32), VM)] * 2 + [(shape((256, 128), F32), VM)],
        10 ** 9, 12 * 10 ** 6,
        [pltpu.VMEM((64, 256), BF), pltpu.VMEM((64, 256), BF), pltpu.VMEM((64, 256), F32)],
    )(part, p1, p2, p3, onehot, place, innov, weight, interp)

    g0, g1, g2, g3 = call(
        gradient_body, [VM] * 8, [(shape((16, 128), F32), VM)] * 4, 5 * 10 ** 8, 2 * 10 ** 6
    )(adj_my, over(adj_mt, 1), m_my, m1, m2, m3, e0, e1)
    r3 = over(g3, 3)
    r2 = over(g2, 2)
    r1 = over(g1, 1)

    (sent,) = call(
        pack_body, [VM] * 5, [(shape((32, 24, 128), F32), VM)], 10 ** 5, 6 * 10 ** 5
    )(g0, r1, r2, r3, slots)
    arrived = lax.all_to_all(sent, "mem", split_axis=0, concat_axis=0, tiled=True)
    gradient_t, departures = call(
        lambda *refs: final_body(scale, *refs), [VM] * 4,
        [(shape((16, 112), F32), VM), (shape((1, 256, 128), F32), VM)], 10 ** 6, 6 * 10 ** 5,
    )(arrived, control.T, innov_own, live_own)
    return (gradient_t.T, departures)


def solution(mesh):
    return jax.shard_map(
        per_device,
        mesh=mesh,
        in_specs=(
            P("band", None, "mem"),
            P("band", None, "mem"),
            P(),
            P("mem", None),
            P("mem", None, None),
            P(),
            P("mem", None, None),
            P("mem", None, None),
        ),
        out_specs=(P(None, "band"), P("mem", None, "band")),
        check_vma=False,
    )
```

time: 88.1 us -> 89.6 us (1.017)
  waiting for transfers between devices: 19.7 us -> 8.36 us
  Pallas kernels: 13 us -> 17.8 us
  blocking collectives: 14.4 us -> 18.4 us
  local copies, waits for them, and re-layouts: 19.8 us -> 23.5 us
  starting transfers between devices: 17.9 us -> 19.9 us
  other arithmetic: 1.62 us -> 0 us
    unnamed x26 -> x42, local copies, waits for them, and re-layouts: 8.86 us -> 23.5 us
    ppermute x10 -> x11, waiting for transfers between devices: 15.8 us -> 8.36 us  [over(): return lax.ppermute(x, 'band', [(i, i ^ bit) for i in range(4)])]
    reshape x4 -> x0, local copies, waits for them, and re-layouts: 5.53 us -> none  [the longest x2 3.77 us: half(): return lax.dynamic_slice_in_dim(x, which * 8, 8, 1).reshape(-1, 1024)]
    pallas_call x7 -> x9, Pallas kernels: 13 us -> 17.8 us  [the longest x1 5.99 us: per_device(): call(obs_body, [VM] * 9, [(shape((8, 1024), F32), VM)] * 2 + [(shape((256...]
    dynamic_slice x1 -> x0, local copies, waits for them, and re-layouts: 4.65 us -> none  [per_device(): quarter = lambda x, d: lax.dynamic_slice_in_dim(x, band * 128, 128, d)]
    all_to_all x1, blocking collectives: 14.4 us -> 18.4 us  [per_device(): lax.all_to_all(sent, 'mem', split_axis=0, concat_axis=0, tiled=True)]
    all_to_all x1, waiting for transfers between devices: 3.97 us -> 0.01 us  [per_device(): lax.all_to_all(payload, 'mem', split_axis=0, concat_axis=0, tiled=True)]
    ppermute x10 -> x11, starting transfers between devices: 10.1 us -> 12 us  [over(): return lax.ppermute(x, 'band', [(i, i ^ bit) for i in range(4)])]
  transfers between devices with their start and end apart: 11 -> 12, of which waited for: 6 -> 5; matrix products, arithmetic and copies ran while one was open for 15% -> 0% of each run, Pallas kernels for 2% -> 4%
where the time goes in v2:
time: 89.6 us; the launch traced here: 88.7 us
  local copies, waits for them, and re-layouts  23.5 us (26%)
  starting transfers between devices  19.9 us (22%)
  blocking collectives  18.4 us (21%)
  Pallas kernels  17.8 us (20%)
  waiting for transfers between devices  8.36 us (9%)
    unnamed x42, local copies, waits for them, and re-layouts  23.5 us
    all_to_all x1, blocking collectives, per_device(): lax.all_to_all(sent, 'mem', split_axis=0, concat_axis=0, tiled=True)  18.4 us
    ppermute x11, starting transfers between devices, over(): return lax.ppermute(x, 'band', [(i, i ^ bit) for i in range(4)])  12 us
    ppermute x11, waiting for transfers between devices, over(): return lax.ppermute(x, 'band', [(i, i ^ bit) for i in range(4)])  8.36 us
    all_to_all x1, starting transfers between devices, per_device(): lax.all_to_all(payload, 'mem', split_axis=0, concat_axis=0, tiled=True)  7.92 us
    pallas_call x1, Pallas kernels, per_device(): call(obs_body, [VM] * 9, [(shape((8, 1024), F32), VM)] * 2 + [(shape((256...  5.99 us
    pallas_call x1, Pallas kernels, per_device(): call(gradient_body, [VM] * 8, [(shape((16, 128), F32), VM)] * 4, 5 * 10 *...  4.13 us
    pallas_call x1, Pallas kernels, per_device(): call(prep_body, [VM, VM, VM, ANY], [(shape((448, 512), BF), VM), (shape((...  2.27 us
  transfers between devices with their start and end apart: 12, of which 5 were waited for; matrix products, arithmetic and copies ran while one was open for 0% of the time, Pallas kernels for 4%

profile of v2, /device:TPU:0, one launch (start us, length us, event | category | flops | bytes accessed | tf_op | source)
XLA Modules:
  0.0 88.7 jit_solution(9681712297983558595)
XLA Ops:
  0.6 1.2 %copy-done.3 = bf16[28,16,1024]{2,1,0:T(8,128)(2,1)S(1)} copy-done((bf16[28,16,1024]{2,1,0:T(8,128)(2,1)S(1)}, bf16[28,16,1024]{2,1,0:T(8,128)(2,1)}, u32[]{:S(2)}) %copy-start.3) | copy-done | bytes 917528
  1.8 1.0 %copy-done.5 = f32[1,256,512]{2,1,0:T(8,128)S(1)} copy-done((f32[1,256,512]{2,1,0:T(8,128)S(1)}, f32[1,256,512]{2,1,0:T(8,128)}, u32[]{:S(2)}) %copy-start.5) | copy-done | bytes 524312
  2.9 1.0 %copy-done.6 = f32[1,256,512]{2,1,0:T(8,128)S(1)} copy-done((f32[1,256,512]{2,1,0:T(8,128)S(1)}, f32[1,256,512]{2,1,0:T(8,128)}, u32[]{:S(2)}) %copy-start.6) | copy-done | bytes 524312
  4.6 1.6 %shard_map.97 = (bf16[28,8,1024]{2,1,0:T(8,128)(2,1)S(1)}, bf16[28,8,1024]{2,1,0:T(8,128)(2,1)}, bf16[32,16,256]{2,1,0:T(8,128)(2,1)}, f32[256,128]{1,0:T(8,128)S(1)}, f32[256,128]{1,0:T(8,128)S(1)}) custom-call(bf16[28,16,1024]{2,1,0:T(8,128)(2,1)S(1)} %copy-done.3, f32[1,256,512]{2,1,0:T(8,128)S(1)} %copy-done.5, f32[1,256,512]{2,1,0:T(8,128)S(1)} %copy-done.6, ...), custom_call_target="tpu_custom_call" | custom-call | flops 1000000 | bytes 5000000 | tf_op jit(solution)/shard_map/pallas_call | solution.py:263
  6.3 1.0 %copy-done.4 = bf16[16,16,1024]{2,1,0:T(8,128)(2,1)S(1)} copy-done((bf16[16,16,1024]{2,1,0:T(8,128)(2,1)S(1)}, bf16[16,16,1024]{2,1,0:T(8,128)(2,1)}, u32[]{:S(2)}) %copy-start.4) | copy-done | bytes 524312
  8.1 4.1 %collective-permute-start.2 = (bf16[128,1024]{1,0:T(8,128)(2,1)}, bf16[128,1024]{1,0:T(8,128)(2,1)}, u32[]{:S(2)}, u32[]{:S(2)}) collective-permute-start(bf16[128,1024]{1,0:T(8,128)(2,1)} %bitcast.4), channel_id=1, source_target_pairs={{0,96},{32,64},{64,32},{96,0},{1,97},{33,65},{65,33},{97,1},{2,98}... | collective-permute-start | bytes 786440 | tf_op jit(solution)/shard_map/ppermute | solution.py:252
  12.7 7.9 %all-to-all-start = ((bf16[32,16,256]{2,1,0:T(8,128)(2,1)}), bf16[32,16,256]{2,1,0:T(8,128)(2,1)S(1)}, u32[]{:S(2)}, u32[]{:S(2)}) async-start(bf16[32,16,256]{2,1,0:T(8,128)(2,1)} %get-tuple-element.30), calls=%async_computation | async-start | bytes 524288 | tf_op jit(solution)/shard_map/all_to_all | solution.py:272
  20.7 5.8 %copy-done = bf16[64,256,512]{2,1,0:T(8,128)(2,1)S(1)} copy-done((bf16[64,256,512]{2,1,0:T(8,128)(2,1)S(1)}, bf16[64,256,512]{2,1,0:T(8,128)(2,1)}, u32[]{:S(2)}) %copy-start) | copy-done | bytes 16777240
  28.6 2.3 %shard_map.95 = (bf16[448,512]{1,0:T(8,128)(2,1)S(1)}, bf16[1024,1024]{1,0:T(8,128)(2,1)S(1)}, bf16[64,256]{1,0:T(8,128)(2,1)S(1)}, bf16[64,256,256]{2,1,0:T(8,128)(2,1)S(1)}) custom-call(f32[64,112]{1,0:T(8,128)S(1)} %bitcast.13, s32[16,64]{1,0:T(8,128)S(1)} %bitcast.17, s32[16,128]{1,0:T(8,128)S(1)} %bitcast.16, bf16[64,256,512]{2,1,0:T(8,128)(2,1)S(1)} %copy-done), custom_call_target="tpu_custom_call" | custom-call | flops 100000000 | bytes 20000000 | tf_op jit(solution)/shard_map/pallas_call | solution.py:274
  30.9 3.3 %copy-done.1 = bf16[64,256,256]{2,1,0:T(8,128)(2,1)} copy-done((bf16[64,256,256]{2,1,0:T(8,128)(2,1)}, bf16[64,256,256]{2,1,0:T(8,128)(2,1)S(1)}, u32[]{:S(2)}) %copy-start.1) | copy-done | bytes 8388632
  34.1 0.8 copy-done.7
  36.5 1.0 %copy-done.8 = bf16[448,512]{1,0:T(8,128)(2,1)S(1)} copy-done((bf16[448,512]{1,0:T(8,128)(2,1)S(1)}, bf16[448,512]{1,0:T(8,128)(2,1)}, u32[]{:S(2)}) %copy-start.8) | copy-done | bytes 458776
  37.5 2.2 %shard_map.99.p0 = f32[8,1024]{1,0:T(8,128)S(1)} custom-call(bf16[448,512]{1,0:T(8,128)(2,1)S(1)} %copy-done.8, bf16[128,1024]{1,0:T(8,128)(2,1)S(1)} %bitcast.11, bf16[128,1024]{1,0:T(8,128)(2,1)} %collective-permute-done.refs_2_.m1, bf16[128,1024]{1,0:T(8,128)(2,1)} %collective-permute-done.1.refs_3_.m2, ...), custom_call_target="tpu_custom_call" | custom-call | flops 500000000 | bytes 2000000 | tf_op jit(solution)/shard_map/pallas_call | solution.py:285
  39.7 3.2 %collective-permute-start.6 = (f32[8,1024]{1,0:T(8,128)S(1)}, f32[8,1024]{1,0:T(8,128)S(1)}, u32[]{:S(2)}, u32[]{:S(2)}) collective-permute-start(f32[8,1024]{1,0:T(8,128)S(1)} %shard_map.99.p0), channel_id=1, source_target_pairs={{0,96},{32,64},{64,32},{96,0},{1,97},{33,65},{65,33},{97,1},{2,98}... | collective-permute-start | bytes 98312 | tf_op jit(solution)/shard_map/ppermute | solution.py:252
  43.5 1.1 %collective-permute-done.6.p3 = f32[8,1024]{1,0:T(8,128)S(1)} collective-permute-done((f32[8,1024]{1,0:T(8,128)S(1)}, f32[8,1024]{1,0:T(8,128)S(1)}, u32[]{:S(2)}, u32[]{:S(2)}) %collective-permute-start.6) | collective-permute-done | bytes 32800 | tf_op jit(solution)/shard_map/ppermute | solution.py:252
  44.7 3.7 %collective-permute-done.5.p2 = f32[8,1024]{1,0:T(8,128)S(1)} collective-permute-done((f32[8,1024]{1,0:T(8,128)S(1)}, f32[8,1024]{1,0:T(8,128)S(1)}, u32[]{:S(2)}, u32[]{:S(2)}) %collective-permute-start.5) | collective-permute-done | bytes 32800 | tf_op jit(solution)/shard_map/ppermute | solution.py:252
  48.3 3.4 %copy-done.2 = bf16[64,256,256]{2,1,0:T(8,128)(2,1)S(1)} copy-done((bf16[64,256,256]{2,1,0:T(8,128)(2,1)S(1)}, bf16[64,256,256]{2,1,0:T(8,128)(2,1)}, u32[]{:S(2)}) %copy-start.2) | copy-done | bytes 8388632
  52.5 6.0 %shard_map.100 = (f32[8,1024]{1,0:T(8,128)S(1)}, f32[8,1024]{1,0:T(8,128)S(1)}, f32[256,128]{1,0:T(8,128)S(1)}) custom-call(f32[8,1024]{1,0:T(8,128)S(1)} %shard_map.99.p0, f32[8,1024]{1,0:T(8,128)S(1)} %collective-permute-done.4.p1, f32[8,1024]{1,0:T(8,128)S(1)} %collective-permute-done.5.p2, f32[8,1024]{1,0:T(8,128)S(1)} %collective-permute-done.6.p3, ...), custom_call_target="tpu_custom_call" | custom-call | flops 1000000000 | bytes 12000000 | tf_op jit(solution)/shard_map/pallas_call | solution.py:293
  58.5 1.2 %collective-permute-done.7.a1 = f32[8,1024]{1,0:T(8,128)S(1)} collective-permute-done((f32[8,1024]{1,0:T(8,128)S(1)}, f32[8,1024]{1,0:T(8,128)S(1)}, u32[]{:S(2)}, u32[]{:S(2)}) %collective-permute-start.7) | collective-permute-done | bytes 32800 | tf_op jit(solution)/shard_map/ppermute | solution.py:252
  59.7 4.1 %shard_map.101 = (f32[16,128]{1,0:T(8,128)S(1)}, f32[16,128]{1,0:T(8,128)S(1)}, f32[16,128]{1,0:T(8,128)S(1)}, f32[16,128]{1,0:T(8,128)S(1)}) custom-call(f32[8,1024]{1,0:T(8,128)S(1)} %get-tuple-element.35.a0, f32[8,1024]{1,0:T(8,128)S(1)} %collective-permute-done.7.a1, bf16[128,1024]{1,0:T(8,128)(2,1)S(1)} %bitcast.12, ...), custom_call_target="tpu_custom_call" | custom-call | flops 500000000 | bytes 2000000 | tf_op jit(solution)/shard_map/pallas_call | solution.py:300
  64.0 1.0 %collective-permute-start.9 = (f32[16,128]{1,0:T(8,128)S(1)}, f32[16,128]{1,0:T(8,128)S(1)}, u32[]{:S(2)}, u32[]{:S(2)}) collective-permute-start(f32[16,128]{1,0:T(8,128)S(1)} %get-tuple-element.39), channel_id=1, source_target_pairs={{0,64},{32,96},{64,0},{96,32},{1,65},{33,97},{65,1},{97,33},{2,66}... | collective-permute-start | bytes 24584 | tf_op jit(solution)/shard_map/ppermute | solution.py:252
  65.0 2.2 %collective-permute-start.10 = (f32[16,128]{1,0:T(8,128)S(1)}, f32[16,128]{1,0:T(8,128)S(1)}, u32[]{:S(2)}, u32[]{:S(2)}) collective-permute-start(f32[16,128]{1,0:T(8,128)S(1)} %get-tuple-element.40), channel_id=1, source_target_pairs={{0,96},{32,64},{64,32},{96,0},{1,97},{33,65},{65,33},{97,1},{2,98}... | collective-permute-start | bytes 24584 | tf_op jit(solution)/shard_map/ppermute | solution.py:252
  67.3 1.9 %collective-permute-done.9.g2 = f32[16,128]{1,0:T(8,128)S(1)} collective-permute-done((f32[16,128]{1,0:T(8,128)S(1)}, f32[16,128]{1,0:T(8,128)S(1)}, u32[]{:S(2)}, u32[]{:S(2)}) %collective-permute-start.9) | collective-permute-done | bytes 8224 | tf_op jit(solution)/shard_map/ppermute | solution.py:252
  69.6 18.4 %all_to_all.10.refs_0_ = f32[32,24,128]{2,1,0:T(8,128)S(1)} all-to-all(f32[32,24,128]{2,1,0:T(8,128)S(1)} %shard_map.102), channel_id=1, replica_groups=mesh['band'=4,'mem'=32] {'mem'}, dimensions={0} | all-to-all | bytes 786432 | tf_op jit(solution)/shard_map/all_to_all | solution.py:310
  (52 shorter events, 8.6 us)
Async XLA Ops:
  0.6 1.2 %copy-start.3 = (bf16[28,16,1024]{2,1,0:T(8,128)(2,1)S(1)}, bf16[28,16,1024]{2,1,0:T(8,128)(2,1)}, u32[]{:S(2)}) copy-start(bf16[28,16,1024]{2,1,0:T(8,128)(2,1)} %eig.1) | copy-start | bytes 2752516
  1.8 1.0 %copy-start.5 = (f32[1,256,512]{2,1,0:T(8,128)S(1)}, f32[1,256,512]{2,1,0:T(8,128)}, u32[]{:S(2)}) copy-start(f32[1,256,512]{2,1,0:T(8,128)} %innovation.1) | copy-start | bytes 1572868
  2.9 1.0 %copy-start.6 = (f32[1,256,512]{2,1,0:T(8,128)S(1)}, f32[1,256,512]{2,1,0:T(8,128)}, u32[]{:S(2)}) copy-start(f32[1,256,512]{2,1,0:T(8,128)} %obs_weight.1) | copy-start | bytes 1572868
  6.2 6.1 %copy-start.14 = (f32[256,128]{1,0:T(8,128)}, f32[256,128]{1,0:T(8,128)S(1)}, u32[]{:S(2)}) copy-start(f32[256,128]{1,0:T(8,128)S(1)} %get-tuple-element.42.refs_2_) | copy-start | bytes 393220
  6.2 6.0 %copy-start.16 = (f32[256,128]{1,0:T(8,128)}, f32[256,128]{1,0:T(8,128)S(1)}, u32[]{:S(2)}) copy-start(f32[256,128]{1,0:T(8,128)S(1)} %get-tuple-element.43.refs_3_) | copy-start | bytes 393220
  6.2 30.3 %collective-permute-start.3 = (bf16[224,1024]{1,0:T(8,128)(2,1)}, bf16[224,1024]{1,0:T(8,128)(2,1)S(1)}, u32[]{:S(2)}, u32[]{:S(2)}) collective-permute-start(bf16[224,1024]{1,0:T(8,128)(2,1)} %bitcast.6), channel_id=1, source_target_pairs={{0,32},{32,0},{64,96},{96,64},{1,33},{33,1},{65,97},{97,65},{2,34}... | collective-permute-start | bytes 1376264 | tf_op jit(solution)/shard_map/ppermute | solution.py:252
  6.3 1.0 %copy-start.4 = (bf16[16,16,1024]{2,1,0:T(8,128)(2,1)S(1)}, bf16[16,16,1024]{2,1,0:T(8,128)(2,1)}, u32[]{:S(2)}) copy-start(bf16[16,16,1024]{2,1,0:T(8,128)(2,1)} %src.1) | copy-start | bytes 1572868
  8.1 28.4 %collective-permute-start.2 = (bf16[128,1024]{1,0:T(8,128)(2,1)}, bf16[128,1024]{1,0:T(8,128)(2,1)}, u32[]{:S(2)}, u32[]{:S(2)}) collective-permute-start(bf16[128,1024]{1,0:T(8,128)(2,1)} %bitcast.4), channel_id=1, source_target_pairs={{0,96},{32,64},{64,32},{96,0},{1,97},{33,65},{65,33},{97,1},{2,98}... | collective-permute-start | bytes 786440 | tf_op jit(solution)/shard_map/ppermute | solution.py:252
  12.2 24.2 %collective-permute-start = (bf16[128,1024]{1,0:T(8,128)(2,1)}, bf16[128,1024]{1,0:T(8,128)(2,1)}, u32[]{:S(2)}, u32[]{:S(2)}) collective-permute-start(bf16[128,1024]{1,0:T(8,128)(2,1)} %bitcast.4), channel_id=1, source_target_pairs={{0,32},{32,0},{64,96},{96,64},{1,33},{33,1},{65,97},{97,65},{2,34}... | collective-permute-start | bytes 786440 | tf_op jit(solution)/shard_map/ppermute | solution.py:252
  12.3 24.2 %collective-permute-start.1 = (bf16[128,1024]{1,0:T(8,128)(2,1)S(1)}, bf16[128,1024]{1,0:T(8,128)(2,1)}, u32[]{:S(2)}, u32[]{:S(2)}) collective-permute-start(bf16[128,1024]{1,0:T(8,128)(2,1)S(1)} %bitcast.10), channel_id=1, source_target_pairs={{0,64},{32,96},{64,0},{96,32},{1,65},{33,97},{65,1},{97,33},{2,66}... | collective-permute-start | bytes 786440 | tf_op jit(solution)/shard_map/ppermute | solution.py:252
  12.7 22.8 %all-to-all-start = ((bf16[32,16,256]{2,1,0:T(8,128)(2,1)}), bf16[32,16,256]{2,1,0:T(8,128)(2,1)S(1)}, u32[]{:S(2)}, u32[]{:S(2)}) async-start(bf16[32,16,256]{2,1,0:T(8,128)(2,1)} %get-tuple-element.30), calls=%async_computation | async-start | bytes 524288 | tf_op jit(solution)/shard_map/all_to_all | solution.py:272
  20.7 5.8 %copy-start = (bf16[64,256,512]{2,1,0:T(8,128)(2,1)S(1)}, bf16[64,256,512]{2,1,0:T(8,128)(2,1)}, u32[]{:S(2)}) copy-start(bf16[64,256,512]{2,1,0:T(8,128)(2,1)} %interpolation.1) | copy-start | bytes 50331652
  30.9 3.3 %copy-start.1 = (bf16[64,256,256]{2,1,0:T(8,128)(2,1)}, bf16[64,256,256]{2,1,0:T(8,128)(2,1)S(1)}, u32[]{:S(2)}) copy-start(bf16[64,256,256]{2,1,0:T(8,128)(2,1)S(1)} %get-tuple-element.34.interp) | copy-start | bytes 25165828
  36.3 51.7 %copy-start.13 = (f32[112,64]{0,1:T(8,128)S(1)}, f32[112,64]{0,1:T(8,128)}, u32[]{:S(2)}) copy-start(f32[112,64]{0,1:T(8,128)} %param.10) | copy-start | bytes 86020
  36.3 51.7 %copy-start.15 = (f32[256,128]{1,0:T(8,128)S(1)}, f32[256,128]{1,0:T(8,128)}, u32[]{:S(2)}) copy-start(f32[256,128]{1,0:T(8,128)} %copy-done.14) | copy-start | bytes 393220
  36.3 51.7 %copy-start.17 = (f32[256,128]{1,0:T(8,128)S(1)}, f32[256,128]{1,0:T(8,128)}, u32[]{:S(2)}) copy-start(f32[256,128]{1,0:T(8,128)} %copy-done.16) | copy-start | bytes 393220
  39.7 4.9 %collective-permute-start.6 = (f32[8,1024]{1,0:T(8,128)S(1)}, f32[8,1024]{1,0:T(8,128)S(1)}, u32[]{:S(2)}, u32[]{:S(2)}) collective-permute-start(f32[8,1024]{1,0:T(8,128)S(1)} %shard_map.99.p0), channel_id=1, source_target_pairs={{0,96},{32,64},{64,32},{96,0},{1,97},{33,65},{65,33},{97,1},{2,98}... | collective-permute-start | bytes 98312 | tf_op jit(solution)/shard_map/ppermute | solution.py:252
  42.9 5.4 %collective-permute-start.5 = (f32[8,1024]{1,0:T(8,128)S(1)}, f32[8,1024]{1,0:T(8,128)S(1)}, u32[]{:S(2)}, u32[]{:S(2)}) collective-permute-start(f32[8,1024]{1,0:T(8,128)S(1)} %shard_map.99.p0), channel_id=1, source_target_pairs={{0,64},{32,96},{64,0},{96,32},{1,65},{33,97},{65,1},{97,33},{2,66}... | collective-permute-start | bytes 98312 | tf_op jit(solution)/shard_map/ppermute | solution.py:252
  43.5 4.8 %collective-permute-start.4 = (f32[8,1024]{1,0:T(8,128)S(1)}, f32[8,1024]{1,0:T(8,128)S(1)}, u32[]{:S(2)}, u32[]{:S(2)}) collective-permute-start(f32[8,1024]{1,0:T(8,128)S(1)} %shard_map.99.p0), channel_id=1, source_target_pairs={{0,32},{32,0},{64,96},{96,64},{1,33},{33,1},{65,97},{97,65},{2,34}... | collective-permute-start | bytes 98312 | tf_op jit(solution)/shard_map/ppermute | solution.py:252
  48.3 3.4 %copy-start.2 = (bf16[64,256,256]{2,1,0:T(8,128)(2,1)S(1)}, bf16[64,256,256]{2,1,0:T(8,128)(2,1)}, u32[]{:S(2)}) copy-start(bf16[64,256,256]{2,1,0:T(8,128)(2,1)} %copy-done.1) | copy-start | bytes 25165828
  58.5 1.3 %collective-permute-start.7 = (f32[8,1024]{1,0:T(8,128)S(1)}, f32[8,1024]{1,0:T(8,128)S(1)}, u32[]{:S(2)}, u32[]{:S(2)}) collective-permute-start(f32[8,1024]{1,0:T(8,128)S(1)} %get-tuple-element.36), channel_id=1, source_target_pairs={{0,32},{32,0},{64,96},{96,64},{1,33},{33,1},{65,97},{97,65},{2,34}... | collective-permute-start | bytes 98312 | tf_op jit(solution)/shard_map/ppermute | solution.py:252
  63.9 3.4 %collective-permute-start.8 = (f32[16,128]{1,0:T(8,128)S(1)}, f32[16,128]{1,0:T(8,128)S(1)}, u32[]{:S(2)}, u32[]{:S(2)}) collective-permute-start(f32[16,128]{1,0:T(8,128)S(1)} %get-tuple-element.38), channel_id=1, source_target_pairs={{0,32},{32,0},{64,96},{96,64},{1,33},{33,1},{65,97},{97,65},{2,34}... | collective-permute-start | bytes 24584 | tf_op jit(solution)/shard_map/ppermute | solution.py:252
  64.0 5.2 %collective-permute-start.9 = (f32[16,128]{1,0:T(8,128)S(1)}, f32[16,128]{1,0:T(8,128)S(1)}, u32[]{:S(2)}, u32[]{:S(2)}) collective-permute-start(f32[16,128]{1,0:T(8,128)S(1)} %get-tuple-element.39), channel_id=1, source_target_pairs={{0,64},{32,96},{64,0},{96,32},{1,65},{33,97},{65,1},{97,33},{2,66}... | collective-permute-start | bytes 24584 | tf_op jit(solution)/shard_map/ppermute | solution.py:252
  65.0 4.6 %collective-permute-start.10 = (f32[16,128]{1,0:T(8,128)S(1)}, f32[16,128]{1,0:T(8,128)S(1)}, u32[]{:S(2)}, u32[]{:S(2)}) collective-permute-start(f32[16,128]{1,0:T(8,128)S(1)} %get-tuple-element.40), channel_id=1, source_target_pairs={{0,96},{32,64},{64,32},{96,0},{1,97},{33,65},{65,33},{97,1},{2,98}... | collective-permute-start | bytes 24584 | tf_op jit(solution)/shard_map/ppermute | solution.py:252
  (9 other events, 6.8 us)

commit v3 on v2

v3 whole, which is shorter than its diff:
```python
import math

import jax
import jax.numpy as jnp
from jax import lax
from jax.experimental import pallas as pl
from jax.experimental.pallas import tpu as pltpu
from jax.sharding import PartitionSpec as P

BF = jnp.bfloat16
F32 = jnp.float32
NN = (((1,), (0,)), ((), ()))
NT = (((1,), (1,)), ((), ()))
TN = (((0,), (0,)), ((), ()))
MIB = 1024 * 1024
VM = pl.BlockSpec(memory_space=pltpu.VMEM)
ANY = pl.BlockSpec(memory_space=pl.ANY)
HB = pl.BlockSpec(memory_space=pltpu.HBM)


def dot(a, b, dims=NN):
    return lax.dot_general(a, b, dims, preferred_element_type=F32)


def parts3(x):
    hi = x.astype(BF)
    rest = x - hi.astype(F32)
    mid = rest.astype(BF)
    lo = (rest - mid.astype(F32)).astype(BF)
    return hi, mid, lo


def iota(dims, dim):
    return lax.broadcasted_iota(jnp.int32, dims, dim)


def ones_where(cond):
    return cond.astype(F32).astype(BF)


def shape(dims, dtype):
    return jax.ShapeDtypeStruct(dims, dtype)


def in_hbm(x):
    return pltpu.with_memory_space_constraint(x, pltpu.HBM)


def in_vmem(x):
    return pltpu.with_memory_space_constraint(x, pltpu.VMEM)


def call(body, ins, outs, flops, nbytes, scratch=(), vmem=16):
    return pl.pallas_call(
        body,
        out_shape=tuple(o for o, _ in outs),
        in_specs=list(ins),
        out_specs=tuple(s for _, s in outs),
        scratch_shapes=list(scratch),
        compiler_params=pltpu.CompilerParams(vmem_limit_bytes=vmem * MIB),
        cost_estimate=pl.CostEstimate(flops=flops, bytes_accessed=nbytes, transcendentals=0),
    )


def start_all(copies):
    for c in copies:
        c.start()
    return copies


def wait_all(copies):
    for c in copies:
        c.wait()


def halves_copies(src, mine, mate, sem, at):
    core = lax.axis_index("band") & 1
    lo = pl.multiple_of(core * 8, 8)
    hi = pl.multiple_of(8 - core * 8, 8)
    return [
        pltpu.make_async_copy(src.at[:, pl.ds(hi, 8), :], mate, sem.at[at]),
        pltpu.make_async_copy(src.at[:, pl.ds(lo, 8), :], mine, sem.at[at + 1]),
    ]


def quarter_at(side):
    core = lax.axis_index("band") & 1
    return pl.ds(pl.multiple_of((core + 2 * side) * 128, 128), 128)


def load_body(mem, eig, innovation, obs_weight, m_mine, m_mate, e_mine, e_mate, payload, iv, sem):
    slices = start_all(halves_copies(mem, m_mine, m_mate, sem, 0))
    copies = start_all([
        pltpu.make_async_copy(
            a.at[0, :, quarter_at(side)], iv.at[n, :, side * 128:(side + 1) * 128], sem.at[4 + 2 * n + side])
        for n, a in enumerate((innovation, obs_weight)) for side in range(2)
    ])
    slices += start_all(halves_copies(eig, e_mine, e_mate, sem, 2))
    wait_all(copies)
    for n in range(2):
        payload[:, n * 8:(n + 1) * 8, :] = iv[n].reshape(32, 8, 256).astype(BF)
    wait_all(slices)


def increment_of(scale, kron, members, eig, cut):
    mixed = dot(kron, members[:, cut])
    return scale * jnp.sum((mixed * eig[:, cut].astype(F32)).reshape(56, 8, 256), axis=0)


def increment_own(scale, control_t, ma, mb, ea, eb, out, kron, ct, members, eig, sem):
    get = start_all([
        pltpu.make_async_copy(a, b, sem.at[n]) for n, (a, b) in enumerate((
            (control_t, ct), (ma, members.at[:128]), (mb, members.at[128:]), (ea, eig.at[:224]), (eb, eig.at[224:])))
    ])
    band = lax.axis_index("band")
    row = iota((448, 112), 0)
    second = (row >= 224).astype(jnp.int32)
    mode = (band ^ second) * 28 + ((row - 224 * second) >> 3)
    pick_rows = ones_where(mode == iota((448, 112), 1))
    col = iota((64, 512), 1)
    member = (band ^ (col >> 7)) * 16 + ((col & 127) >> 3)
    pick_cols = ones_where(member == iota((64, 512), 0))
    same = (iota((448, 512), 0) & 7) == (iota((448, 512), 1) & 7)
    get[0].wait()
    rows = dot(pick_rows, ct[...].astype(BF), NT).astype(BF)
    full = jnp.where(same, dot(rows, pick_cols), 0.0).astype(BF)
    kron[...] = full[:, 256:]
    wait_all(get[1:])
    for g in range(0, 1024, 256):
        cut = slice(g, g + 256)
        out[:, cut] = increment_of(scale, full[:, :256], members, eig, cut)


def increment_other(scale, kron_in, before_in, m0, m1, m2, m3, ea, eb, _, out, eig, members, kron, before, sem):
    first = start_all([pltpu.make_async_copy(kron_in, kron, sem.at[0]), pltpu.make_async_copy(before_in, before, sem.at[1])])
    chunks = [slice(g, g + 256) for g in range(0, 1024, 256)]
    later = [
        start_all([
            pltpu.make_async_copy(a.at[:, cut], b.at[rows, cut], sem.at[2 + 4 * n + i]) for i, (a, b, rows) in enumerate((
                (m2, members, slice(256, 384)), (m3, members, slice(384, 512)),
                (ea, eig, slice(0, 224)), (eb, eig, slice(224, 448))))
        ]) for n, cut in enumerate(chunks)
    ]
    last = start_all([
        pltpu.make_async_copy(m0, members.at[:128], sem.at[18]), pltpu.make_async_copy(m1, members.at[128:256], sem.at[19])])
    wait_all(first)
    for cut, get in zip(chunks, later):
        wait_all(get)
        out[:, cut] = before[:, cut] + increment_of(scale, kron[...], members.at[256:], eig, cut)
    wait_all(last)


def prep_body(columns_t, owners_in, interpolation, got_in, innovation, obs_weight, _,
              onehot, place, interp, innov, weight, innov_own, live_own,
              cols_s, own_s, got, sem):
    band = lax.axis_index("band")
    tile = lax.axis_index("mem")
    quarter = pl.ds(pl.multiple_of(band * 128, 128), 128)
    small = [(columns_t, cols_s), (owners_in, own_s), (got_in, got)]
    mid = [(innovation.at[0, :, quarter], innov_own), (obs_weight.at[0, :, quarter], live_own)]
    big = [(interpolation.at[:, :, quarter_at(side)], interp.at[:, :, side * 128:(side + 1) * 128]) for side in range(2)]
    copies = start_all([pltpu.make_async_copy(a, b, sem.at[n]) for n, (a, b) in enumerate(small + mid + big)])
    wait_all(copies[:3])
    t = iota((64, 1024), 1)
    cols = cols_s[...].astype(F32).T.astype(jnp.int32)
    for c in range(16):
        onehot[c * 64:(c + 1) * 64, :] = ones_where(cols[:, c:c + 1] == t)
    pair = own_s[pl.ds(tile >> 1, 1), :].astype(F32)
    own = jnp.where((tile & 1) == 1, pair[:, 64:], pair[:, :64])
    own_row = jnp.broadcast_to(own, (64, 64))
    own_col = own_row.T
    earlier = iota((64, 64), 1) < iota((64, 64), 0)
    rank = jnp.sum(jnp.where((own_row == own_col) & earlier, 1.0, 0.0), axis=1, keepdims=True)
    target = (own_col[:, :1] * 8.0 + rank).astype(jnp.int32)
    sel = ones_where(target == iota((64, 256), 1))
    place[...] = sel
    x = got[...].astype(F32)
    innov[...] = dot(sel, x[:, :8].reshape(256, 256).astype(BF))
    weight[...] = dot(sel, x[:, 8:].reshape(256, 256).astype(BF))
    hit = ones_where(own_s[...] == tile)
    pair = ones_where((iota((256, 16), 0) >> 4) == iota((256, 16), 1))
    odd = (iota((256, 128), 0) >> 3) & 1
    side = jnp.where((iota((256, 128), 1) >> 6) == odd, dot(pair, hit), 0.0)
    count = jnp.sum(side, axis=1, keepdims=True)
    live = jnp.where((iota((256, 1), 0) & 7).astype(F32) < count, 1.0, 0.0)
    wait_all(copies[3:5])
    live_own[...] = live * live_own[...]
    wait_all(copies[5:])


def add_body(a, b, _, out):
    out[...] = (a[...] + b[...]).astype(BF)


def obs_body(inc_my, inc_mt, onehot, place, innov, weight, interp, adj_my, adj_mt, slots, picked, depb, spread):
    band = lax.axis_index("band")
    first = (band & 1) == 0
    mine = inc_my[...].astype(F32)
    mate = inc_mt[...].astype(F32)
    inc = jnp.concatenate([jnp.where(first, mine, mate), jnp.where(first, mate, mine)], axis=0).astype(BF)
    picks = dot(onehot[...], inc, NT)
    by_col = jnp.concatenate([picks[c * 64:(c + 1) * 64] for c in range(16)], axis=1).astype(BF)
    r0 = iota((256, 256), 0)
    r1 = iota((256, 256), 1)
    swap = ones_where(((r0 & 15) * 16 + (r0 >> 4)) == r1)
    picked[...] = dot(by_col, swap).astype(BF)
    rows = iota((16, 256), 0)
    image = []
    for b in range(4):
        lhs = picked[b * 16:(b + 1) * 16, :]
        acc = jnp.zeros((16, 256), F32)
        for i in range(16):
            acc = jnp.where(rows == i, dot(lhs, interp[b * 16 + i]), acc)
        image.append(acc)
    image = jnp.concatenate(image, axis=0)
    depb[...] = (weight[...] * (innov[...] - image)).astype(BF)
    for b in range(4):
        lhs = depb[b * 16:(b + 1) * 16, :]
        acc = jnp.zeros((16, 256), F32)
        for i in range(16):
            acc = jnp.where(rows == i, dot(lhs, interp[b * 16 + i], NT), acc)
        spread[b * 16:(b + 1) * 16, :] = acc
    x = spread[...]
    hi = x.astype(BF)
    lo = (x - hi.astype(F32)).astype(BF)
    terms = []
    for part in (hi, lo):
        turned = dot(swap, part, NT)
        terms.append(jnp.concatenate([turned[c * 16:(c + 1) * 16] for c in range(16)], axis=1))
    both = dot(jnp.concatenate(terms, axis=0).astype(BF), onehot[...])
    adj = both[:16] + both[16:]
    adj_my[...] = jnp.where(first, adj[:8], adj[8:])
    adj_mt[...] = jnp.where(first, adj[8:], adj[:8])
    sel = place[...]
    hi, mid, lo = parts3(jnp.where((band >> 1) == 0, image[:, :128], image[:, 128:]))
    slots[...] = dot(sel, hi, TN) + dot(sel, mid, TN) + dot(sel, lo, TN)


def gradient_body(a0, a1, eig, members, mate, mine):
    first = (lax.axis_index("band") & 1) == 0
    adj = a0[...] + a1[...]
    wide = jnp.broadcast_to(adj[None], (16, 8, 1024)).reshape(128, 1024)
    same = (iota((448, 256), 0) & 7) == (iota((448, 256), 1) & 7)
    sel = ones_where((iota((32, 256), 1) >> 3) == iota((32, 256), 0))
    for a, b, g in ((1, 3, mate), (0, 2, mine)):
        weighted = jnp.concatenate(
            [(members[p * 128:(p + 1) * 128].astype(F32) * wide).astype(BF) for p in (a, b)], axis=0)
        full = jnp.where(same, dot(eig[...], weighted, NT), 0.0)
        own = jnp.sum(full.reshape(56, 8, 256), axis=1)
        own = jnp.where(first, own, jnp.concatenate([own[28:], own[:28]], axis=0))
        hi, mid, lo = parts3(own)
        g[...] = dot(sel, hi, NT) + dot(sel, mid, NT) + dot(sel, lo, NT)


def pack_body(mine, came, slots, out):
    total = mine[...] + came[...]
    gap = jnp.zeros((8, 8), F32)
    flat = [
        jnp.concatenate([total[r:r + 8], gap, total[r + 8:r + 16], gap], axis=1) for r in (0, 16)
    ]
    high = (lax.axis_index("band") >> 1) == 1
    image = slots[...].reshape(32, 8, 128)
    for side in range(2):
        here = high if side else jnp.logical_not(high)
        rows = slice(side * 32, side * 32 + 32)
        out[rows, :8, :] = image
        out[rows, 8:, :] = jnp.broadcast_to(jnp.where(here, flat[0], flat[1])[None], (32, 8, 128))


def final_body(scale, got, control_t, innov, live, gradient_t, departures):
    band = lax.axis_index("band")
    image = got[pl.ds((band >> 1) * 32, 32), :8, :].reshape(256, 128)
    departures[...] = (live[...] * (innov[...] - image)).reshape(1, 256, 128)
    low = jnp.sum(got[:32, 8:, :], axis=0)
    top = jnp.sum(got[32:, 8:, :], axis=0)
    total = jnp.concatenate([
        jnp.concatenate([low[:, :56], top[:, :56]], axis=1),
        jnp.concatenate([low[:, 64:120], top[:, 64:120]], axis=1),
    ], axis=0)
    own = ones_where(iota((16, 64), 1) == band * 16 + iota((16, 64), 0))
    hi, mid, lo = parts3(control_t[...])
    gradient_t[...] = dot(own, hi) + dot(own, mid) + dot(own, lo) - scale * total


def per_device(members, eigvecs, control, columns, interpolation, owners, innovation, obs_weight):
    scale = 1.0 / math.sqrt(112 * 64)
    owners = owners.reshape(16, 128)

    def over(x, bit):
        return lax.ppermute(x, "band", [(i, i ^ bit) for i in range(4)])

    dma = pltpu.SemaphoreType.DMA
    m_my, m_mt, e_my, e_mt, payload = call(
        load_body,
        [HB] * 4,
        [(pltpu.HBM((16, 8, 1024), BF), HB)] * 2 + [(pltpu.HBM((28, 8, 1024), BF), HB)] * 2
        + [(pltpu.HBM((32, 16, 256), BF), VM)],
        10 ** 6, 5 * 10 ** 6,
        [pltpu.VMEM((2, 256, 256), F32), dma((8,))],
    )(in_hbm(members), in_hbm(eigvecs), in_hbm(innovation), in_hbm(obs_weight))
    m_my, m_mt, e0, e_mt = [in_hbm(a.reshape(-1, 1024)) for a in (m_my, m_mt, e_my, e_mt)]
    m3 = over(m_mt, 3)
    m2 = over(m_my, 2)
    m1 = over(m_mt, 1)
    got = lax.all_to_all(payload, "mem", split_axis=0, concat_axis=0, tiled=True)
    e1 = over(e_mt, 1)
    m1, m2, m3, e1 = [in_vmem(a) for a in (m1, m2, m3, e1)]

    part, kron = call(
        lambda *refs: increment_own(scale, *refs), [HB, HB, VM, HB, VM],
        [(pltpu.HBM((8, 1024), F32), VM), (pltpu.HBM((448, 256), BF), VM)],
        25 * 10 ** 7, 2 * 10 ** 6,
        [pltpu.VMEM((64, 112), F32), pltpu.VMEM((256, 1024), BF), pltpu.VMEM((448, 1024), BF), dma((5,))],
    )(in_hbm(control.T), m_my, m1, e0, e1)
    part, eig, ensemble = call(
        lambda *refs: increment_other(scale, *refs), [HB] * 3 + [VM] * 3 + [HB, VM, ANY],
        [(shape((8, 1024), F32), VM), (pltpu.VMEM((448, 1024), BF), VM), (pltpu.VMEM((512, 1024), BF), VM)],
        25 * 10 ** 7, 2 * 10 ** 6,
        [pltpu.VMEM((448, 256), BF), pltpu.VMEM((8, 1024), F32), dma((20,))],
    )(in_hbm(kron), in_hbm(part), m_my, m1, m2, m3, e0, e1, got)
    eig, ensemble = in_vmem(eig), in_vmem(ensemble)

    kept = call(
        prep_body,
        [HB] * 3 + [ANY] + [HB] * 2 + [ANY],
        [(pltpu.VMEM(d, t), VM) for d, t in (
            ((1024, 1024), BF), ((64, 256), BF), ((64, 256, 256), BF), ((64, 256), F32), ((64, 256), F32),
            ((256, 128), F32), ((256, 128), F32))],
        10 ** 8, 12 * 10 ** 6,
        [pltpu.VMEM((16, 64), jnp.int32), pltpu.VMEM((16, 128), jnp.int32), pltpu.VMEM((32, 16, 256), BF), dma((7,))],
    )(in_hbm(columns.T), in_hbm(owners), in_hbm(interpolation), got, in_hbm(innovation), in_hbm(obs_weight), part)
    onehot, place, interp, innov, weight, innov_own, live_own = [in_vmem(a) for a in kept]

    (inc_my,) = call(
        add_body, [VM, VM, ANY], [(shape((8, 1024), BF), VM)], 10 ** 4, 10 ** 5
    )(part, over(part, 2), place)
    inc_mt = over(inc_my, 1)
    adj_my, adj_mt, slots = call(
        obs_body, [VM] * 7,
        [(shape((8, 1024), F32), VM)] * 2 + [(pltpu.VMEM((256, 128), F32), VM)],
        10 ** 9, 12 * 10 ** 6,
        [pltpu.VMEM((64, 256), BF), pltpu.VMEM((64, 256), BF), pltpu.VMEM((64, 256), F32)],
    )(inc_my, inc_mt, onehot, place, innov, weight, interp)

    g_mt, g_my = call(
        gradient_body, [VM] * 4, [(shape((32, 56), F32), VM)] * 2, 5 * 10 ** 8, 2 * 10 ** 6
    )(adj_my, over(adj_mt, 1), eig, ensemble)

    (sent,) = call(
        pack_body, [VM] * 3, [(shape((64, 16, 128), F32), VM)], 10 ** 5, 6 * 10 ** 5
    )(g_my, over(g_mt, 1), in_vmem(slots))
    groups = [[(2 * z + core) * 32 + t for z in range(2) for t in range(32)] for core in range(2)]
    arrived = lax.all_to_all(
        sent, ("band", "mem"), split_axis=0, concat_axis=0, axis_index_groups=groups, tiled=True)
    gradient_t, departures = call(
        lambda *refs: final_body(scale, *refs), [VM] * 4,
        [(shape((16, 112), F32), VM), (shape((1, 256, 128), F32), VM)], 10 ** 6, 6 * 10 ** 5,
    )(arrived, control.T, innov_own, live_own)
    return (gradient_t.T, departures)


def solution(mesh):
    return jax.shard_map(
        per_device,
        mesh=mesh,
        in_specs=(
            P("band", None, "mem"),
            P("band", None, "mem"),
            P(),
            P("mem", None),
            P("mem", None, None),
            P(),
            P("mem", None, None),
            P("mem", None, None),
        ),
        out_specs=(P(None, "band"), P("mem", None, "band")),
        check_vma=False,
    )
```

time: 89.6 us -> 109 us (1.22)
  Pallas kernels: 17.8 us -> 62.3 us
  local copies, waits for them, and re-layouts: 23.5 us -> 0.01 us
  starting transfers between devices: 19.9 us -> 16.5 us
  waiting for transfers between devices: 8.36 us -> 11.2 us
    pallas_call x8, Pallas kernels: 17.1 us -> 61.5 us  [the longest x1 45.6 us: per_device(): call(load_body, [HB] * 4, [(pltpu.HBM((16, 8, 1024), BF), HB)] * 2 + [(pl...]
    unnamed x42 -> x2, local copies, waits for them, and re-layouts: 23.5 us -> 0.01 us
    all_to_all x1, waiting for transfers between devices: 0.01 us -> 7.93 us  [per_device(): lax.all_to_all(payload, 'mem', split_axis=0, concat_axis=0, tiled=True)]
    ppermute x11 -> x8, waiting for transfers between devices: 8.36 us -> 3.25 us  [over(): return lax.ppermute(x, 'band', [(i, i ^ bit) for i in range(4)])]
    ppermute x11 -> x8, starting transfers between devices: 12 us -> 8.76 us  [over(): return lax.ppermute(x, 'band', [(i, i ^ bit) for i in range(4)])]
  transfers between devices with their start and end apart: 12 -> 9, of which waited for: 5 -> 4; matrix products, arithmetic and copies ran while one was open for 0% -> 0% of each run, Pallas kernels for 4% -> 5%
where the time goes in v3:
time: 109 us
  Pallas kernels  62.3 us (57%)
  blocking collectives  18.4 us (17%)
  starting transfers between devices  16.5 us (15%)
  waiting for transfers between devices  11.2 us (10%)
    pallas_call x1, Pallas kernels, per_device(): call(load_body, [HB] * 4, [(pltpu.HBM((16, 8, 1024), BF), HB)] * 2 + [(pl...  45.6 us
    all_to_all x1, blocking collectives, per_device(): lax.all_to_all(sent, ('band', 'mem'), split_axis=0, concat_axis=0, axis_i...  18.4 us
    ppermute x8, starting transfers between devices, over(): return lax.ppermute(x, 'band', [(i, i ^ bit) for i in range(4)])  8.76 us
    all_to_all x1, waiting for transfers between devices, per_device(): lax.all_to_all(payload, 'mem', split_axis=0, concat_axis=0, tiled=True)  7.93 us
    all_to_all x1, starting transfers between devices, per_device(): lax.all_to_all(payload, 'mem', split_axis=0, concat_axis=0, tiled=True)  7.79 us
    pallas_call x1, Pallas kernels, per_device(): call(obs_body, [VM] * 7, [(shape((8, 1024), F32), VM)] * 2 + [(pltpu.VMEM...  5.99 us
    pallas_call x1, Pallas kernels, per_device(): call(prep_body, [HB] * 3 + [ANY] + [HB] * 2 + [ANY], [(pltpu.VMEM(d, t),...  3.72 us
    ppermute x8, waiting for transfers between devices, over(): return lax.ppermute(x, 'band', [(i, i ^ bit) for i in range(4)])  3.25 us
  transfers between devices with their start and end apart: 9, of which 4 were waited for; matrix products, arithmetic and copies ran while one was open for 0% of the time, Pallas kernels for 5%

profile of v3, /device:TPU:0, one launch (start us, length us, event | category | flops | bytes accessed | tf_op | source)
XLA Modules:
  0.0 109.2 jit_solution(13140137720955958203)
XLA Ops:
  0.6 45.6 %shard_map.95 = (bf16[16,8,1024]{2,1,0:T(8,128)(2,1)}, bf16[16,8,1024]{2,1,0:T(8,128)(2,1)}, bf16[28,8,1024]{2,1,0:T(8,128)(2,1)}, bf16[28,8,1024]{2,1,0:T(8,128)(2,1)}, bf16[32,16,256]{2,1,0:T(8,128)(2,1)}) custom-call(bf16[16,16,1024]{2,1,0:T(8,128)(2,1)} %mem.1, bf16[28,16,1024]{2,1,0:T(8,128)(2,1)} %eig.1, f32[1,256,512]{2,1,0:T(8,128)} %innovation.3, ...), custom_call_target="tpu_custom_call" | custom-call | flops 1000000 | bytes 5000000 | tf_op jit(solution)/shard_map/pallas_call | solution.py:293
  46.2 0.1 collective-permute-start.1
  46.3 0.5 collective-permute-start
  46.8 4.0 %collective-permute-start.2 = (bf16[128,1024]{1,0:T(8,128)(2,1)}, bf16[128,1024]{1,0:T(8,128)(2,1)S(1)}, u32[]{:S(2)}, u32[]{:S(2)}) collective-permute-start(bf16[128,1024]{1,0:T(8,128)(2,1)} %bitcast.12), channel_id=1, source_target_pairs={{0,64},{32,96},{64,0},{96,32},{1,65},{33,97},{65,1},{97,33},{2,66}... | collective-permute-start | bytes 786440 | tf_op jit(solution)/shard_map/ppermute | solution.py:290
  50.7 0.0 collective-permute-start.3
  50.7 7.8 %all-to-all-start = ((bf16[32,16,256]{2,1,0:T(8,128)(2,1)}), bf16[32,16,256]{2,1,0:T(8,128)(2,1)S(1)}, u32[]{:S(2)}, u32[]{:S(2)}) async-start(bf16[32,16,256]{2,1,0:T(8,128)(2,1)} %get-tuple-element.32), calls=%async_computation | async-start | bytes 524288 | tf_op jit(solution)/shard_map/all_to_all | solution.py:305
  58.6 0.0 collective-permute-done.1.refs_4_.refs_7_
  58.6 2.3 %shard_map.96 = (f32[8,1024]{1,0:T(8,128)}, bf16[448,256]{1,0:T(8,128)(2,1)}) custom-call(f32[64,112]{1,0:T(8,128)} %bitcast.8, bf16[128,1024]{1,0:T(8,128)(2,1)} %bitcast.13, bf16[128,1024]{1,0:T(8,128)(2,1)S(1)} %collective-permute-done.refs_2_.refs_3_, bf16[224,1024]{1,0:T(8,128)(2,1)} %bitcast.10, ...), custom_call_target="tpu_custom_call" | custom-call | flops 250000000 | bytes 2000000 | tf_op jit(solution)/shard_map/pallas_call | solution.py:309
  60.8 7.9 %all-to-all-done.refs_8_.got_in = bf16[32,16,256]{2,1,0:T(8,128)(2,1)S(1)} async-done(((bf16[32,16,256]{2,1,0:T(8,128)(2,1)}), bf16[32,16,256]{2,1,0:T(8,128)(2,1)S(1)}, u32[]{:S(2)}, u32[]{:S(2)}) %all-to-all-start) | async-done | bytes 262176 | tf_op jit(solution)/shard_map/all_to_all | solution.py:305
  68.8 2.3 %shard_map.97 = (f32[8,1024]{1,0:T(8,128)S(1)}, bf16[448,1024]{1,0:T(8,128)(2,1)S(1)}, bf16[512,1024]{1,0:T(8,128)(2,1)S(1)}) custom-call(bf16[448,256]{1,0:T(8,128)(2,1)} %get-tuple-element.30.refs_0_, f32[8,1024]{1,0:T(8,128)} %get-tuple-element.31.refs_1_, bf16[128,1024]{1,0:T(8,128)(2,1)} %bitcast.14, ...), custom_call_target="tpu_custom_call" | custom-call | flops 250000000 | bytes 2000000 | tf_op jit(solution)/shard_map/pallas_call | solution.py:315
  71.1 3.7 %collective-permute-start.4 = (f32[8,1024]{1,0:T(8,128)S(1)}, f32[8,1024]{1,0:T(8,128)S(1)}, u32[]{:S(2)}, u32[]{:S(2)}) collective-permute-start(f32[8,1024]{1,0:T(8,128)S(1)} %get-tuple-element.33._.a), channel_id=1, source_target_pairs={{0,64},{32,96},{64,0},{96,32},{1,65},{33,97},{65,1},{97,33},{2,66}... | collective-permute-start | bytes 98312 | tf_op jit(solution)/shard_map/ppermute | solution.py:290
  74.8 3.7 %shard_map.98 = (bf16[1024,1024]{1,0:T(8,128)(2,1)S(1)}, bf16[64,256]{1,0:T(8,128)(2,1)S(1)}, bf16[64,256,256]{2,1,0:T(8,128)(2,1)S(1)}, f32[64,256]{1,0:T(8,128...) custom-call(s32[16,64]{1,0:T(8,128)} %bitcast.15, s32[16,128]{1,0:T(8,128)} %bitcast.16, ...), custom_call_target="tpu_custom_call" | custom-call | flops 100000000 | bytes 12000000 | tf_op jit(solution)/shard_map/pallas_call | solution.py:323
  78.5 0.0 copy-start
  78.6 0.1 collective-permute-start.5
  78.7 1.2 %collective-permute-done.5.inc_mt = bf16[8,1024]{1,0:T(8,128)(2,1)S(1)} collective-permute-done((bf16[8,1024]{1,0:T(8,128)(2,1)S(1)}, bf16[8,1024]{1,0:T(8,128)(2,1)S(1)}, u32[]{:S(2)}, u32[]{:S(2)}) %collective-permute-start.5) | collective-permute-done | bytes 16416 | tf_op jit(solution)/shard_map/ppermute | solution.py:290
  79.8 6.0 %shard_map.100 = (f32[8,1024]{1,0:T(8,128)S(1)}, f32[8,1024]{1,0:T(8,128)S(1)}, f32[256,128]{1,0:T(8,128)S(1)}) custom-call(bf16[8,1024]{1,0:T(8,128)(2,1)S(1)} %shard_map.99.inc_my, bf16[8,1024]{1,0:T(8,128)(2,1)S(1)} %collective-permute-done.5.inc_mt, bf16[1024,1024]{1,0:T(8,128)(2,1)S(1)} %get-tuple-element.35.onehot, ...), custom_call_target="tpu_custom_call" | custom-call | flops 1000000000 | bytes 12000000 | tf_op jit(solution)/shard_map/pallas_call | solution.py:338
  85.8 0.2 collective-permute-start.6
  86.1 1.0 collective-permute-done.6.a1
  87.1 1.6 %shard_map.101 = (f32[32,56]{1,0:T(8,128)S(1)}, f32[32,56]{1,0:T(8,128)S(1)}) custom-call(f32[8,1024]{1,0:T(8,128)S(1)} %get-tuple-element.39.a0, f32[8,1024]{1,0:T(8,128)S(1)} %collective-permute-done.6.a1, bf16[448,1024]{1,0:T(8,128)(2,1)S(1)} %get-tuple-element.41.eig, bf16[512,1024]{1,0:T(8,128)(2,1)S(1)} %get-tuple-element.42.members), custom_call_target="tpu_custom_call" | custom-call | flops 500000000 | bytes 2000000 | tf_op jit(solution)/shard_map/pallas_call | solution.py:345
  88.7 0.2 collective-permute-start.7
  88.9 1.0 collective-permute-done.7.came
  89.9 0.1 shard_map.102
  90.0 18.4 %all_to_all.10.refs_0_ = f32[64,16,128]{2,1,0:T(8,128)S(1)} all-to-all(f32[64,16,128]{2,1,0:T(8,128)S(1)} %shard_map.102), channel_id=1, replica_groups={{0,1,2,3,4,5,6,7,8,9,10,11,12,13,14,15,16,17,18,19,20,21,22,23,24,25,26..., dimensions={0} | all-to-all | bytes 1048576 | tf_op jit(solution)/shard_map/all_to_all | solution.py:353
  108.4 0.7 shard_map.103
  (6 shorter events, 0.0 us)
Async XLA Ops:
  46.2 12.4 %collective-permute-start.1 = (bf16[224,1024]{1,0:T(8,128)(2,1)}, bf16[224,1024]{1,0:T(8,128)(2,1)S(1)}, u32[]{:S(2)}, u32[]{:S(2)}) collective-permute-start(bf16[224,1024]{1,0:T(8,128)(2,1)} %bitcast.17), channel_id=1, source_target_pairs={{0,32},{32,0},{64,96},{96,64},{1,33},{33,1},{65,97},{97,65},{2,34}... | collective-permute-start | bytes 1376264 | tf_op jit(solution)/shard_map/ppermute | solution.py:290
  46.3 12.3 %collective-permute-start = (bf16[128,1024]{1,0:T(8,128)(2,1)}, bf16[128,1024]{1,0:T(8,128)(2,1)S(1)}, u32[]{:S(2)}, u32[]{:S(2)}) collective-permute-start(bf16[128,1024]{1,0:T(8,128)(2,1)} %bitcast.18), channel_id=1, source_target_pairs={{0,32},{32,0},{64,96},{96,64},{1,33},{33,1},{65,97},{97,65},{2,34}... | collective-permute-start | bytes 786440 | tf_op jit(solution)/shard_map/ppermute | solution.py:290
  46.8 22.0 %collective-permute-start.2 = (bf16[128,1024]{1,0:T(8,128)(2,1)}, bf16[128,1024]{1,0:T(8,128)(2,1)S(1)}, u32[]{:S(2)}, u32[]{:S(2)}) collective-permute-start(bf16[128,1024]{1,0:T(8,128)(2,1)} %bitcast.12), channel_id=1, source_target_pairs={{0,64},{32,96},{64,0},{96,32},{1,65},{33,97},{65,1},{97,33},{2,66}... | collective-permute-start | bytes 786440 | tf_op jit(solution)/shard_map/ppermute | solution.py:290
  50.7 18.0 %collective-permute-start.3 = (bf16[128,1024]{1,0:T(8,128)(2,1)}, bf16[128,1024]{1,0:T(8,128)(2,1)S(1)}, u32[]{:S(2)}, u32[]{:S(2)}) collective-permute-start(bf16[128,1024]{1,0:T(8,128)(2,1)} %bitcast.19), channel_id=1, source_target_pairs={{0,96},{32,64},{64,32},{96,0},{1,97},{33,65},{65,33},{97,1},{2,98}... | collective-permute-start | bytes 786440 | tf_op jit(solution)/shard_map/ppermute | solution.py:290
  50.7 18.0 %all-to-all-start = ((bf16[32,16,256]{2,1,0:T(8,128)(2,1)}), bf16[32,16,256]{2,1,0:T(8,128)(2,1)S(1)}, u32[]{:S(2)}, u32[]{:S(2)}) async-start(bf16[32,16,256]{2,1,0:T(8,128)(2,1)} %get-tuple-element.32), calls=%async_computation | async-start | bytes 524288 | tf_op jit(solution)/shard_map/all_to_all | solution.py:305
  71.1 7.4 %collective-permute-start.4 = (f32[8,1024]{1,0:T(8,128)S(1)}, f32[8,1024]{1,0:T(8,128)S(1)}, u32[]{:S(2)}, u32[]{:S(2)}) collective-permute-start(f32[8,1024]{1,0:T(8,128)S(1)} %get-tuple-element.33._.a), channel_id=1, source_target_pairs={{0,64},{32,96},{64,0},{96,32},{1,65},{33,97},{65,1},{97,33},{2,66}... | collective-permute-start | bytes 98312 | tf_op jit(solution)/shard_map/ppermute | solution.py:290
  78.5 29.9 %copy-start = (f32[112,64]{0,1:T(8,128)S(1)}, f32[112,64]{0,1:T(8,128)}, u32[]{:S(2)}) copy-start(f32[112,64]{0,1:T(8,128)} %param.10) | copy-start | bytes 86020
  78.6 1.3 %collective-permute-start.5 = (bf16[8,1024]{1,0:T(8,128)(2,1)S(1)}, bf16[8,1024]{1,0:T(8,128)(2,1)S(1)}, u32[]{:S(2)}, u32[]{:S(2)}) collective-permute-start(bf16[8,1024]{1,0:T(8,128)(2,1)S(1)} %shard_map.99.inc_my), channel_id=1, source_target_pairs={{0,32},{32,0},{64,96},{96,64},{1,33},{33,1},{65,97},{97,65},{2,34}... | collective-permute-start | bytes 49160 | tf_op jit(solution)/shard_map/ppermute | solution.py:290
  85.8 1.3 %collective-permute-start.6 = (f32[8,1024]{1,0:T(8,128)S(1)}, f32[8,1024]{1,0:T(8,128)S(1)}, u32[]{:S(2)}, u32[]{:S(2)}) collective-permute-start(f32[8,1024]{1,0:T(8,128)S(1)} %get-tuple-element.40), channel_id=1, source_target_pairs={{0,32},{32,0},{64,96},{96,64},{1,33},{33,1},{65,97},{97,65},{2,34}... | collective-permute-start | bytes 98312 | tf_op jit(solution)/shard_map/ppermute | solution.py:290
  88.7 1.2 %collective-permute-start.7 = (f32[32,56]{1,0:T(8,128)S(1)}, f32[32,56]{1,0:T(8,128)S(1)}, u32[]{:S(2)}, u32[]{:S(2)}) collective-permute-start(f32[32,56]{1,0:T(8,128)S(1)} %get-tuple-element.44), channel_id=1, source_target_pairs={{0,32},{32,0},{64,96},{96,64},{1,33},{33,1},{65,97},{97,65},{2,34}... | collective-permute-start | bytes 21512 | tf_op jit(solution)/shard_map/ppermute | solution.py:290

commit v4 on v3

--- a/solution.py
+++ b/solution.py
@@ -102,16 +102,16 @@
     wait_all(slices)
 
 
-def increment_of(scale, kron, members, eig, cut):
-    mixed = dot(kron, members[:, cut])
-    return scale * jnp.sum((mixed * eig[:, cut].astype(F32)).reshape(56, 8, 256), axis=0)
-
-
-def increment_own(scale, control_t, ma, mb, ea, eb, out, kron, ct, members, eig, sem):
-    get = start_all([
-        pltpu.make_async_copy(a, b, sem.at[n]) for n, (a, b) in enumerate((
-            (control_t, ct), (ma, members.at[:128]), (mb, members.at[128:]), (ea, eig.at[:224]), (eb, eig.at[224:])))
-    ])
+def increment_of(scale, kron, ma, mb, ea, eb, cut):
+    mixed = dot(kron, jnp.concatenate([ma[:, cut], mb[:, cut]], axis=0))
+    total = jnp.sum((mixed[:224] * ea[:, cut].astype(F32)).reshape(28, 8, 256), axis=0)
+    total = total + jnp.sum((mixed[224:] * eb[:, cut].astype(F32)).reshape(28, 8, 256), axis=0)
+    return scale * total
+
+
+def increment_own(scale, control_t, ma, mb, ea, eb, out, kron, ct, sem):
+    get = pltpu.make_async_copy(control_t, ct, sem)
+    get.start()
     band = lax.axis_index("band")
     row = iota((448, 112), 0)
     second = (row >= 224).astype(jnp.int32)
@@ -121,33 +121,19 @@
     member = (band ^ (col >> 7)) * 16 + ((col & 127) >> 3)
     pick_cols = ones_where(member == iota((64, 512), 0))
     same = (iota((448, 512), 0) & 7) == (iota((448, 512), 1) & 7)
-    get[0].wait()
+    get.wait()
     rows = dot(pick_rows, ct[...].astype(BF), NT).astype(BF)
     full = jnp.where(same, dot(rows, pick_cols), 0.0).astype(BF)
     kron[...] = full[:, 256:]
-    wait_all(get[1:])
     for g in range(0, 1024, 256):
         cut = slice(g, g + 256)
-        out[:, cut] = increment_of(scale, full[:, :256], members, eig, cut)
-
-
-def increment_other(scale, kron_in, before_in, m0, m1, m2, m3, ea, eb, _, out, eig, members, kron, before, sem):
-    first = start_all([pltpu.make_async_copy(kron_in, kron, sem.at[0]), pltpu.make_async_copy(before_in, before, sem.at[1])])
-    chunks = [slice(g, g + 256) for g in range(0, 1024, 256)]
-    later = [
-        start_all([
-            pltpu.make_async_copy(a.at[:, cut], b.at[rows, cut], sem.at[2 + 4 * n + i]) for i, (a, b, rows) in enumerate((
-                (m2, members, slice(256, 384)), (m3, members, slice(384, 512)),
-                (ea, eig, slice(0, 224)), (eb, eig, slice(224, 448))))
-        ]) for n, cut in enumerate(chunks)
-    ]
-    last = start_all([
-        pltpu.make_async_copy(m0, members.at[:128], sem.at[18]), pltpu.make_async_copy(m1, members.at[128:256], sem.at[19])])
-    wait_all(first)
-    for cut, get in zip(chunks, later):
-        wait_all(get)
-        out[:, cut] = before[:, cut] + increment_of(scale, kron[...], members.at[256:], eig, cut)
-    wait_all(last)
+        out[:, cut] = increment_of(scale, full[:, :256], ma, mb, ea, eb, cut)
+
+
+def increment_other(scale, kron, before, ma, mb, ea, eb, _, out):
+    for g in range(0, 1024, 256):
+        cut = slice(g, g + 256)
+        out[:, cut] = before[:, cut] + increment_of(scale, kron[...], ma, mb, ea, eb, cut)
 
 
 def prep_body(columns_t, owners_in, interpolation, got_in, innovation, obs_weight, _,
@@ -236,16 +222,17 @@
     slots[...] = dot(sel, hi, TN) + dot(sel, mid, TN) + dot(sel, lo, TN)
 
 
-def gradient_body(a0, a1, eig, members, mate, mine):
+def gradient_body(a0, a1, m0, m1, m2, m3, e0, e1, mate, mine):
     first = (lax.axis_index("band") & 1) == 0
     adj = a0[...] + a1[...]
     wide = jnp.broadcast_to(adj[None], (16, 8, 1024)).reshape(128, 1024)
     same = (iota((448, 256), 0) & 7) == (iota((448, 256), 1) & 7)
     sel = ones_where((iota((32, 256), 1) >> 3) == iota((32, 256), 0))
-    for a, b, g in ((1, 3, mate), (0, 2, mine)):
+    eig = jnp.concatenate([e0[...], e1[...]], axis=0)
+    for ma, mb, g in ((m1, m3, mate), (m0, m2, mine)):
         weighted = jnp.concatenate(
-            [(members[p * 128:(p + 1) * 128].astype(F32) * wide).astype(BF) for p in (a, b)], axis=0)
-        full = jnp.where(same, dot(eig[...], weighted, NT), 0.0)
+            [(m[...].astype(F32) * wide).astype(BF) for m in (ma, mb)], axis=0)
+        full = jnp.where(same, dot(eig, weighted, NT), 0.0)
         own = jnp.sum(full.reshape(56, 8, 256), axis=1)
         own = jnp.where(first, own, jnp.concatenate([own[28:], own[:28]], axis=0))
         hi, mid, lo = parts3(own)
@@ -293,12 +280,12 @@
     m_my, m_mt, e_my, e_mt, payload = call(
         load_body,
         [HB] * 4,
-        [(pltpu.HBM((16, 8, 1024), BF), HB)] * 2 + [(pltpu.HBM((28, 8, 1024), BF), HB)] * 2
+        [(pltpu.VMEM((16, 8, 1024), BF), VM)] * 2 + [(pltpu.VMEM((28, 8, 1024), BF), VM)] * 2
         + [(pltpu.HBM((32, 16, 256), BF), VM)],
         10 ** 6, 5 * 10 ** 6,
         [pltpu.VMEM((2, 256, 256), F32), dma((8,))],
     )(in_hbm(members), in_hbm(eigvecs), in_hbm(innovation), in_hbm(obs_weight))
-    m_my, m_mt, e0, e_mt = [in_hbm(a.reshape(-1, 1024)) for a in (m_my, m_mt, e_my, e_mt)]
+    m_my, m_mt, e0, e_mt = [in_vmem(a.reshape(-1, 1024)) for a in (m_my, m_mt, e_my, e_mt)]
     m3 = over(m_mt, 3)
     m2 = over(m_my, 2)
     m1 = over(m_mt, 1)
@@ -307,18 +294,14 @@
     m1, m2, m3, e1 = [in_vmem(a) for a in (m1, m2, m3, e1)]
 
     part, kron = call(
-        lambda *refs: increment_own(scale, *refs), [HB, HB, VM, HB, VM],
-        [(pltpu.HBM((8, 1024), F32), VM), (pltpu.HBM((448, 256), BF), VM)],
+        lambda *refs: increment_own(scale, *refs), [HB] + [VM] * 4,
+        [(pltpu.VMEM((8, 1024), F32), VM), (pltpu.VMEM((448, 256), BF), VM)],
+        25 * 10 ** 7, 2 * 10 ** 6, [pltpu.VMEM((64, 112), F32), dma(())],
+    )(in_hbm(control.T), m_my, m1, e0, e1)
+    (part,) = call(
+        lambda *refs: increment_other(scale, *refs), [VM] * 6 + [ANY], [(shape((8, 1024), F32), VM)],
         25 * 10 ** 7, 2 * 10 ** 6,
-        [pltpu.VMEM((64, 112), F32), pltpu.VMEM((256, 1024), BF), pltpu.VMEM((448, 1024), BF), dma((5,))],
-    )(in_hbm(control.T), m_my, m1, e0, e1)
-    part, eig, ensemble = call(
-        lambda *refs: increment_other(scale, *refs), [HB] * 3 + [VM] * 3 + [HB, VM, ANY],
-        [(shape((8, 1024), F32), VM), (pltpu.VMEM((448, 1024), BF), VM), (pltpu.VMEM((512, 1024), BF), VM)],
-        25 * 10 ** 7, 2 * 10 ** 6,
-        [pltpu.VMEM((448, 256), BF), pltpu.VMEM((8, 1024), F32), dma((20,))],
-    )(in_hbm(kron), in_hbm(part), m_my, m1, m2, m3, e0, e1, got)
-    eig, ensemble = in_vmem(eig), in_vmem(ensemble)
+    )(in_vmem(kron), in_vmem(part), m2, m3, e0, e1, got)
 
     kept = call(
         prep_body,
@@ -343,8 +326,8 @@
     )(inc_my, inc_mt, onehot, place, innov, weight, interp)
 
     g_mt, g_my = call(
-        gradient_body, [VM] * 4, [(shape((32, 56), F32), VM)] * 2, 5 * 10 ** 8, 2 * 10 ** 6
-    )(adj_my, over(adj_mt, 1), eig, ensemble)
+        gradient_body, [VM] * 8, [(shape((32, 56), F32), VM)] * 2, 5 * 10 ** 8, 2 * 10 ** 6
+    )(adj_my, over(adj_mt, 1), m_my, m1, m2, m3, e0, e1)
 
     (sent,) = call(
         pack_body, [VM] * 3, [(shape((64, 16, 128), F32), VM)], 10 ** 5, 6 * 10 ** 5

time: 109 us -> 64.2 us (0.59)
  Pallas kernels: 62.3 us -> 16.2 us
    pallas_call x4, Pallas kernels: 51.7 us -> 5.7 us  [the longest x1 2.26 us: per_device(): call(load_body, [HB] * 4, [(pltpu.VMEM((16, 8, 1024), BF), VM)] * 2 + [(p...]
  transfers between devices with their start and end apart: 9 -> 9, of which waited for: 4 -> 4; matrix products, arithmetic and copies ran while one was open for 0% -> 0% of each run, Pallas kernels for 5% -> 8%
where the time goes in v4:
time: 64.2 us; the launch traced here: 63.9 us
  blocking collectives  18.4 us (29%)
  starting transfers between devices  16.5 us (26%)
  Pallas kernels  16.2 us (25%)
  waiting for transfers between devices  12 us (19%)
  between operations  0.74 us (1%)
    all_to_all x1, blocking collectives, per_device(): lax.all_to_all(sent, ('band', 'mem'), split_axis=0, concat_axis=0, axis_i...  18.4 us
    ppermute x8, starting transfers between devices, over(): return lax.ppermute(x, 'band', [(i, i ^ bit) for i in range(4)])  8.76 us
    all_to_all x1, waiting for transfers between devices, per_device(): lax.all_to_all(payload, 'mem', split_axis=0, concat_axis=0, tiled=True)  8.76 us
    all_to_all x1, starting transfers between devices, per_device(): lax.all_to_all(payload, 'mem', split_axis=0, concat_axis=0, tiled=True)  7.79 us
    pallas_call x1, Pallas kernels, per_device(): call(obs_body, [VM] * 7, [(shape((8, 1024), F32), VM)] * 2 + [(pltpu.VMEM...  5.99 us
    pallas_call x1, Pallas kernels, per_device(): call(prep_body, [HB] * 3 + [ANY] + [HB] * 2 + [ANY], [(pltpu.VMEM(d, t),...  3.72 us
    ppermute x8, waiting for transfers between devices, over(): return lax.ppermute(x, 'band', [(i, i ^ bit) for i in range(4)])  3.25 us
    pallas_call x1, Pallas kernels, per_device(): call(load_body, [HB] * 4, [(pltpu.VMEM((16, 8, 1024), BF), VM)] * 2 + [(p...  2.26 us
  transfers between devices with their start and end apart: 9, of which 4 were waited for; matrix products, arithmetic and copies ran while one was open for 0% of the time, Pallas kernels for 8%

profile of v4, /device:TPU:0, one launch (start us, length us, event | category | flops | bytes accessed | tf_op | source)
XLA Modules:
  0.0 63.9 jit_solution(9769460374897549649)
XLA Ops:
  0.6 2.3 %shard_map.95 = (bf16[16,8,1024]{2,1,0:T(8,128)(2,1)S(1)}, bf16[16,8,1024]{2,1,0:T(8,128)(2,1)S(1)}, bf16[28,8,1024]{2,1,0:T(8,128)(2,1)S(1)}, bf16[28,8,1024]{2,1,0:T(8,128)(2,1)S(1)}, bf16[32,16,256]{2,1,0:T(8,128)(2,1)}) custom-call(bf16[16,16,1024]{2,1,0:T(8,128)(2,1)} %mem.1, bf16[28,16,1024]{2,1,0:T(8,128)(2,1)} %eig.1, f32[1,256,512]{2,1,0:T(8,128)} %innovation.3, ...), custom_call_target="tpu_custom_call" | custom-call | flops 1000000 | bytes 5000000 | tf_op jit(solution)/shard_map/pallas_call | solution.py:280
  2.9 0.1 collective-permute-start.1
  3.0 0.5 collective-permute-start
  3.5 4.0 %collective-permute-start.2 = (bf16[128,1024]{1,0:T(8,128)(2,1)S(1)}, bf16[128,1024]{1,0:T(8,128)(2,1)S(1)}, u32[]{:S(2)}, u32[]{:S(2)}) collective-permute-start(bf16[128,1024]{1,0:T(8,128)(2,1)S(1)} %bitcast.11), channel_id=1, source_target_pairs={{0,64},{32,96},{64,0},{96,32},{1,65},{33,97},{65,1},{97,33},{2,66}... | collective-permute-start | bytes 786440 | tf_op jit(solution)/shard_map/ppermute | solution.py:277
  7.5 0.0 collective-permute-start.3
  7.5 7.8 %all-to-all-start = ((bf16[32,16,256]{2,1,0:T(8,128)(2,1)}), bf16[32,16,256]{2,1,0:T(8,128)(2,1)S(1)}, u32[]{:S(2)}, u32[]{:S(2)}) async-start(bf16[32,16,256]{2,1,0:T(8,128)(2,1)} %get-tuple-element.29), calls=%async_computation | async-start | bytes 524288 | tf_op jit(solution)/shard_map/all_to_all | solution.py:292
  15.3 0.0 collective-permute-done.refs_2_.m1
  15.3 1.4 %shard_map.96 = (f32[8,1024]{1,0:T(8,128)S(1)}, bf16[448,256]{1,0:T(8,128)(2,1)S(1)}) custom-call(f32[64,112]{1,0:T(8,128)} %bitcast.14, bf16[128,1024]{1,0:T(8,128)(2,1)S(1)} %bitcast.12, bf16[128,1024]{1,0:T(8,128)(2,1)S(1)} %collective-permute-done.refs_2_.m1, bf16[224,1024]{1,0:T(8,128)(2,1)S(1)} %bitcast.8, ...), custom_call_target="tpu_custom_call" | custom-call | flops 250000000 | bytes 2000000 | tf_op jit(solution)/shard_map/pallas_call | solution.py:296
  16.7 8.8 %all-to-all-done.refs_6_.got_in = bf16[32,16,256]{2,1,0:T(8,128)(2,1)S(1)} async-done(((bf16[32,16,256]{2,1,0:T(8,128)(2,1)}), bf16[32,16,256]{2,1,0:T(8,128)(2,1)S(1)}, u32[]{:S(2)}, u32[]{:S(2)}) %all-to-all-start) | async-done | bytes 262176 | tf_op jit(solution)/shard_map/all_to_all | solution.py:292
  25.5 0.4 shard_map.97._.a
  25.9 3.7 %collective-permute-start.4 = (f32[8,1024]{1,0:T(8,128)S(1)}, f32[8,1024]{1,0:T(8,128)S(1)}, u32[]{:S(2)}, u32[]{:S(2)}) collective-permute-start(f32[8,1024]{1,0:T(8,128)S(1)} %shard_map.97._.a), channel_id=1, source_target_pairs={{0,64},{32,96},{64,0},{96,32},{1,65},{33,97},{65,1},{97,33},{2,66}... | collective-permute-start | bytes 98312 | tf_op jit(solution)/shard_map/ppermute | solution.py:277
  29.6 3.7 %shard_map.98 = (bf16[1024,1024]{1,0:T(8,128)(2,1)S(1)}, bf16[64,256]{1,0:T(8,128)(2,1)S(1)}, bf16[64,256,256]{2,1,0:T(8,128)(2,1)S(1)}, f32[64,256]{1,0:T(8,128...) custom-call(s32[16,64]{1,0:T(8,128)} %bitcast.19, s32[16,128]{1,0:T(8,128)} %bitcast.20, ...), custom_call_target="tpu_custom_call" | custom-call | flops 100000000 | bytes 12000000 | tf_op jit(solution)/shard_map/pallas_call | solution.py:306
  33.3 0.0 copy-start
  33.4 0.1 collective-permute-start.5
  33.5 1.2 %collective-permute-done.5.inc_mt = bf16[8,1024]{1,0:T(8,128)(2,1)S(1)} collective-permute-done((bf16[8,1024]{1,0:T(8,128)(2,1)S(1)}, bf16[8,1024]{1,0:T(8,128)(2,1)S(1)}, u32[]{:S(2)}, u32[]{:S(2)}) %collective-permute-start.5) | collective-permute-done | bytes 16416 | tf_op jit(solution)/shard_map/ppermute | solution.py:277
  34.6 6.0 %shard_map.100 = (f32[8,1024]{1,0:T(8,128)S(1)}, f32[8,1024]{1,0:T(8,128)S(1)}, f32[256,128]{1,0:T(8,128)S(1)}) custom-call(bf16[8,1024]{1,0:T(8,128)(2,1)S(1)} %shard_map.99.inc_my, bf16[8,1024]{1,0:T(8,128)(2,1)S(1)} %collective-permute-done.5.inc_mt, bf16[1024,1024]{1,0:T(8,128)(2,1)S(1)} %get-tuple-element.31.onehot, ...), custom_call_target="tpu_custom_call" | custom-call | flops 1000000000 | bytes 12000000 | tf_op jit(solution)/shard_map/pallas_call | solution.py:321
  40.6 0.2 collective-permute-start.6
  40.9 1.0 %collective-permute-done.6.a1 = f32[8,1024]{1,0:T(8,128)S(1)} collective-permute-done((f32[8,1024]{1,0:T(8,128)S(1)}, f32[8,1024]{1,0:T(8,128)S(1)}, u32[]{:S(2)}, u32[]{:S(2)}) %collective-permute-start.6) | collective-permute-done | bytes 32800 | tf_op jit(solution)/shard_map/ppermute | solution.py:277
  41.9 1.6 %shard_map.101 = (f32[32,56]{1,0:T(8,128)S(1)}, f32[32,56]{1,0:T(8,128)S(1)}) custom-call(f32[8,1024]{1,0:T(8,128)S(1)} %get-tuple-element.35.a0, f32[8,1024]{1,0:T(8,128)S(1)} %collective-permute-done.6.a1, bf16[128,1024]{1,0:T(8,128)(2,1)S(1)} %bitcast.13, bf16[128,1024]{1,0:T(8,128)(2,1)S(1)} %collective-permute-done.refs_2_.m1, ...), custom_call_target="tpu_custom_call" | custom-call | flops 500000000 | bytes 2000000 | tf_op jit(solution)/shard_map/pallas_call | solution.py:328
  43.5 0.2 collective-permute-start.7
  43.7 1.0 %collective-permute-done.7.came = f32[32,56]{1,0:T(8,128)S(1)} collective-permute-done((f32[32,56]{1,0:T(8,128)S(1)}, f32[32,56]{1,0:T(8,128)S(1)}, u32[]{:S(2)}, u32[]{:S(2)}) %collective-permute-start.7) | collective-permute-done | bytes 7200 | tf_op jit(solution)/shard_map/ppermute | solution.py:277
  44.7 0.1 shard_map.102
  44.8 18.4 %all_to_all.10.refs_0_ = f32[64,16,128]{2,1,0:T(8,128)S(1)} all-to-all(f32[64,16,128]{2,1,0:T(8,128)S(1)} %shard_map.102), channel_id=1, replica_groups={{0,1,2,3,4,5,6,7,8,9,10,11,12,13,14,15,16,17,18,19,20,21,22,23,24,25,26..., dimensions={0} | all-to-all | bytes 1048576 | tf_op jit(solution)/shard_map/all_to_all | solution.py:336
  63.2 0.7 %shard_map.103 = (f32[16,112]{1,0:T(8,128)}, f32[1,256,128]{2,1,0:T(8,128)}) custom-call(f32[64,16,128]{2,1,0:T(8,128)S(1)} %all_to_all.10.refs_0_, f32[64,112]{1,0:T(8,128)S(1)} %bitcast.15, f32[256,128]{1,0:T(8,128)S(1)} %get-tuple-element.40.refs_2_, f32[256,128]{1,0:T(8,128)S(1)} %get-tuple-element.41.refs_3_), custom_call_target="tpu_custom_call" | custom-call | flops 1000000 | bytes 600000 | tf_op jit(solution)/shard_map/pallas_call | solution.py:338
  (6 shorter events, 0.0 us)
Async XLA Ops:
  2.9 12.4 %collective-permute-start.1 = (bf16[224,1024]{1,0:T(8,128)(2,1)S(1)}, bf16[224,1024]{1,0:T(8,128)(2,1)S(1)}, u32[]{:S(2)}, u32[]{:S(2)}) collective-permute-start(bf16[224,1024]{1,0:T(8,128)(2,1)S(1)} %bitcast.16), channel_id=1, source_target_pairs={{0,32},{32,0},{64,96},{96,64},{1,33},{33,1},{65,97},{97,65},{2,34}... | collective-permute-start | bytes 1376264 | tf_op jit(solution)/shard_map/ppermute | solution.py:277
  3.0 12.3 %collective-permute-start = (bf16[128,1024]{1,0:T(8,128)(2,1)S(1)}, bf16[128,1024]{1,0:T(8,128)(2,1)S(1)}, u32[]{:S(2)}, u32[]{:S(2)}) collective-permute-start(bf16[128,1024]{1,0:T(8,128)(2,1)S(1)} %bitcast.17), channel_id=1, source_target_pairs={{0,32},{32,0},{64,96},{96,64},{1,33},{33,1},{65,97},{97,65},{2,34}... | collective-permute-start | bytes 786440 | tf_op jit(solution)/shard_map/ppermute | solution.py:277
  3.5 22.0 %collective-permute-start.2 = (bf16[128,1024]{1,0:T(8,128)(2,1)S(1)}, bf16[128,1024]{1,0:T(8,128)(2,1)S(1)}, u32[]{:S(2)}, u32[]{:S(2)}) collective-permute-start(bf16[128,1024]{1,0:T(8,128)(2,1)S(1)} %bitcast.11), channel_id=1, source_target_pairs={{0,64},{32,96},{64,0},{96,32},{1,65},{33,97},{65,1},{97,33},{2,66}... | collective-permute-start | bytes 786440 | tf_op jit(solution)/shard_map/ppermute | solution.py:277
  7.5 18.0 %collective-permute-start.3 = (bf16[128,1024]{1,0:T(8,128)(2,1)S(1)}, bf16[128,1024]{1,0:T(8,128)(2,1)S(1)}, u32[]{:S(2)}, u32[]{:S(2)}) collective-permute-start(bf16[128,1024]{1,0:T(8,128)(2,1)S(1)} %bitcast.18), channel_id=1, source_target_pairs={{0,96},{32,64},{64,32},{96,0},{1,97},{33,65},{65,33},{97,1},{2,98}... | collective-permute-start | bytes 786440 | tf_op jit(solution)/shard_map/ppermute | solution.py:277
  7.5 18.0 %all-to-all-start = ((bf16[32,16,256]{2,1,0:T(8,128)(2,1)}), bf16[32,16,256]{2,1,0:T(8,128)(2,1)S(1)}, u32[]{:S(2)}, u32[]{:S(2)}) async-start(bf16[32,16,256]{2,1,0:T(8,128)(2,1)} %get-tuple-element.29), calls=%async_computation | async-start | bytes 524288 | tf_op jit(solution)/shard_map/all_to_all | solution.py:292
  25.9 7.4 %collective-permute-start.4 = (f32[8,1024]{1,0:T(8,128)S(1)}, f32[8,1024]{1,0:T(8,128)S(1)}, u32[]{:S(2)}, u32[]{:S(2)}) collective-permute-start(f32[8,1024]{1,0:T(8,128)S(1)} %shard_map.97._.a), channel_id=1, source_target_pairs={{0,64},{32,96},{64,0},{96,32},{1,65},{33,97},{65,1},{97,33},{2,66}... | collective-permute-start | bytes 98312 | tf_op jit(solution)/shard_map/ppermute | solution.py:277
  33.3 29.8 %copy-start = (f32[112,64]{0,1:T(8,128)S(1)}, f32[112,64]{0,1:T(8,128)}, u32[]{:S(2)}) copy-start(f32[112,64]{0,1:T(8,128)} %param.10) | copy-start | bytes 86020
  33.4 1.3 %collective-permute-start.5 = (bf16[8,1024]{1,0:T(8,128)(2,1)S(1)}, bf16[8,1024]{1,0:T(8,128)(2,1)S(1)}, u32[]{:S(2)}, u32[]{:S(2)}) collective-permute-start(bf16[8,1024]{1,0:T(8,128)(2,1)S(1)} %shard_map.99.inc_my), channel_id=1, source_target_pairs={{0,32},{32,0},{64,96},{96,64},{1,33},{33,1},{65,97},{97,65},{2,34}... | collective-permute-start | bytes 49160 | tf_op jit(solution)/shard_map/ppermute | solution.py:277
  40.6 1.3 %collective-permute-start.6 = (f32[8,1024]{1,0:T(8,128)S(1)}, f32[8,1024]{1,0:T(8,128)S(1)}, u32[]{:S(2)}, u32[]{:S(2)}) collective-permute-start(f32[8,1024]{1,0:T(8,128)S(1)} %get-tuple-element.36), channel_id=1, source_target_pairs={{0,32},{32,0},{64,96},{96,64},{1,33},{33,1},{65,97},{97,65},{2,34}... | collective-permute-start | bytes 98312 | tf_op jit(solution)/shard_map/ppermute | solution.py:277
  43.5 1.2 %collective-permute-start.7 = (f32[32,56]{1,0:T(8,128)S(1)}, f32[32,56]{1,0:T(8,128)S(1)}, u32[]{:S(2)}, u32[]{:S(2)}) collective-permute-start(f32[32,56]{1,0:T(8,128)S(1)} %get-tuple-element.38), channel_id=1, source_target_pairs={{0,32},{32,0},{64,96},{96,64},{1,33},{33,1},{65,97},{97,65},{2,34}... | collective-permute-start | bytes 21512 | tf_op jit(solution)/shard_map/ppermute | solution.py:277

commit v5 on v4

--- a/solution.py
+++ b/solution.py
@@ -137,20 +137,23 @@
 
 
 def prep_body(columns_t, owners_in, interpolation, got_in, innovation, obs_weight, _,
-              onehot, place, interp, innov, weight, innov_own, live_own,
+              onehot, onehot_t, place, interp, innov, weight, innov_own, live_own,
               cols_s, own_s, got, sem):
     band = lax.axis_index("band")
     tile = lax.axis_index("mem")
     quarter = pl.ds(pl.multiple_of(band * 128, 128), 128)
     small = [(columns_t, cols_s), (owners_in, own_s), (got_in, got)]
     mid = [(innovation.at[0, :, quarter], innov_own), (obs_weight.at[0, :, quarter], live_own)]
-    big = [(interpolation.at[:, :, quarter_at(side)], interp.at[:, :, side * 128:(side + 1) * 128]) for side in range(2)]
+    big = [(interpolation.at[:32, :, quarter_at(side)], interp.at[:, :, side * 128:(side + 1) * 128]) for side in range(2)]
     copies = start_all([pltpu.make_async_copy(a, b, sem.at[n]) for n, (a, b) in enumerate(small + mid + big)])
     wait_all(copies[:3])
     t = iota((64, 1024), 1)
     cols = cols_s[...].astype(F32).T.astype(jnp.int32)
     for c in range(16):
         onehot[c * 64:(c + 1) * 64, :] = ones_where(cols[:, c:c + 1] == t)
+    flat = jnp.concatenate([cols_s[c:c + 1, :] for c in range(16)], axis=1)
+    for r in range(0, 1024, 128):
+        onehot_t[r:r + 128, :] = ones_where(flat == iota((128, 1024), 0) + r)
     pair = own_s[pl.ds(tile >> 1, 1), :].astype(F32)
     own = jnp.where((tile & 1) == 1, pair[:, 64:], pair[:, :64])
     own_row = jnp.broadcast_to(own, (64, 64))
@@ -178,25 +181,41 @@
     out[...] = (a[...] + b[...]).astype(BF)
 
 
-def obs_body(inc_my, inc_mt, onehot, place, innov, weight, interp, adj_my, adj_mt, slots, picked, depb, spread):
+def obs_body(inc_my, inc_mt, onehot, onehot_t, place, innov, weight, near, interpolation,
+             adj_my, adj_mt, slots, picked, depb, spread, far, sem):
+    fetch = [
+        start_all([
+            pltpu.make_async_copy(
+                interpolation.at[32 + j:40 + j, :, quarter_at(side)],
+                far.at[j:j + 8, :, side * 128:(side + 1) * 128], sem.at[j // 4 + side])
+            for side in range(2)
+        ]) for j in range(0, 32, 8)
+    ]
+
+    def block(j):
+        return near[j] if j < 32 else far[j - 32]
+
     band = lax.axis_index("band")
     first = (band & 1) == 0
     mine = inc_my[...].astype(F32)
     mate = inc_mt[...].astype(F32)
     inc = jnp.concatenate([jnp.where(first, mine, mate), jnp.where(first, mate, mine)], axis=0).astype(BF)
-    picks = dot(onehot[...], inc, NT)
-    by_col = jnp.concatenate([picks[c * 64:(c + 1) * 64] for c in range(16)], axis=1).astype(BF)
     r0 = iota((256, 256), 0)
     r1 = iota((256, 256), 1)
     swap = ones_where(((r0 & 15) * 16 + (r0 >> 4)) == r1)
-    picked[...] = dot(by_col, swap).astype(BF)
+    picks = dot(inc, onehot_t[...])
+    by_col = jnp.concatenate([picks[:, c * 64:(c + 1) * 64] for c in range(16)], axis=0).astype(BF)
+    picked[...] = dot(by_col, swap, TN).astype(BF)
     rows = iota((16, 256), 0)
     image = []
     for b in range(4):
         lhs = picked[b * 16:(b + 1) * 16, :]
         acc = jnp.zeros((16, 256), F32)
         for i in range(16):
-            acc = jnp.where(rows == i, dot(lhs, interp[b * 16 + i]), acc)
+            j = b * 16 + i
+            if j >= 32 and j % 8 == 0:
+                wait_all(fetch[(j - 32) // 8])
+            acc = jnp.where(rows == i, dot(lhs, block(j)), acc)
         image.append(acc)
     image = jnp.concatenate(image, axis=0)
     depb[...] = (weight[...] * (innov[...] - image)).astype(BF)
@@ -204,7 +223,7 @@
         lhs = depb[b * 16:(b + 1) * 16, :]
         acc = jnp.zeros((16, 256), F32)
         for i in range(16):
-            acc = jnp.where(rows == i, dot(lhs, interp[b * 16 + i], NT), acc)
+            acc = jnp.where(rows == i, dot(lhs, block(b * 16 + i), NT), acc)
         spread[b * 16:(b + 1) * 16, :] = acc
     x = spread[...]
     hi = x.astype(BF)
@@ -301,29 +320,30 @@
     (part,) = call(
         lambda *refs: increment_other(scale, *refs), [VM] * 6 + [ANY], [(shape((8, 1024), F32), VM)],
         25 * 10 ** 7, 2 * 10 ** 6,
-    )(in_vmem(kron), in_vmem(part), m2, m3, e0, e1, got)
+    )(in_vmem(kron), in_vmem(part), m2, m3, e0, e1, m3)
 
     kept = call(
         prep_body,
         [HB] * 3 + [ANY] + [HB] * 2 + [ANY],
         [(pltpu.VMEM(d, t), VM) for d, t in (
-            ((1024, 1024), BF), ((64, 256), BF), ((64, 256, 256), BF), ((64, 256), F32), ((64, 256), F32),
+            ((1024, 1024), BF), ((1024, 1024), BF), ((64, 256), BF), ((32, 256, 256), BF), ((64, 256), F32), ((64, 256), F32),
             ((256, 128), F32), ((256, 128), F32))],
         10 ** 8, 12 * 10 ** 6,
         [pltpu.VMEM((16, 64), jnp.int32), pltpu.VMEM((16, 128), jnp.int32), pltpu.VMEM((32, 16, 256), BF), dma((7,))],
     )(in_hbm(columns.T), in_hbm(owners), in_hbm(interpolation), got, in_hbm(innovation), in_hbm(obs_weight), part)
-    onehot, place, interp, innov, weight, innov_own, live_own = [in_vmem(a) for a in kept]
+    onehot, onehot_t, place, interp, innov, weight, innov_own, live_own = [in_vmem(a) for a in kept]
 
     (inc_my,) = call(
         add_body, [VM, VM, ANY], [(shape((8, 1024), BF), VM)], 10 ** 4, 10 ** 5
     )(part, over(part, 2), place)
     inc_mt = over(inc_my, 1)
     adj_my, adj_mt, slots = call(
-        obs_body, [VM] * 7,
+        obs_body, [VM] * 8 + [HB],
         [(shape((8, 1024), F32), VM)] * 2 + [(pltpu.VMEM((256, 128), F32), VM)],
         10 ** 9, 12 * 10 ** 6,
-        [pltpu.VMEM((64, 256), BF), pltpu.VMEM((64, 256), BF), pltpu.VMEM((64, 256), F32)],
-    )(inc_my, inc_mt, onehot, place, innov, weight, interp)
+        [pltpu.VMEM((64, 256), BF), pltpu.VMEM((64, 256), BF), pltpu.VMEM((64, 256), F32),
+         pltpu.VMEM((32, 256, 256), BF), dma((8,))],
+    )(inc_my, inc_mt, onehot, onehot_t, place, innov, weight, interp, in_hbm(interpolation))
 
     g_mt, g_my = call(
         gradient_body, [VM] * 8, [(shape((32, 56), F32), VM)] * 2, 5 * 10 ** 8, 2 * 10 ** 6

time: 64.2 us -> 63.3 us (0.986)
  blocking collectives: 18.4 us -> 23.1 us
  waiting for transfers between devices: 12 us -> 9.73 us
  starting transfers between devices: 16.5 us -> 14.8 us
  Pallas kernels: 16.2 us -> 14.6 us
    all_to_all x1, waiting for transfers between devices: 8.76 us -> 2.89 us  [per_device(): lax.all_to_all(payload, 'mem', split_axis=0, concat_axis=0, tiled=True)]
    all_to_all x1, blocking collectives: 18.4 us -> 23.1 us  [per_device(): lax.all_to_all(sent, ('band', 'mem'), split_axis=0, concat_axis=0, axis_i...]
    ppermute x8, waiting for transfers between devices: 3.25 us -> 6.84 us  [over(): return lax.ppermute(x, 'band', [(i, i ^ bit) for i in range(4)])]
    ppermute x8, starting transfers between devices: 8.76 us -> 7.01 us  [over(): return lax.ppermute(x, 'band', [(i, i ^ bit) for i in range(4)])]
    pallas_call x1, Pallas kernels: 3.72 us -> 2.48 us  [per_device(): call(prep_body, [HB] * 3 + [ANY] + [HB] * 2 + [ANY], [(pltpu.VMEM(d, t),...]
  transfers between devices with their start and end apart: 9 -> 9, of which waited for: 4 -> 5; matrix products, arithmetic and copies ran while one was open for 0% -> 0% of each run, Pallas kernels for 8% -> 7%
where the time goes in v5:
time: 63.3 us; the launch traced here: 63 us
  blocking collectives  23.1 us (36%)
  starting transfers between devices  14.8 us (23%)
  Pallas kernels  14.6 us (23%)
  waiting for transfers between devices  9.73 us (15%)
  between operations  0.75 us (1%)
    all_to_all x1, blocking collectives, per_device(): lax.all_to_all(sent, ('band', 'mem'), split_axis=0, concat_axis=0, axis_i...  23.1 us
    all_to_all x1, starting transfers between devices, per_device(): lax.all_to_all(payload, 'mem', split_axis=0, concat_axis=0, tiled=True)  7.79 us
    ppermute x8, starting transfers between devices, over(): return lax.ppermute(x, 'band', [(i, i ^ bit) for i in range(4)])  7.01 us
    ppermute x8, waiting for transfers between devices, over(): return lax.ppermute(x, 'band', [(i, i ^ bit) for i in range(4)])  6.84 us
    pallas_call x1, Pallas kernels, per_device(): call(obs_body, [VM] * 8 + [HB], [(shape((8, 1024), F32), VM)] * 2 + [(plt...  5.54 us
    all_to_all x1, waiting for transfers between devices, per_device(): lax.all_to_all(payload, 'mem', split_axis=0, concat_axis=0, tiled=True)  2.89 us
    pallas_call x1, Pallas kernels, per_device(): call(prep_body, [HB] * 3 + [ANY] + [HB] * 2 + [ANY], [(pltpu.VMEM(d, t),...  2.48 us
    pallas_call x1, Pallas kernels, per_device(): call(load_body, [HB] * 4, [(pltpu.VMEM((16, 8, 1024), BF), VM)] * 2 + [(p...  2.26 us
  transfers between devices with their start and end apart: 9, of which 5 were waited for; matrix products, arithmetic and copies ran while one was open for 0% of the time, Pallas kernels for 7%

profile of v5, /device:TPU:0, one launch (start us, length us, event | category | flops | bytes accessed | tf_op | source)
XLA Modules:
  0.0 63.0 jit_solution(2707949346278102343)
XLA Ops:
  0.6 2.3 %shard_map.95 = (bf16[16,8,1024]{2,1,0:T(8,128)(2,1)S(1)}, bf16[16,8,1024]{2,1,0:T(8,128)(2,1)S(1)}, bf16[28,8,1024]{2,1,0:T(8,128)(2,1)S(1)}, bf16[28,8,1024]{2,1,0:T(8,128)(2,1)S(1)}, bf16[32,16,256]{2,1,0:T(8,128)(2,1)}) custom-call(bf16[16,16,1024]{2,1,0:T(8,128)(2,1)} %mem.1, bf16[28,16,1024]{2,1,0:T(8,128)(2,1)} %eig.1, f32[1,256,512]{2,1,0:T(8,128)} %innovation.3, ...), custom_call_target="tpu_custom_call" | custom-call | flops 1000000 | bytes 5000000 | tf_op jit(solution)/shard_map/pallas_call | solution.py:299
  2.9 0.1 collective-permute-start.1
  3.0 0.5 collective-permute-start
  3.5 4.0 %collective-permute-start.2 = (bf16[128,1024]{1,0:T(8,128)(2,1)S(1)}, bf16[128,1024]{1,0:T(8,128)(2,1)S(1)}, u32[]{:S(2)}, u32[]{:S(2)}) collective-permute-start(bf16[128,1024]{1,0:T(8,128)(2,1)S(1)} %bitcast.11), channel_id=1, source_target_pairs={{0,64},{32,96},{64,0},{96,32},{1,65},{33,97},{65,1},{97,33},{2,66}... | collective-permute-start | bytes 786440 | tf_op jit(solution)/shard_map/ppermute | solution.py:296
  7.5 0.0 collective-permute-start.3
  7.5 7.8 %all-to-all-start = ((bf16[32,16,256]{2,1,0:T(8,128)(2,1)}), bf16[32,16,256]{2,1,0:T(8,128)(2,1)S(1)}, u32[]{:S(2)}, u32[]{:S(2)}) async-start(bf16[32,16,256]{2,1,0:T(8,128)(2,1)} %get-tuple-element.30), calls=%async_computation | async-start | bytes 524288 | tf_op jit(solution)/shard_map/all_to_all | solution.py:311
  15.3 0.0 collective-permute-done.refs_2_.m1
  15.3 1.4 %shard_map.96 = (f32[8,1024]{1,0:T(8,128)S(1)}, bf16[448,256]{1,0:T(8,128)(2,1)S(1)}) custom-call(f32[64,112]{1,0:T(8,128)} %bitcast.14, bf16[128,1024]{1,0:T(8,128)(2,1)S(1)} %bitcast.12, bf16[128,1024]{1,0:T(8,128)(2,1)S(1)} %collective-permute-done.refs_2_.m1, bf16[224,1024]{1,0:T(8,128)(2,1)S(1)} %bitcast.8, ...), custom_call_target="tpu_custom_call" | custom-call | flops 250000000 | bytes 2000000 | tf_op jit(solution)/shard_map/pallas_call | solution.py:315
  16.7 3.6 %collective-permute-done.3.refs_3_.refs_6_.m3 = bf16[128,1024]{1,0:T(8,128)(2,1)S(1)} collective-permute-done((bf16[128,1024]{1,0:T(8,128)(2,1)S(1)}, bf16[128,1024]{1,0:T(8,128)(2,1)S(1)}, u32[]{:S(2)}, u32[]{:S(2)}) %collective-permute-start.3) | collective-permute-done | bytes 262176 | tf_op jit(solution)/shard_map/ppermute | solution.py:296
  20.3 0.4 shard_map.97._.a
  20.7 1.9 %collective-permute-start.4 = (f32[8,1024]{1,0:T(8,128)S(1)}, f32[8,1024]{1,0:T(8,128)S(1)}, u32[]{:S(2)}, u32[]{:S(2)}) collective-permute-start(f32[8,1024]{1,0:T(8,128)S(1)} %shard_map.97._.a), channel_id=1, source_target_pairs={{0,64},{32,96},{64,0},{96,32},{1,65},{33,97},{65,1},{97,33},{2,66}... | collective-permute-start | bytes 98312 | tf_op jit(solution)/shard_map/ppermute | solution.py:296
  22.7 2.9 %all-to-all-done.got_in = bf16[32,16,256]{2,1,0:T(8,128)(2,1)S(1)} async-done(((bf16[32,16,256]{2,1,0:T(8,128)(2,1)}), bf16[32,16,256]{2,1,0:T(8,128)(2,1)S(1)}, u32[]{:S(2)}, u32[]{:S(2)}) %all-to-all-start) | async-done | bytes 262176 | tf_op jit(solution)/shard_map/all_to_all | solution.py:311
  25.6 2.5 %shard_map.98 = (bf16[1024,1024]{1,0:T(8,128)(2,1)S(1)}, bf16[1024,1024]{1,0:T(8,128)(2,1)S(1)}, bf16[64,256]{1,0:T(8,128)(2,1)S(1)}, bf16[32,256,256]{2,1,0:T(8...) custom-call(s32[16,64]{1,0:T(8,128)} %bitcast.19, ...), custom_call_target="tpu_custom_call" | custom-call | flops 100000000 | bytes 12000000 | tf_op jit(solution)/shard_map/pallas_call | solution.py:325
  28.1 0.1 collective-permute-start.5
  28.2 1.2 %collective-permute-done.5.inc_mt = bf16[8,1024]{1,0:T(8,128)(2,1)S(1)} collective-permute-done((bf16[8,1024]{1,0:T(8,128)(2,1)S(1)}, bf16[8,1024]{1,0:T(8,128)(2,1)S(1)}, u32[]{:S(2)}, u32[]{:S(2)}) %collective-permute-start.5) | collective-permute-done | bytes 16416 | tf_op jit(solution)/shard_map/ppermute | solution.py:296
  29.4 5.5 %shard_map.100 = (f32[8,1024]{1,0:T(8,128)S(1)}, f32[8,1024]{1,0:T(8,128)S(1)}, f32[256,128]{1,0:T(8,128)S(1)}) custom-call(bf16[8,1024]{1,0:T(8,128)(2,1)S(1)} %shard_map.99.inc_my, bf16[8,1024]{1,0:T(8,128)(2,1)S(1)} %collective-permute-done.5.inc_mt, bf16[1024,1024]{1,0:T(8,128)(2,1)S(1)} %get-tuple-element.32.onehot, ...), custom_call_target="tpu_custom_call" | custom-call | flops 1000000000 | bytes 12000000 | tf_op jit(solution)/shard_map/pallas_call | solution.py:340
  34.9 0.2 collective-permute-start.6
  35.2 1.0 %collective-permute-done.6.a1 = f32[8,1024]{1,0:T(8,128)S(1)} collective-permute-done((f32[8,1024]{1,0:T(8,128)S(1)}, f32[8,1024]{1,0:T(8,128)S(1)}, u32[]{:S(2)}, u32[]{:S(2)}) %collective-permute-start.6) | collective-permute-done | bytes 32800 | tf_op jit(solution)/shard_map/ppermute | solution.py:296
  36.2 1.6 %shard_map.101 = (f32[32,56]{1,0:T(8,128)S(1)}, f32[32,56]{1,0:T(8,128)S(1)}) custom-call(f32[8,1024]{1,0:T(8,128)S(1)} %get-tuple-element.37.a0, f32[8,1024]{1,0:T(8,128)S(1)} %collective-permute-done.6.a1, bf16[128,1024]{1,0:T(8,128)(2,1)S(1)} %bitcast.13, bf16[128,1024]{1,0:T(8,128)(2,1)S(1)} %collective-permute-done.refs_2_.m1, ...), custom_call_target="tpu_custom_call" | custom-call | flops 500000000 | bytes 2000000 | tf_op jit(solution)/shard_map/pallas_call | solution.py:348
  37.8 0.2 collective-permute-start.7
  38.0 1.0 %collective-permute-done.7.came = f32[32,56]{1,0:T(8,128)S(1)} collective-permute-done((f32[32,56]{1,0:T(8,128)S(1)}, f32[32,56]{1,0:T(8,128)S(1)}, u32[]{:S(2)}, u32[]{:S(2)}) %collective-permute-start.7) | collective-permute-done | bytes 7200 | tf_op jit(solution)/shard_map/ppermute | solution.py:296
  39.0 0.1 shard_map.102
  39.1 23.1 %all_to_all.10.refs_0_ = f32[64,16,128]{2,1,0:T(8,128)S(1)} all-to-all(f32[64,16,128]{2,1,0:T(8,128)S(1)} %shard_map.102), channel_id=1, replica_groups={{0,1,2,3,4,5,6,7,8,9,10,11,12,13,14,15,16,17,18,19,20,21,22,23,24,25,26..., dimensions={0} | all-to-all | bytes 1048576 | tf_op jit(solution)/shard_map/all_to_all | solution.py:356
  62.2 0.7 %shard_map.103 = (f32[16,112]{1,0:T(8,128)}, f32[1,256,128]{2,1,0:T(8,128)}) custom-call(f32[64,16,128]{2,1,0:T(8,128)S(1)} %all_to_all.10.refs_0_, f32[64,112]{1,0:T(8,128)S(1)} %bitcast.15, f32[256,128]{1,0:T(8,128)S(1)} %get-tuple-element.42.refs_2_, f32[256,128]{1,0:T(8,128)S(1)} %get-tuple-element.43.refs_3_), custom_call_target="tpu_custom_call" | custom-call | flops 1000000 | bytes 600000 | tf_op jit(solution)/shard_map/pallas_call | solution.py:358
  (6 shorter events, 0.0 us)
Async XLA Ops:
  2.9 12.4 %collective-permute-start.1 = (bf16[224,1024]{1,0:T(8,128)(2,1)S(1)}, bf16[224,1024]{1,0:T(8,128)(2,1)S(1)}, u32[]{:S(2)}, u32[]{:S(2)}) collective-permute-start(bf16[224,1024]{1,0:T(8,128)(2,1)S(1)} %bitcast.16), channel_id=1, source_target_pairs={{0,32},{32,0},{64,96},{96,64},{1,33},{33,1},{65,97},{97,65},{2,34}... | collective-permute-start | bytes 1376264 | tf_op jit(solution)/shard_map/ppermute | solution.py:296
  3.0 12.3 %collective-permute-start = (bf16[128,1024]{1,0:T(8,128)(2,1)S(1)}, bf16[128,1024]{1,0:T(8,128)(2,1)S(1)}, u32[]{:S(2)}, u32[]{:S(2)}) collective-permute-start(bf16[128,1024]{1,0:T(8,128)(2,1)S(1)} %bitcast.17), channel_id=1, source_target_pairs={{0,32},{32,0},{64,96},{96,64},{1,33},{33,1},{65,97},{97,65},{2,34}... | collective-permute-start | bytes 786440 | tf_op jit(solution)/shard_map/ppermute | solution.py:296
  3.5 13.2 %collective-permute-start.2 = (bf16[128,1024]{1,0:T(8,128)(2,1)S(1)}, bf16[128,1024]{1,0:T(8,128)(2,1)S(1)}, u32[]{:S(2)}, u32[]{:S(2)}) collective-permute-start(bf16[128,1024]{1,0:T(8,128)(2,1)S(1)} %bitcast.11), channel_id=1, source_target_pairs={{0,64},{32,96},{64,0},{96,32},{1,65},{33,97},{65,1},{97,33},{2,66}... | collective-permute-start | bytes 786440 | tf_op jit(solution)/shard_map/ppermute | solution.py:296
  7.5 12.9 %collective-permute-start.3 = (bf16[128,1024]{1,0:T(8,128)(2,1)S(1)}, bf16[128,1024]{1,0:T(8,128)(2,1)S(1)}, u32[]{:S(2)}, u32[]{:S(2)}) collective-permute-start(bf16[128,1024]{1,0:T(8,128)(2,1)S(1)} %bitcast.18), channel_id=1, source_target_pairs={{0,96},{32,64},{64,32},{96,0},{1,97},{33,65},{65,33},{97,1},{2,98}... | collective-permute-start | bytes 786440 | tf_op jit(solution)/shard_map/ppermute | solution.py:296
  7.5 18.1 %all-to-all-start = ((bf16[32,16,256]{2,1,0:T(8,128)(2,1)}), bf16[32,16,256]{2,1,0:T(8,128)(2,1)S(1)}, u32[]{:S(2)}, u32[]{:S(2)}) async-start(bf16[32,16,256]{2,1,0:T(8,128)(2,1)} %get-tuple-element.30), calls=%async_computation | async-start | bytes 524288 | tf_op jit(solution)/shard_map/all_to_all | solution.py:311
  20.7 7.3 %collective-permute-start.4 = (f32[8,1024]{1,0:T(8,128)S(1)}, f32[8,1024]{1,0:T(8,128)S(1)}, u32[]{:S(2)}, u32[]{:S(2)}) collective-permute-start(f32[8,1024]{1,0:T(8,128)S(1)} %shard_map.97._.a), channel_id=1, source_target_pairs={{0,64},{32,96},{64,0},{96,32},{1,65},{33,97},{65,1},{97,33},{2,66}... | collective-permute-start | bytes 98312 | tf_op jit(solution)/shard_map/ppermute | solution.py:296
  28.1 1.3 %collective-permute-start.5 = (bf16[8,1024]{1,0:T(8,128)(2,1)S(1)}, bf16[8,1024]{1,0:T(8,128)(2,1)S(1)}, u32[]{:S(2)}, u32[]{:S(2)}) collective-permute-start(bf16[8,1024]{1,0:T(8,128)(2,1)S(1)} %shard_map.99.inc_my), channel_id=1, source_target_pairs={{0,32},{32,0},{64,96},{96,64},{1,33},{33,1},{65,97},{97,65},{2,34}... | collective-permute-start | bytes 49160 | tf_op jit(solution)/shard_map/ppermute | solution.py:296
  29.4 32.9 %copy-start = (f32[112,64]{0,1:T(8,128)S(1)}, f32[112,64]{0,1:T(8,128)}, u32[]{:S(2)}) copy-start(f32[112,64]{0,1:T(8,128)} %param.10) | copy-start | bytes 86020
  34.9 1.3 %collective-permute-start.6 = (f32[8,1024]{1,0:T(8,128)S(1)}, f32[8,1024]{1,0:T(8,128)S(1)}, u32[]{:S(2)}, u32[]{:S(2)}) collective-permute-start(f32[8,1024]{1,0:T(8,128)S(1)} %get-tuple-element.38), channel_id=1, source_target_pairs={{0,32},{32,0},{64,96},{96,64},{1,33},{33,1},{65,97},{97,65},{2,34}... | collective-permute-start | bytes 98312 | tf_op jit(solution)/shard_map/ppermute | solution.py:296
  37.8 1.2 %collective-permute-start.7 = (f32[32,56]{1,0:T(8,128)S(1)}, f32[32,56]{1,0:T(8,128)S(1)}, u32[]{:S(2)}, u32[]{:S(2)}) collective-permute-start(f32[32,56]{1,0:T(8,128)S(1)} %get-tuple-element.40), channel_id=1, source_target_pairs={{0,32},{32,0},{64,96},{96,64},{1,33},{33,1},{65,97},{97,65},{2,34}... | collective-permute-start | bytes 21512 | tf_op jit(solution)/shard_map/ppermute | solution.py:296

commit v6 on v5

--- a/solution.py
+++ b/solution.py
@@ -137,7 +137,7 @@
 
 
 def prep_body(columns_t, owners_in, interpolation, got_in, innovation, obs_weight, _,
-              onehot, onehot_t, place, interp, innov, weight, innov_own, live_own,
+              onehot, onehot_t, place_hi, place_lo, interp, innov, weight, innov_own, live_own,
               cols_s, own_s, got, sem):
     band = lax.axis_index("band")
     tile = lax.axis_index("mem")
@@ -162,7 +162,10 @@
     rank = jnp.sum(jnp.where((own_row == own_col) & earlier, 1.0, 0.0), axis=1, keepdims=True)
     target = (own_col[:, :1] * 8.0 + rank).astype(jnp.int32)
     sel = ones_where(target == iota((64, 256), 1))
-    place[...] = sel
+    slot = iota((64, 256), 1)
+    half = 4 * (band >> 1)
+    place_hi[...] = ones_where((target == slot + half) & ((slot & 7) < 4))
+    place_lo[...] = ones_where((target == slot + half - 4) & ((slot & 7) >= 4))
     x = got[...].astype(F32)
     innov[...] = dot(sel, x[:, :8].reshape(256, 256).astype(BF))
     weight[...] = dot(sel, x[:, 8:].reshape(256, 256).astype(BF))
@@ -181,8 +184,8 @@
     out[...] = (a[...] + b[...]).astype(BF)
 
 
-def obs_body(inc_my, inc_mt, onehot, onehot_t, place, innov, weight, near, interpolation,
-             adj_my, adj_mt, slots, picked, depb, spread, far, sem):
+def obs_body(inc_my, inc_mt, onehot, onehot_t, innov, weight, near, interpolation,
+             adj_my, adj_mt, image_out, picked, depb, spread, far, sem):
     fetch = [
         start_all([
             pltpu.make_async_copy(
@@ -218,6 +221,7 @@
             acc = jnp.where(rows == i, dot(lhs, block(j)), acc)
         image.append(acc)
     image = jnp.concatenate(image, axis=0)
+    image_out[...] = image
     depb[...] = (weight[...] * (innov[...] - image)).astype(BF)
     for b in range(4):
         lhs = depb[b * 16:(b + 1) * 16, :]
@@ -236,9 +240,11 @@
     adj = both[:16] + both[16:]
     adj_my[...] = jnp.where(first, adj[:8], adj[8:])
     adj_mt[...] = jnp.where(first, adj[8:], adj[:8])
-    sel = place[...]
-    hi, mid, lo = parts3(jnp.where((band >> 1) == 0, image[:, :128], image[:, 128:]))
-    slots[...] = dot(sel, hi, TN) + dot(sel, mid, TN) + dot(sel, lo, TN)
+
+
+def slots_body(place_hi, place_lo, image, out):
+    hi, lo, _ = parts3(image[...])
+    out[...] = dot(place_hi[...], hi, TN) + dot(place_lo[...], lo, TN)
 
 
 def gradient_body(a0, a1, m0, m1, m2, m3, e0, e1, mate, mine):
@@ -265,20 +271,23 @@
         jnp.concatenate([total[r:r + 8], gap, total[r + 8:r + 16], gap], axis=1) for r in (0, 16)
     ]
     high = (lax.axis_index("band") >> 1) == 1
-    image = slots[...].reshape(32, 8, 128)
     for side in range(2):
         here = high if side else jnp.logical_not(high)
-        rows = slice(side * 32, side * 32 + 32)
-        out[rows, :8, :] = image
-        out[rows, 8:, :] = jnp.broadcast_to(jnp.where(here, flat[0], flat[1])[None], (32, 8, 128))
+        term = jnp.broadcast_to(jnp.where(here, flat[0], flat[1])[None], (32, 8, 128))
+        image = slots[:, side * 128:(side + 1) * 128].reshape(32, 8, 128)
+        out[side * 32:(side + 1) * 32] = jnp.concatenate([term, image], axis=1).astype(BF)
 
 
 def final_body(scale, got, control_t, innov, live, gradient_t, departures):
     band = lax.axis_index("band")
-    image = got[pl.ds((band >> 1) * 32, 32), :8, :].reshape(256, 128)
+    sums, halves = [], []
+    for side in range(2):
+        x = got[side * 32:(side + 1) * 32].astype(F32)
+        sums.append(jnp.sum(x[:, :8], axis=0))
+        halves.append(x[:, 8:12] + x[:, 12:])
+    image = jnp.concatenate(halves, axis=1).reshape(256, 128)
     departures[...] = (live[...] * (innov[...] - image)).reshape(1, 256, 128)
-    low = jnp.sum(got[:32, 8:, :], axis=0)
-    top = jnp.sum(got[32:, 8:, :], axis=0)
+    low, top = sums
     total = jnp.concatenate([
         jnp.concatenate([low[:, :56], top[:, :56]], axis=1),
         jnp.concatenate([low[:, 64:120], top[:, 64:120]], axis=1),
@@ -326,31 +335,34 @@
         prep_body,
         [HB] * 3 + [ANY] + [HB] * 2 + [ANY],
         [(pltpu.VMEM(d, t), VM) for d, t in (
-            ((1024, 1024), BF), ((1024, 1024), BF), ((64, 256), BF), ((32, 256, 256), BF), ((64, 256), F32), ((64, 256), F32),
+            ((1024, 1024), BF), ((1024, 1024), BF), ((64, 256), BF), ((64, 256), BF), ((32, 256, 256), BF), ((64, 256), F32), ((64, 256), F32),
             ((256, 128), F32), ((256, 128), F32))],
         10 ** 8, 12 * 10 ** 6,
         [pltpu.VMEM((16, 64), jnp.int32), pltpu.VMEM((16, 128), jnp.int32), pltpu.VMEM((32, 16, 256), BF), dma((7,))],
     )(in_hbm(columns.T), in_hbm(owners), in_hbm(interpolation), got, in_hbm(innovation), in_hbm(obs_weight), part)
-    onehot, onehot_t, place, interp, innov, weight, innov_own, live_own = [in_vmem(a) for a in kept]
+    onehot, onehot_t, place_hi, place_lo, interp, innov, weight, innov_own, live_own = [in_vmem(a) for a in kept]
 
     (inc_my,) = call(
         add_body, [VM, VM, ANY], [(shape((8, 1024), BF), VM)], 10 ** 4, 10 ** 5
-    )(part, over(part, 2), place)
+    )(part, over(part, 2), place_hi)
     inc_mt = over(inc_my, 1)
-    adj_my, adj_mt, slots = call(
-        obs_body, [VM] * 8 + [HB],
-        [(shape((8, 1024), F32), VM)] * 2 + [(pltpu.VMEM((256, 128), F32), VM)],
+    adj_my, adj_mt, image = call(
+        obs_body, [VM] * 7 + [HB],
+        [(shape((8, 1024), F32), VM)] * 2 + [(pltpu.VMEM((64, 256), F32), VM)],
         10 ** 9, 12 * 10 ** 6,
         [pltpu.VMEM((64, 256), BF), pltpu.VMEM((64, 256), BF), pltpu.VMEM((64, 256), F32),
          pltpu.VMEM((32, 256, 256), BF), dma((8,))],
-    )(inc_my, inc_mt, onehot, onehot_t, place, innov, weight, interp, in_hbm(interpolation))
-
+    )(inc_my, inc_mt, onehot, onehot_t, innov, weight, interp, in_hbm(interpolation))
+
+    (slots,) = call(
+        slots_body, [VM] * 3, [(pltpu.VMEM((256, 256), F32), VM)], 10 ** 7, 5 * 10 ** 5
+    )(place_hi, place_lo, in_vmem(image))
     g_mt, g_my = call(
         gradient_body, [VM] * 8, [(shape((32, 56), F32), VM)] * 2, 5 * 10 ** 8, 2 * 10 ** 6
     )(adj_my, over(adj_mt, 1), m_my, m1, m2, m3, e0, e1)
 
     (sent,) = call(
-        pack_body, [VM] * 3, [(shape((64, 16, 128), F32), VM)], 10 ** 5, 6 * 10 ** 5
+        pack_body, [VM] * 3, [(shape((64, 16, 128), BF), VM)], 10 ** 5, 6 * 10 ** 5
     )(g_my, over(g_mt, 1), in_vmem(slots))
     groups = [[(2 * z + core) * 32 + t for z in range(2) for t in range(32)] for core in range(2)]
     arrived = lax.all_to_all(

time: 63.3 us -> 60.7 us (0.959)
  blocking collectives: 23.1 us -> 20.6 us
    all_to_all x1, blocking collectives: 23.1 us -> 20.6 us  [per_device(): lax.all_to_all(sent, ('band', 'mem'), split_axis=0, concat_axis=0, axis_i...]
    pallas_call x2 -> x3, Pallas kernels: 5.63 us -> 5.82 us  [the longest x1 5.47 us: per_device(): call(obs_body, [VM] * 7 + [HB], [(shape((8, 1024), F32), VM)] * 2 + [(plt...]
  transfers between devices with their start and end apart: 9 -> 9, of which waited for: 5 -> 5; matrix products, arithmetic and copies ran while one was open for 0% -> 0% of each run, Pallas kernels for 7% -> 8%
where the time goes in v6:
time: 60.7 us; the launch traced here: 60.4 us
  blocking collectives  20.6 us (34%)
  Pallas kernels  14.8 us (24%)
  starting transfers between devices  14.8 us (24%)
  waiting for transfers between devices  9.47 us (16%)
  between operations  0.75 us (1%)
    all_to_all x1, blocking collectives, per_device(): lax.all_to_all(sent, ('band', 'mem'), split_axis=0, concat_axis=0, axis_i...  20.6 us
    all_to_all x1, starting transfers between devices, per_device(): lax.all_to_all(payload, 'mem', split_axis=0, concat_axis=0, tiled=True)  7.79 us
    ppermute x8, starting transfers between devices, over(): return lax.ppermute(x, 'band', [(i, i ^ bit) for i in range(4)])  7.01 us
    ppermute x8, waiting for transfers between devices, over(): return lax.ppermute(x, 'band', [(i, i ^ bit) for i in range(4)])  6.58 us
    pallas_call x1, Pallas kernels, per_device(): call(obs_body, [VM] * 7 + [HB], [(shape((8, 1024), F32), VM)] * 2 + [(plt...  5.47 us
    all_to_all x1, waiting for transfers between devices, per_device(): lax.all_to_all(payload, 'mem', split_axis=0, concat_axis=0, tiled=True)  2.89 us
    pallas_call x1, Pallas kernels, per_device(): call(prep_body, [HB] * 3 + [ANY] + [HB] * 2 + [ANY], [(pltpu.VMEM(d, t),...  2.48 us
    pallas_call x1, Pallas kernels, per_device(): call(load_body, [HB] * 4, [(pltpu.VMEM((16, 8, 1024), BF), VM)] * 2 + [(p...  2.26 us
  transfers between devices with their start and end apart: 9, of which 5 were waited for; matrix products, arithmetic and copies ran while one was open for 0% of the time, Pallas kernels for 8%

profile of v6, /device:TPU:0, one launch (start us, length us, event | category | flops | bytes accessed | tf_op | source)
XLA Modules:
  0.0 60.4 jit_solution(4306129284524378534)
XLA Ops:
  0.6 2.3 %shard_map.95 = (bf16[16,8,1024]{2,1,0:T(8,128)(2,1)S(1)}, bf16[16,8,1024]{2,1,0:T(8,128)(2,1)S(1)}, bf16[28,8,1024]{2,1,0:T(8,128)(2,1)S(1)}, bf16[28,8,1024]{2,1,0:T(8,128)(2,1)S(1)}, bf16[32,16,256]{2,1,0:T(8,128)(2,1)}) custom-call(bf16[16,16,1024]{2,1,0:T(8,128)(2,1)} %mem.1, bf16[28,16,1024]{2,1,0:T(8,128)(2,1)} %eig.1, f32[1,256,512]{2,1,0:T(8,128)} %innovation.3, ...), custom_call_target="tpu_custom_call" | custom-call | flops 1000000 | bytes 5000000 | tf_op jit(solution)/shard_map/pallas_call | solution.py:308
  2.9 0.1 collective-permute-start.1
  3.0 0.5 collective-permute-start
  3.5 4.0 %collective-permute-start.2 = (bf16[128,1024]{1,0:T(8,128)(2,1)S(1)}, bf16[128,1024]{1,0:T(8,128)(2,1)S(1)}, u32[]{:S(2)}, u32[]{:S(2)}) collective-permute-start(bf16[128,1024]{1,0:T(8,128)(2,1)S(1)} %bitcast.11), channel_id=1, source_target_pairs={{0,64},{32,96},{64,0},{96,32},{1,65},{33,97},{65,1},{97,33},{2,66}... | collective-permute-start | bytes 786440 | tf_op jit(solution)/shard_map/ppermute | solution.py:305
  7.5 7.8 %all-to-all-start = ((bf16[32,16,256]{2,1,0:T(8,128)(2,1)}), bf16[32,16,256]{2,1,0:T(8,128)(2,1)S(1)}, u32[]{:S(2)}, u32[]{:S(2)}) async-start(bf16[32,16,256]{2,1,0:T(8,128)(2,1)} %get-tuple-element.31), calls=%async_computation | async-start | bytes 524288 | tf_op jit(solution)/shard_map/all_to_all | solution.py:320
  15.3 0.0 collective-permute-done.1.refs_4_.refs_5_.e1
  15.3 1.4 %shard_map.96 = (f32[8,1024]{1,0:T(8,128)S(1)}, bf16[448,256]{1,0:T(8,128)(2,1)S(1)}) custom-call(f32[64,112]{1,0:T(8,128)} %bitcast.14, bf16[128,1024]{1,0:T(8,128)(2,1)S(1)} %bitcast.12, bf16[128,1024]{1,0:T(8,128)(2,1)S(1)} %collective-permute-done.refs_2_.m1, bf16[224,1024]{1,0:T(8,128)(2,1)S(1)} %bitcast.8, ...), custom_call_target="tpu_custom_call" | custom-call | flops 250000000 | bytes 2000000 | tf_op jit(solution)/shard_map/pallas_call | solution.py:324
  16.7 3.6 %collective-permute-done.3.refs_3_.refs_6_.m3 = bf16[128,1024]{1,0:T(8,128)(2,1)S(1)} collective-permute-done((bf16[128,1024]{1,0:T(8,128)(2,1)S(1)}, bf16[128,1024]{1,0:T(8,128)(2,1)S(1)}, u32[]{:S(2)}, u32[]{:S(2)}) %collective-permute-start.3) | collective-permute-done | bytes 262176 | tf_op jit(solution)/shard_map/ppermute | solution.py:305
  20.3 0.4 shard_map.97._.a
  20.7 1.9 %collective-permute-start.4 = (f32[8,1024]{1,0:T(8,128)S(1)}, f32[8,1024]{1,0:T(8,128)S(1)}, u32[]{:S(2)}, u32[]{:S(2)}) collective-permute-start(f32[8,1024]{1,0:T(8,128)S(1)} %shard_map.97._.a), channel_id=1, source_target_pairs={{0,64},{32,96},{64,0},{96,32},{1,65},{33,97},{65,1},{97,33},{2,66}... | collective-permute-start | bytes 98312 | tf_op jit(solution)/shard_map/ppermute | solution.py:305
  22.7 2.9 %all-to-all-done.got_in = bf16[32,16,256]{2,1,0:T(8,128)(2,1)S(1)} async-done(((bf16[32,16,256]{2,1,0:T(8,128)(2,1)}), bf16[32,16,256]{2,1,0:T(8,128)(2,1)S(1)}, u32[]{:S(2)}, u32[]{:S(2)}) %all-to-all-start) | async-done | bytes 262176 | tf_op jit(solution)/shard_map/all_to_all | solution.py:320
  25.6 2.5 %shard_map.98 = (bf16[1024,1024]{1,0:T(8,128)(2,1)S(1)}, bf16[1024,1024]{1,0:T(8,128)(2,1)S(1)}, bf16[64,256]{1,0:T(8,128)(2,1)S(1)}, bf16[64,256]{1,0:T(8,128)(...) custom-call(s32[16,64]{1,0:T(8,128)} %bitcast.19, ...), custom_call_target="tpu_custom_call" | custom-call | flops 100000000 | bytes 12000000 | tf_op jit(solution)/shard_map/pallas_call | solution.py:334
  28.1 0.1 collective-permute-start.5
  28.2 1.2 %collective-permute-done.5.inc_mt = bf16[8,1024]{1,0:T(8,128)(2,1)S(1)} collective-permute-done((bf16[8,1024]{1,0:T(8,128)(2,1)S(1)}, bf16[8,1024]{1,0:T(8,128)(2,1)S(1)}, u32[]{:S(2)}, u32[]{:S(2)}) %collective-permute-start.5) | collective-permute-done | bytes 16416 | tf_op jit(solution)/shard_map/ppermute | solution.py:305
  29.4 5.5 %shard_map.100 = (f32[8,1024]{1,0:T(8,128)S(1)}, f32[8,1024]{1,0:T(8,128)S(1)}, f32[64,256]{1,0:T(8,128)S(1)}) custom-call(bf16[8,1024]{1,0:T(8,128)(2,1)S(1)} %shard_map.99.inc_my, bf16[8,1024]{1,0:T(8,128)(2,1)S(1)} %collective-permute-done.5.inc_mt, bf16[1024,1024]{1,0:T(8,128)(2,1)S(1)} %get-tuple-element.33.onehot, ...), custom_call_target="tpu_custom_call" | custom-call | flops 1000000000 | bytes 12000000 | tf_op jit(solution)/shard_map/pallas_call | solution.py:349
  34.8 0.2 collective-permute-start.6
  35.1 1.0 %collective-permute-done.6.a1 = f32[8,1024]{1,0:T(8,128)S(1)} collective-permute-done((f32[8,1024]{1,0:T(8,128)S(1)}, f32[8,1024]{1,0:T(8,128)S(1)}, u32[]{:S(2)}, u32[]{:S(2)}) %collective-permute-start.6) | collective-permute-done | bytes 32800 | tf_op jit(solution)/shard_map/ppermute | solution.py:305
  36.1 1.6 %shard_map.101 = (f32[32,56]{1,0:T(8,128)S(1)}, f32[32,56]{1,0:T(8,128)S(1)}) custom-call(f32[8,1024]{1,0:T(8,128)S(1)} %get-tuple-element.38.a0, f32[8,1024]{1,0:T(8,128)S(1)} %collective-permute-done.6.a1, bf16[128,1024]{1,0:T(8,128)(2,1)S(1)} %bitcast.13, bf16[128,1024]{1,0:T(8,128)(2,1)S(1)} %collective-permute-done.refs_2_.m1, ...), custom_call_target="tpu_custom_call" | custom-call | flops 500000000 | bytes 2000000 | tf_op jit(solution)/shard_map/pallas_call | solution.py:360
  37.7 0.2 collective-permute-start.7
  37.9 0.2 shard_map.102.slots
  38.2 0.8 %collective-permute-done.7.came = f32[32,56]{1,0:T(8,128)S(1)} collective-permute-done((f32[32,56]{1,0:T(8,128)S(1)}, f32[32,56]{1,0:T(8,128)S(1)}, u32[]{:S(2)}, u32[]{:S(2)}) %collective-permute-start.7) | collective-permute-done | bytes 7200 | tf_op jit(solution)/shard_map/ppermute | solution.py:305
  38.9 0.1 shard_map.103
  39.0 20.6 %all_to_all.10.refs_0_ = bf16[64,16,128]{2,1,0:T(8,128)(2,1)S(1)} all-to-all(bf16[64,16,128]{2,1,0:T(8,128)(2,1)S(1)} %shard_map.103), channel_id=1, replica_groups={{0,1,2,3,4,5,6,7,8,9,10,11,12,13,14,15,16,17,18,19,20,21,22,23,24,25,26..., dimensions={0} | all-to-all | bytes 524288 | tf_op jit(solution)/shard_map/all_to_all | solution.py:368
  59.6 0.8 %shard_map.104 = (f32[16,112]{1,0:T(8,128)}, f32[1,256,128]{2,1,0:T(8,128)}) custom-call(bf16[64,16,128]{2,1,0:T(8,128)(2,1)S(1)} %all_to_all.10.refs_0_, f32[64,112]{1,0:T(8,128)S(1)} %bitcast.15, f32[256,128]{1,0:T(8,128)S(1)} %get-tuple-element.44.refs_2_, f32[256,128]{1,0:T(8,128)S(1)} %get-tuple-element.45.refs_3_), custom_call_target="tpu_custom_call" | custom-call | flops 1000000 | bytes 600000 | tf_op jit(solution)/shard_map/pallas_call | solution.py:370
  (7 shorter events, 0.0 us)
Async XLA Ops:
  2.9 12.4 %collective-permute-start.1 = (bf16[224,1024]{1,0:T(8,128)(2,1)S(1)}, bf16[224,1024]{1,0:T(8,128)(2,1)S(1)}, u32[]{:S(2)}, u32[]{:S(2)}) collective-permute-start(bf16[224,1024]{1,0:T(8,128)(2,1)S(1)} %bitcast.16), channel_id=1, source_target_pairs={{0,32},{32,0},{64,96},{96,64},{1,33},{33,1},{65,97},{97,65},{2,34}... | collective-permute-start | bytes 1376264 | tf_op jit(solution)/shard_map/ppermute | solution.py:305
  3.0 12.3 %collective-permute-start = (bf16[128,1024]{1,0:T(8,128)(2,1)S(1)}, bf16[128,1024]{1,0:T(8,128)(2,1)S(1)}, u32[]{:S(2)}, u32[]{:S(2)}) collective-permute-start(bf16[128,1024]{1,0:T(8,128)(2,1)S(1)} %bitcast.17), channel_id=1, source_target_pairs={{0,32},{32,0},{64,96},{96,64},{1,33},{33,1},{65,97},{97,65},{2,34}... | collective-permute-start | bytes 786440 | tf_op jit(solution)/shard_map/ppermute | solution.py:305
  3.5 13.2 %collective-permute-start.2 = (bf16[128,1024]{1,0:T(8,128)(2,1)S(1)}, bf16[128,1024]{1,0:T(8,128)(2,1)S(1)}, u32[]{:S(2)}, u32[]{:S(2)}) collective-permute-start(bf16[128,1024]{1,0:T(8,128)(2,1)S(1)} %bitcast.11), channel_id=1, source_target_pairs={{0,64},{32,96},{64,0},{96,32},{1,65},{33,97},{65,1},{97,33},{2,66}... | collective-permute-start | bytes 786440 | tf_op jit(solution)/shard_map/ppermute | solution.py:305
  7.5 12.9 %collective-permute-start.3 = (bf16[128,1024]{1,0:T(8,128)(2,1)S(1)}, bf16[128,1024]{1,0:T(8,128)(2,1)S(1)}, u32[]{:S(2)}, u32[]{:S(2)}) collective-permute-start(bf16[128,1024]{1,0:T(8,128)(2,1)S(1)} %bitcast.18), channel_id=1, source_target_pairs={{0,96},{32,64},{64,32},{96,0},{1,97},{33,65},{65,33},{97,1},{2,98}... | collective-permute-start | bytes 786440 | tf_op jit(solution)/shard_map/ppermute | solution.py:305
  7.5 18.1 %all-to-all-start = ((bf16[32,16,256]{2,1,0:T(8,128)(2,1)}), bf16[32,16,256]{2,1,0:T(8,128)(2,1)S(1)}, u32[]{:S(2)}, u32[]{:S(2)}) async-start(bf16[32,16,256]{2,1,0:T(8,128)(2,1)} %get-tuple-element.31), calls=%async_computation | async-start | bytes 524288 | tf_op jit(solution)/shard_map/all_to_all | solution.py:320
  20.7 7.3 %collective-permute-start.4 = (f32[8,1024]{1,0:T(8,128)S(1)}, f32[8,1024]{1,0:T(8,128)S(1)}, u32[]{:S(2)}, u32[]{:S(2)}) collective-permute-start(f32[8,1024]{1,0:T(8,128)S(1)} %shard_map.97._.a), channel_id=1, source_target_pairs={{0,64},{32,96},{64,0},{96,32},{1,65},{33,97},{65,1},{97,33},{2,66}... | collective-permute-start | bytes 98312 | tf_op jit(solution)/shard_map/ppermute | solution.py:305
  28.1 1.3 %collective-permute-start.5 = (bf16[8,1024]{1,0:T(8,128)(2,1)S(1)}, bf16[8,1024]{1,0:T(8,128)(2,1)S(1)}, u32[]{:S(2)}, u32[]{:S(2)}) collective-permute-start(bf16[8,1024]{1,0:T(8,128)(2,1)S(1)} %shard_map.99.inc_my), channel_id=1, source_target_pairs={{0,32},{32,0},{64,96},{96,64},{1,33},{33,1},{65,97},{97,65},{2,34}... | collective-permute-start | bytes 49160 | tf_op jit(solution)/shard_map/ppermute | solution.py:305
  29.4 30.3 %copy-start = (f32[112,64]{0,1:T(8,128)S(1)}, f32[112,64]{0,1:T(8,128)}, u32[]{:S(2)}) copy-start(f32[112,64]{0,1:T(8,128)} %param.10) | copy-start | bytes 86020
  34.8 1.3 %collective-permute-start.6 = (f32[8,1024]{1,0:T(8,128)S(1)}, f32[8,1024]{1,0:T(8,128)S(1)}, u32[]{:S(2)}, u32[]{:S(2)}) collective-permute-start(f32[8,1024]{1,0:T(8,128)S(1)} %get-tuple-element.39), channel_id=1, source_target_pairs={{0,32},{32,0},{64,96},{96,64},{1,33},{33,1},{65,97},{97,65},{2,34}... | collective-permute-start | bytes 98312 | tf_op jit(solution)/shard_map/ppermute | solution.py:305
  37.7 1.2 %collective-permute-start.7 = (f32[32,56]{1,0:T(8,128)S(1)}, f32[32,56]{1,0:T(8,128)S(1)}, u32[]{:S(2)}, u32[]{:S(2)}) collective-permute-start(f32[32,56]{1,0:T(8,128)S(1)} %get-tuple-element.41), channel_id=1, source_target_pairs={{0,32},{32,0},{64,96},{96,64},{1,33},{33,1},{65,97},{97,65},{2,34}... | collective-permute-start | bytes 21512 | tf_op jit(solution)/shard_map/ppermute | solution.py:305

commit v7 on v6

--- a/solution.py
+++ b/solution.py
@@ -88,18 +88,19 @@
     return pl.ds(pl.multiple_of((core + 2 * side) * 128, 128), 128)
 
 
-def load_body(mem, eig, innovation, obs_weight, m_mine, m_mate, e_mine, e_mate, payload, iv, sem):
-    slices = start_all(halves_copies(mem, m_mine, m_mate, sem, 0))
+def split_body(mem, eig, m_mine, m_mate, e_mine, e_mate, sem):
+    wait_all(start_all(halves_copies(mem, m_mine, m_mate, sem, 0) + halves_copies(eig, e_mine, e_mate, sem, 2)))
+
+
+def load_body(innovation, obs_weight, _, payload, iv, sem):
     copies = start_all([
         pltpu.make_async_copy(
-            a.at[0, :, quarter_at(side)], iv.at[n, :, side * 128:(side + 1) * 128], sem.at[4 + 2 * n + side])
+            a.at[0, :, quarter_at(side)], iv.at[n, :, side * 128:(side + 1) * 128], sem.at[2 * n + side])
         for n, a in enumerate((innovation, obs_weight)) for side in range(2)
     ])
-    slices += start_all(halves_copies(eig, e_mine, e_mate, sem, 2))
-    wait_all(copies)
     for n in range(2):
+        wait_all(copies[2 * n:2 * n + 2])
         payload[:, n * 8:(n + 1) * 8, :] = iv[n].reshape(32, 8, 256).astype(BF)
-    wait_all(slices)
 
 
 def increment_of(scale, kron, ma, mb, ea, eb, cut):
@@ -260,8 +261,8 @@
         full = jnp.where(same, dot(eig, weighted, NT), 0.0)
         own = jnp.sum(full.reshape(56, 8, 256), axis=1)
         own = jnp.where(first, own, jnp.concatenate([own[28:], own[:28]], axis=0))
-        hi, mid, lo = parts3(own)
-        g[...] = dot(sel, hi, NT) + dot(sel, mid, NT) + dot(sel, lo, NT)
+        hi, mid, _ = parts3(own)
+        g[...] = dot(sel, hi, NT) + dot(sel, mid, NT)
 
 
 def pack_body(mine, came, slots, out):
@@ -305,18 +306,18 @@
         return lax.ppermute(x, "band", [(i, i ^ bit) for i in range(4)])
 
     dma = pltpu.SemaphoreType.DMA
-    m_my, m_mt, e_my, e_mt, payload = call(
-        load_body,
-        [HB] * 4,
-        [(pltpu.VMEM((16, 8, 1024), BF), VM)] * 2 + [(pltpu.VMEM((28, 8, 1024), BF), VM)] * 2
-        + [(pltpu.HBM((32, 16, 256), BF), VM)],
-        10 ** 6, 5 * 10 ** 6,
-        [pltpu.VMEM((2, 256, 256), F32), dma((8,))],
-    )(in_hbm(members), in_hbm(eigvecs), in_hbm(innovation), in_hbm(obs_weight))
+    m_my, m_mt, e_my, e_mt = call(
+        split_body, [HB] * 2,
+        [(pltpu.VMEM((16, 8, 1024), BF), VM)] * 2 + [(pltpu.VMEM((28, 8, 1024), BF), VM)] * 2, 0, 0, [dma((4,))],
+    )(in_hbm(members), in_hbm(eigvecs))
     m_my, m_mt, e0, e_mt = [in_vmem(a.reshape(-1, 1024)) for a in (m_my, m_mt, e_my, e_mt)]
     m3 = over(m_mt, 3)
     m2 = over(m_my, 2)
     m1 = over(m_mt, 1)
+    (payload,) = call(
+        load_body, [HB] * 2 + [ANY], [(pltpu.HBM((32, 16, 256), BF), VM)],
+        0, 0, [pltpu.VMEM((2, 256, 256), F32), dma((4,))],
+    )(in_hbm(innovation), in_hbm(obs_weight), m_my)
     got = lax.all_to_all(payload, "mem", split_axis=0, concat_axis=0, tiled=True)
     e1 = over(e_mt, 1)
     m1, m2, m3, e1 = [in_vmem(a) for a in (m1, m2, m3, e1)]

time: 60.7 us -> 59.3 us (0.977)
  blocking collectives: 20.6 us -> 18.3 us
  waiting for transfers between devices: 9.47 us -> 8.19 us
  starting transfers between devices: 14.8 us -> 16 us
  Pallas kernels: 14.8 us -> 15.7 us
    ppermute x8, waiting for transfers between devices: 6.58 us -> 3.49 us  [over(): return lax.ppermute(x, 'band', [(i, i ^ bit) for i in range(4)])]
    all_to_all x1, blocking collectives: 20.6 us -> 18.3 us  [per_device(): lax.all_to_all(sent, ('band', 'mem'), split_axis=0, concat_axis=0, axis_i...]
    all_to_all x1, waiting for transfers between devices: 2.89 us -> 4.71 us  [per_device(): lax.all_to_all(payload, 'mem', split_axis=0, concat_axis=0, tiled=True)]
    ppermute x8, starting transfers between devices: 7.01 us -> 8.19 us  [over(): return lax.ppermute(x, 'band', [(i, i ^ bit) for i in range(4)])]
    pallas_call x1 -> x2, Pallas kernels: 2.26 us -> 3.2 us  [the longest x1 1.84 us: per_device(): call(load_body, [HB] * 2 + [ANY], [(pltpu.HBM((32, 16, 256), BF), VM)], 0...]
  transfers between devices with their start and end apart: 9 -> 9, of which waited for: 5 -> 5; matrix products, arithmetic and copies ran while one was open for 0% -> 0% of each run, Pallas kernels for 8% -> 11%
where the time goes in v7:
time: 59.3 us; the launch traced here: 58.9 us
  blocking collectives  18.3 us (31%)
  starting transfers between devices  16 us (27%)
  Pallas kernels  15.7 us (26%)
  waiting for transfers between devices  8.19 us (14%)
  between operations  0.76 us (1%)
    all_to_all x1, blocking collectives, per_device(): lax.all_to_all(sent, ('band', 'mem'), split_axis=0, concat_axis=0, axis_i...  18.3 us
    ppermute x8, starting transfers between devices, over(): return lax.ppermute(x, 'band', [(i, i ^ bit) for i in range(4)])  8.19 us
    all_to_all x1, starting transfers between devices, per_device(): lax.all_to_all(payload, 'mem', split_axis=0, concat_axis=0, tiled=True)  7.8 us
    pallas_call x1, Pallas kernels, per_device(): call(obs_body, [VM] * 7 + [HB], [(shape((8, 1024), F32), VM)] * 2 + [(plt...  5.48 us
    all_to_all x1, waiting for transfers between devices, per_device(): lax.all_to_all(payload, 'mem', split_axis=0, concat_axis=0, tiled=True)  4.71 us
    ppermute x8, waiting for transfers between devices, over(): return lax.ppermute(x, 'band', [(i, i ^ bit) for i in range(4)])  3.49 us
    pallas_call x1, Pallas kernels, per_device(): call(prep_body, [HB] * 3 + [ANY] + [HB] * 2 + [ANY], [(pltpu.VMEM(d, t),...  2.48 us
    pallas_call x1, Pallas kernels, per_device(): call(load_body, [HB] * 2 + [ANY], [(pltpu.HBM((32, 16, 256), BF), VM)], 0...  1.84 us
  transfers between devices with their start and end apart: 9, of which 5 were waited for; matrix products, arithmetic and copies ran while one was open for 0% of the time, Pallas kernels for 11%

profile of v7, /device:TPU:0, one launch (start us, length us, event | category | flops | bytes accessed | tf_op | source)
XLA Modules:
  0.0 58.9 jit_solution(12506237432462138067)
XLA Ops:
  0.6 1.4 %shard_map.95 = (bf16[16,8,1024]{2,1,0:T(8,128)(2,1)S(1)}, bf16[16,8,1024]{2,1,0:T(8,128)(2,1)S(1)}, bf16[28,8,1024]{2,1,0:T(8,128)(2,1)S(1)}, bf16[28,8,1024]{2,1,0:T(8,128)(2,1)S(1)}) custom-call(bf16[16,16,1024]{2,1,0:T(8,128)(2,1)} %mem.1, bf16[28,16,1024]{2,1,0:T(8,128)(2,1)} %eig.1), custom_call_target="tpu_custom_call" | custom-call | tf_op jit(solution)/shard_map/pallas_call | solution.py:309
  2.0 0.1 collective-permute-start.1
  2.1 0.5 collective-permute-start
  2.6 4.0 %collective-permute-start.2 = (bf16[128,1024]{1,0:T(8,128)(2,1)S(1)}, bf16[128,1024]{1,0:T(8,128)(2,1)S(1)}, u32[]{:S(2)}, u32[]{:S(2)}) collective-permute-start(bf16[128,1024]{1,0:T(8,128)(2,1)S(1)} %bitcast.11), channel_id=1, source_target_pairs={{0,64},{32,96},{64,0},{96,32},{1,65},{33,97},{65,1},{97,33},{2,66}... | collective-permute-start | bytes 786440 | tf_op jit(solution)/shard_map/ppermute | solution.py:306
  6.6 1.8 %shard_map.98 = bf16[32,16,256]{2,1,0:T(8,128)(2,1)} custom-call(f32[1,256,512]{2,1,0:T(8,128)} %innovation.3, f32[1,256,512]{2,1,0:T(8,128)} %obs_weight.3, bf16[128,1024]{1,0:T(8,128)(2,1)S(1)} %bitcast.12), custom_call_target="tpu_custom_call" | custom-call | tf_op jit(solution)/shard_map/pallas_call | solution.py:317
  8.4 7.8 %all-to-all-start = ((bf16[32,16,256]{2,1,0:T(8,128)(2,1)}), bf16[32,16,256]{2,1,0:T(8,128)(2,1)S(1)}, u32[]{:S(2)}, u32[]{:S(2)}) async-start(bf16[32,16,256]{2,1,0:T(8,128)(2,1)} %shard_map.98), calls=%async_computation | async-start | bytes 524288 | tf_op jit(solution)/shard_map/all_to_all | solution.py:321
  16.2 1.4 %shard_map.96 = (f32[8,1024]{1,0:T(8,128)S(1)}, bf16[448,256]{1,0:T(8,128)(2,1)S(1)}) custom-call(f32[64,112]{1,0:T(8,128)} %bitcast.15, bf16[128,1024]{1,0:T(8,128)(2,1)S(1)} %bitcast.13, bf16[128,1024]{1,0:T(8,128)(2,1)S(1)} %collective-permute-done.refs_2_.m1, bf16[224,1024]{1,0:T(8,128)(2,1)S(1)} %bitcast.8, ...), custom_call_target="tpu_custom_call" | custom-call | flops 250000000 | bytes 2000000 | tf_op jit(solution)/shard_map/pallas_call | solution.py:325
  17.7 0.5 collective-permute-done.3.refs_3_.refs_6_.m3
  18.2 0.4 shard_map.97._.a
  18.6 3.1 %collective-permute-start.4 = (f32[8,1024]{1,0:T(8,128)S(1)}, f32[8,1024]{1,0:T(8,128)S(1)}, u32[]{:S(2)}, u32[]{:S(2)}) collective-permute-start(f32[8,1024]{1,0:T(8,128)S(1)} %shard_map.97._.a), channel_id=1, source_target_pairs={{0,64},{32,96},{64,0},{96,32},{1,65},{33,97},{65,1},{97,33},{2,66}... | collective-permute-start | bytes 98312 | tf_op jit(solution)/shard_map/ppermute | solution.py:306
  21.7 4.7 %all-to-all-done.got_in = bf16[32,16,256]{2,1,0:T(8,128)(2,1)S(1)} async-done(((bf16[32,16,256]{2,1,0:T(8,128)(2,1)}), bf16[32,16,256]{2,1,0:T(8,128)(2,1)S(1)}, u32[]{:S(2)}, u32[]{:S(2)}) %all-to-all-start) | async-done | bytes 262176 | tf_op jit(solution)/shard_map/all_to_all | solution.py:321
  26.4 2.5 %shard_map.99 = (bf16[1024,1024]{1,0:T(8,128)(2,1)S(1)}, bf16[1024,1024]{1,0:T(8,128)(2,1)S(1)}, bf16[64,256]{1,0:T(8,128)(2,1)S(1)}, bf16[64,256]{1,0:T(8,128)(...) custom-call(s32[16,64]{1,0:T(8,128)} %bitcast.20, ...), custom_call_target="tpu_custom_call" | custom-call | flops 100000000 | bytes 12000000 | tf_op jit(solution)/shard_map/pallas_call | solution.py:335
  29.0 0.1 collective-permute-start.5
  29.0 1.2 %collective-permute-done.5.inc_mt = bf16[8,1024]{1,0:T(8,128)(2,1)S(1)} collective-permute-done((bf16[8,1024]{1,0:T(8,128)(2,1)S(1)}, bf16[8,1024]{1,0:T(8,128)(2,1)S(1)}, u32[]{:S(2)}, u32[]{:S(2)}) %collective-permute-start.5) | collective-permute-done | bytes 16416 | tf_op jit(solution)/shard_map/ppermute | solution.py:306
  30.2 5.5 %shard_map.101 = (f32[8,1024]{1,0:T(8,128)S(1)}, f32[8,1024]{1,0:T(8,128)S(1)}, f32[64,256]{1,0:T(8,128)S(1)}) custom-call(bf16[8,1024]{1,0:T(8,128)(2,1)S(1)} %shard_map.100.inc_my, bf16[8,1024]{1,0:T(8,128)(2,1)S(1)} %collective-permute-done.5.inc_mt, bf16[1024,1024]{1,0:T(8,128)(2,1)S(1)} %get-tuple-element.31.onehot, ...), custom_call_target="tpu_custom_call" | custom-call | flops 1000000000 | bytes 12000000 | tf_op jit(solution)/shard_map/pallas_call | solution.py:350
  35.7 0.2 collective-permute-start.6
  36.0 1.0 %collective-permute-done.6.a1 = f32[8,1024]{1,0:T(8,128)S(1)} collective-permute-done((f32[8,1024]{1,0:T(8,128)S(1)}, f32[8,1024]{1,0:T(8,128)S(1)}, u32[]{:S(2)}, u32[]{:S(2)}) %collective-permute-start.6) | collective-permute-done | bytes 32800 | tf_op jit(solution)/shard_map/ppermute | solution.py:306
  37.0 1.6 %shard_map.102 = (f32[32,56]{1,0:T(8,128)S(1)}, f32[32,56]{1,0:T(8,128)S(1)}) custom-call(f32[8,1024]{1,0:T(8,128)S(1)} %get-tuple-element.36.a0, f32[8,1024]{1,0:T(8,128)S(1)} %collective-permute-done.6.a1, bf16[128,1024]{1,0:T(8,128)(2,1)S(1)} %bitcast.14, bf16[128,1024]{1,0:T(8,128)(2,1)S(1)} %collective-permute-done.refs_2_.m1, ...), custom_call_target="tpu_custom_call" | custom-call | flops 500000000 | bytes 2000000 | tf_op jit(solution)/shard_map/pallas_call | solution.py:361
  38.5 0.2 collective-permute-start.7
  38.7 0.2 shard_map.103.slots
  39.0 0.8 %collective-permute-done.7.came = f32[32,56]{1,0:T(8,128)S(1)} collective-permute-done((f32[32,56]{1,0:T(8,128)S(1)}, f32[32,56]{1,0:T(8,128)S(1)}, u32[]{:S(2)}, u32[]{:S(2)}) %collective-permute-start.7) | collective-permute-done | bytes 7200 | tf_op jit(solution)/shard_map/ppermute | solution.py:306
  39.8 0.1 shard_map.104
  39.9 18.3 %all_to_all.10.refs_0_ = bf16[64,16,128]{2,1,0:T(8,128)(2,1)S(1)} all-to-all(bf16[64,16,128]{2,1,0:T(8,128)(2,1)S(1)} %shard_map.104), channel_id=1, replica_groups={{0,1,2,3,4,5,6,7,8,9,10,11,12,13,14,15,16,17,18,19,20,21,22,23,24,25,26..., dimensions={0} | all-to-all | bytes 524288 | tf_op jit(solution)/shard_map/all_to_all | solution.py:369
  58.1 0.8 %shard_map.105 = (f32[16,112]{1,0:T(8,128)}, f32[1,256,128]{2,1,0:T(8,128)}) custom-call(bf16[64,16,128]{2,1,0:T(8,128)(2,1)S(1)} %all_to_all.10.refs_0_, f32[64,112]{1,0:T(8,128)S(1)} %bitcast.16, f32[256,128]{1,0:T(8,128)S(1)} %get-tuple-element.42.refs_2_, f32[256,128]{1,0:T(8,128)S(1)} %get-tuple-element.43.refs_3_), custom_call_target="tpu_custom_call" | custom-call | flops 1000000 | bytes 600000 | tf_op jit(solution)/shard_map/pallas_call | solution.py:371
  (8 shorter events, 0.0 us)
Async XLA Ops:
  2.0 14.2 %collective-permute-start.1 = (bf16[224,1024]{1,0:T(8,128)(2,1)S(1)}, bf16[224,1024]{1,0:T(8,128)(2,1)S(1)}, u32[]{:S(2)}, u32[]{:S(2)}) collective-permute-start(bf16[224,1024]{1,0:T(8,128)(2,1)S(1)} %bitcast.17), channel_id=1, source_target_pairs={{0,32},{32,0},{64,96},{96,64},{1,33},{33,1},{65,97},{97,65},{2,34}... | collective-permute-start | bytes 1376264 | tf_op jit(solution)/shard_map/ppermute | solution.py:306
  2.1 14.1 %collective-permute-start = (bf16[128,1024]{1,0:T(8,128)(2,1)S(1)}, bf16[128,1024]{1,0:T(8,128)(2,1)S(1)}, u32[]{:S(2)}, u32[]{:S(2)}) collective-permute-start(bf16[128,1024]{1,0:T(8,128)(2,1)S(1)} %bitcast.18), channel_id=1, source_target_pairs={{0,32},{32,0},{64,96},{96,64},{1,33},{33,1},{65,97},{97,65},{2,34}... | collective-permute-start | bytes 786440 | tf_op jit(solution)/shard_map/ppermute | solution.py:306
  2.6 15.1 %collective-permute-start.2 = (bf16[128,1024]{1,0:T(8,128)(2,1)S(1)}, bf16[128,1024]{1,0:T(8,128)(2,1)S(1)}, u32[]{:S(2)}, u32[]{:S(2)}) collective-permute-start(bf16[128,1024]{1,0:T(8,128)(2,1)S(1)} %bitcast.11), channel_id=1, source_target_pairs={{0,64},{32,96},{64,0},{96,32},{1,65},{33,97},{65,1},{97,33},{2,66}... | collective-permute-start | bytes 786440 | tf_op jit(solution)/shard_map/ppermute | solution.py:306
  6.6 11.6 %collective-permute-start.3 = (bf16[128,1024]{1,0:T(8,128)(2,1)S(1)}, bf16[128,1024]{1,0:T(8,128)(2,1)S(1)}, u32[]{:S(2)}, u32[]{:S(2)}) collective-permute-start(bf16[128,1024]{1,0:T(8,128)(2,1)S(1)} %bitcast.19), channel_id=1, source_target_pairs={{0,96},{32,64},{64,32},{96,0},{1,97},{33,65},{65,33},{97,1},{2,98}... | collective-permute-start | bytes 786440 | tf_op jit(solution)/shard_map/ppermute | solution.py:306
  8.4 18.0 %all-to-all-start = ((bf16[32,16,256]{2,1,0:T(8,128)(2,1)}), bf16[32,16,256]{2,1,0:T(8,128)(2,1)S(1)}, u32[]{:S(2)}, u32[]{:S(2)}) async-start(bf16[32,16,256]{2,1,0:T(8,128)(2,1)} %shard_map.98), calls=%async_computation | async-start | bytes 524288 | tf_op jit(solution)/shard_map/all_to_all | solution.py:321
  18.6 10.3 %collective-permute-start.4 = (f32[8,1024]{1,0:T(8,128)S(1)}, f32[8,1024]{1,0:T(8,128)S(1)}, u32[]{:S(2)}, u32[]{:S(2)}) collective-permute-start(f32[8,1024]{1,0:T(8,128)S(1)} %shard_map.97._.a), channel_id=1, source_target_pairs={{0,64},{32,96},{64,0},{96,32},{1,65},{33,97},{65,1},{97,33},{2,66}... | collective-permute-start | bytes 98312 | tf_op jit(solution)/shard_map/ppermute | solution.py:306
  29.0 1.3 %collective-permute-start.5 = (bf16[8,1024]{1,0:T(8,128)(2,1)S(1)}, bf16[8,1024]{1,0:T(8,128)(2,1)S(1)}, u32[]{:S(2)}, u32[]{:S(2)}) collective-permute-start(bf16[8,1024]{1,0:T(8,128)(2,1)S(1)} %shard_map.100.inc_my), channel_id=1, source_target_pairs={{0,32},{32,0},{64,96},{96,64},{1,33},{33,1},{65,97},{97,65},{2,34}... | collective-permute-start | bytes 49160 | tf_op jit(solution)/shard_map/ppermute | solution.py:306
  30.2 27.9 %copy-start = (f32[112,64]{0,1:T(8,128)S(1)}, f32[112,64]{0,1:T(8,128)}, u32[]{:S(2)}) copy-start(f32[112,64]{0,1:T(8,128)} %param.10) | copy-start | bytes 86020
  35.7 1.3 %collective-permute-start.6 = (f32[8,1024]{1,0:T(8,128)S(1)}, f32[8,1024]{1,0:T(8,128)S(1)}, u32[]{:S(2)}, u32[]{:S(2)}) collective-permute-start(f32[8,1024]{1,0:T(8,128)S(1)} %get-tuple-element.37), channel_id=1, source_target_pairs={{0,32},{32,0},{64,96},{96,64},{1,33},{33,1},{65,97},{97,65},{2,34}... | collective-permute-start | bytes 98312 | tf_op jit(solution)/shard_map/ppermute | solution.py:306
  38.5 1.2 %collective-permute-start.7 = (f32[32,56]{1,0:T(8,128)S(1)}, f32[32,56]{1,0:T(8,128)S(1)}, u32[]{:S(2)}, u32[]{:S(2)}) collective-permute-start(f32[32,56]{1,0:T(8,128)S(1)} %get-tuple-element.39), channel_id=1, source_target_pairs={{0,32},{32,0},{64,96},{96,64},{1,33},{33,1},{65,97},{97,65},{2,34}... | collective-permute-start | bytes 21512 | tf_op jit(solution)/shard_map/ppermute | solution.py:306

commit v8 on v6

--- a/solution.py
+++ b/solution.py
@@ -50,13 +50,14 @@
     return pltpu.with_memory_space_constraint(x, pltpu.VMEM)
 
 
-def call(body, ins, outs, flops, nbytes, scratch=(), vmem=16):
+def call(body, ins, outs, flops, nbytes, scratch=(), vmem=16, aliases=None):
     return pl.pallas_call(
         body,
         out_shape=tuple(o for o, _ in outs),
         in_specs=list(ins),
         out_specs=tuple(s for _, s in outs),
         scratch_shapes=list(scratch),
+        input_output_aliases=aliases or {},
         compiler_params=pltpu.CompilerParams(vmem_limit_bytes=vmem * MIB),
         cost_estimate=pl.CostEstimate(flops=flops, bytes_accessed=nbytes, transcendentals=0),
     )
@@ -88,18 +89,18 @@
     return pl.ds(pl.multiple_of((core + 2 * side) * 128, 128), 128)
 
 
-def load_body(mem, eig, innovation, obs_weight, m_mine, m_mate, e_mine, e_mate, payload, iv, sem):
-    slices = start_all(halves_copies(mem, m_mine, m_mate, sem, 0))
-    copies = start_all([
+def split_body(mem, eig, innovation, obs_weight, m_mine, m_mate, e_mine, e_mate, iv, sem):
+    copies = halves_copies(mem, m_mine, m_mate, sem, 0) + halves_copies(eig, e_mine, e_mate, sem, 2) + [
         pltpu.make_async_copy(
             a.at[0, :, quarter_at(side)], iv.at[n, :, side * 128:(side + 1) * 128], sem.at[4 + 2 * n + side])
         for n, a in enumerate((innovation, obs_weight)) for side in range(2)
-    ])
-    slices += start_all(halves_copies(eig, e_mine, e_mate, sem, 2))
-    wait_all(copies)
+    ]
+    wait_all(start_all(copies))
+
+
+def load_body(iv, _, payload):
     for n in range(2):
         payload[:, n * 8:(n + 1) * 8, :] = iv[n].reshape(32, 8, 256).astype(BF)
-    wait_all(slices)
 
 
 def increment_of(scale, kron, ma, mb, ea, eb, cut):
@@ -130,7 +131,7 @@
         out[:, cut] = increment_of(scale, full[:, :256], ma, mb, ea, eb, cut)
 
 
-def increment_other(scale, kron, before, ma, mb, ea, eb, _, out):
+def increment_other(scale, kron, before, ma, mb, ea, eb, out):
     for g in range(0, 1024, 256):
         cut = slice(g, g + 256)
         out[:, cut] = before[:, cut] + increment_of(scale, kron[...], ma, mb, ea, eb, cut)
@@ -184,8 +185,12 @@
     out[...] = (a[...] + b[...]).astype(BF)
 
 
+def pass_body(_, x, same_x):
+    del x, same_x
+
+
 def obs_body(inc_my, inc_mt, onehot, onehot_t, innov, weight, near, interpolation,
-             adj_my, adj_mt, image_out, picked, depb, spread, far, sem):
+             adj_all, image_out, picked, depb, spread, far, sem):
     fetch = [
         start_all([
             pltpu.make_async_copy(
@@ -238,8 +243,8 @@
         terms.append(jnp.concatenate([turned[c * 16:(c + 1) * 16] for c in range(16)], axis=1))
     both = dot(jnp.concatenate(terms, axis=0).astype(BF), onehot[...])
     adj = both[:16] + both[16:]
-    adj_my[...] = jnp.where(first, adj[:8], adj[8:])
-    adj_mt[...] = jnp.where(first, adj[8:], adj[:8])
+    adj_all[:8] = jnp.where(first, adj[8:], adj[:8])
+    adj_all[8:] = jnp.where(first, adj[:8], adj[8:])
 
 
 def slots_body(place_hi, place_lo, image, out):
@@ -247,25 +252,25 @@
     out[...] = dot(place_hi[...], hi, TN) + dot(place_lo[...], lo, TN)
 
 
-def gradient_body(a0, a1, m0, m1, m2, m3, e0, e1, mate, mine):
+def gradient_body(adj, came, m_my, m_mt, o_my, o_mt, e_my, e_mt, f_my, f_mt, out):
     first = (lax.axis_index("band") & 1) == 0
-    adj = a0[...] + a1[...]
-    wide = jnp.broadcast_to(adj[None], (16, 8, 1024)).reshape(128, 1024)
     same = (iota((448, 256), 0) & 7) == (iota((448, 256), 1) & 7)
     sel = ones_where((iota((32, 256), 1) >> 3) == iota((32, 256), 0))
-    eig = jnp.concatenate([e0[...], e1[...]], axis=0)
-    for ma, mb, g in ((m1, m3, mate), (m0, m2, mine)):
-        weighted = jnp.concatenate(
-            [(m[...].astype(F32) * wide).astype(BF) for m in (ma, mb)], axis=0)
-        full = jnp.where(same, dot(eig, weighted, NT), 0.0)
-        own = jnp.sum(full.reshape(56, 8, 256), axis=1)
-        own = jnp.where(first, own, jnp.concatenate([own[28:], own[:28]], axis=0))
-        hi, mid, lo = parts3(own)
-        g[...] = dot(sel, hi, NT) + dot(sel, mid, NT) + dot(sel, lo, NT)
-
-
-def pack_body(mine, came, slots, out):
-    total = mine[...] + came[...]
+    total = None
+    for here, there, members, eigs in (
+            (adj[8:], came[:8], (m_my, o_my), (e_my, f_my)), (adj[:8], came[8:], (m_mt, o_mt), (e_mt, f_mt))):
+        wide = jnp.broadcast_to((here + there)[None], (16, 8, 1024)).reshape(128, 1024)
+        weighted = jnp.concatenate([(m[...].astype(F32) * wide).astype(BF) for m in members], axis=0)
+        term = dot(jnp.concatenate([e[...] for e in eigs], axis=0), weighted, NT)
+        total = term if total is None else total + term
+    own = jnp.sum(jnp.where(same, total, 0.0).reshape(56, 8, 256), axis=1)
+    own = jnp.where(first, own, jnp.concatenate([own[28:], own[:28]], axis=0))
+    hi, mid, _ = parts3(own)
+    out[...] = dot(sel, hi, NT) + dot(sel, mid, NT)
+
+
+def pack_body(mine, slots, out):
+    total = mine[...]
     gap = jnp.zeros((8, 8), F32)
     flat = [
         jnp.concatenate([total[r:r + 8], gap, total[r + 8:r + 16], gap], axis=1) for r in (0, 16)
@@ -305,18 +310,18 @@
         return lax.ppermute(x, "band", [(i, i ^ bit) for i in range(4)])
 
     dma = pltpu.SemaphoreType.DMA
-    m_my, m_mt, e_my, e_mt, payload = call(
-        load_body,
-        [HB] * 4,
+    m_my, m_mt, e_my, e_mt, iv = call(
+        split_body, [HB] * 4,
         [(pltpu.VMEM((16, 8, 1024), BF), VM)] * 2 + [(pltpu.VMEM((28, 8, 1024), BF), VM)] * 2
-        + [(pltpu.HBM((32, 16, 256), BF), VM)],
-        10 ** 6, 5 * 10 ** 6,
-        [pltpu.VMEM((2, 256, 256), F32), dma((8,))],
+        + [(pltpu.VMEM((2, 256, 256), F32), VM)], 0, 0, [dma((8,))],
     )(in_hbm(members), in_hbm(eigvecs), in_hbm(innovation), in_hbm(obs_weight))
     m_my, m_mt, e0, e_mt = [in_vmem(a.reshape(-1, 1024)) for a in (m_my, m_mt, e_my, e_mt)]
     m3 = over(m_mt, 3)
     m2 = over(m_my, 2)
     m1 = over(m_mt, 1)
+    (payload,) = call(
+        load_body, [VM, ANY], [(pltpu.VMEM((32, 16, 256), BF), VM)], 0, 0,
+    )(in_vmem(iv), m_my)
     got = lax.all_to_all(payload, "mem", split_axis=0, concat_axis=0, tiled=True)
     e1 = over(e_mt, 1)
     m1, m2, m3, e1 = [in_vmem(a) for a in (m1, m2, m3, e1)]
@@ -327,9 +332,9 @@
         25 * 10 ** 7, 2 * 10 ** 6, [pltpu.VMEM((64, 112), F32), dma(())],
     )(in_hbm(control.T), m_my, m1, e0, e1)
     (part,) = call(
-        lambda *refs: increment_other(scale, *refs), [VM] * 6 + [ANY], [(shape((8, 1024), F32), VM)],
+        lambda *refs: increment_other(scale, *refs), [VM] * 6, [(shape((8, 1024), F32), VM)],
         25 * 10 ** 7, 2 * 10 ** 6,
-    )(in_vmem(kron), in_vmem(part), m2, m3, e0, e1, m3)
+    )(in_vmem(kron), in_vmem(part), m2, m3, e0, e1)
 
     kept = call(
         prep_body,
@@ -343,12 +348,15 @@
     onehot, onehot_t, place_hi, place_lo, interp, innov, weight, innov_own, live_own = [in_vmem(a) for a in kept]
 
     (inc_my,) = call(
-        add_body, [VM, VM, ANY], [(shape((8, 1024), BF), VM)], 10 ** 4, 10 ** 5
+        add_body, [VM, VM, ANY], [(shape((8, 1024), BF), VM)], 10 ** 4, 10 ** 5,
     )(part, over(part, 2), place_hi)
     inc_mt = over(inc_my, 1)
-    adj_my, adj_mt, image = call(
+    (m3,) = call(
+        pass_body, [ANY, VM], [(pltpu.VMEM((128, 1024), BF), VM)], 0, 0, aliases={1: 0}
+    )(inc_mt, m3)
+    adj, image = call(
         obs_body, [VM] * 7 + [HB],
-        [(shape((8, 1024), F32), VM)] * 2 + [(pltpu.VMEM((64, 256), F32), VM)],
+        [(shape((16, 1024), F32), VM), (pltpu.VMEM((64, 256), F32), VM)],
         10 ** 9, 12 * 10 ** 6,
         [pltpu.VMEM((64, 256), BF), pltpu.VMEM((64, 256), BF), pltpu.VMEM((64, 256), F32),
          pltpu.VMEM((32, 256, 256), BF), dma((8,))],
@@ -357,13 +365,15 @@
     (slots,) = call(
         slots_body, [VM] * 3, [(pltpu.VMEM((256, 256), F32), VM)], 10 ** 7, 5 * 10 ** 5
     )(place_hi, place_lo, in_vmem(image))
-    g_mt, g_my = call(
-        gradient_body, [VM] * 8, [(shape((32, 56), F32), VM)] * 2, 5 * 10 ** 8, 2 * 10 ** 6
-    )(adj_my, over(adj_mt, 1), m_my, m1, m2, m3, e0, e1)
+    f_mt = over(e0, 1)
+    o_mt = over(in_vmem(m3), 1)
+    (terms,) = call(
+        gradient_body, [VM] * 10, [(shape((32, 56), F32), VM)], 5 * 10 ** 8, 2 * 10 ** 6
+    )(adj, over(adj, 1), m_my, m_mt, m2, o_mt, e0, e_mt, e1, f_mt)
 
     (sent,) = call(
-        pack_body, [VM] * 3, [(shape((64, 16, 128), BF), VM)], 10 ** 5, 6 * 10 ** 5
-    )(g_my, over(g_mt, 1), in_vmem(slots))
+        pack_body, [VM] * 2, [(shape((64, 16, 128), BF), VM)], 10 ** 5, 6 * 10 ** 5
+    )(terms, in_vmem(slots))
     groups = [[(2 * z + core) * 32 + t for z in range(2) for t in range(32)] for core in range(2)]
     arrived = lax.all_to_all(
         sent, ("band", "mem"), split_axis=0, concat_axis=0, axis_index_groups=groups, tiled=True)

time: 60.7 us -> 58.6 us (0.965)
  waiting for transfers between devices: 9.47 us -> 6.8 us
  starting transfers between devices: 14.8 us -> 16.4 us
    ppermute x8 -> x9, waiting for transfers between devices: 6.58 us -> 3.13 us  [over(): return lax.ppermute(x, 'band', [(i, i ^ bit) for i in range(4)])]
    ppermute x8 -> x9, starting transfers between devices: 7.01 us -> 8.59 us  [over(): return lax.ppermute(x, 'band', [(i, i ^ bit) for i in range(4)])]
    all_to_all x1, waiting for transfers between devices: 2.89 us -> 3.67 us  [per_device(): lax.all_to_all(payload, 'mem', split_axis=0, concat_axis=0, tiled=True)]
    pallas_call x5 -> x7, Pallas kernels: 9.82 us -> 9.21 us  [the longest x1 5.52 us: per_device(): call(obs_body, [VM] * 7 + [HB], [(shape((16, 1024), F32), VM), (pltpu.VME...]
  transfers between devices with their start and end apart: 9 -> 10, of which waited for: 5 -> 4; matrix products, arithmetic and copies ran while one was open for 0% -> 0% of each run, Pallas kernels for 8% -> 19%
where the time goes in v8:
time: 58.6 us; the launch traced here: 58.3 us
  blocking collectives  20.2 us (34%)
  starting transfers between devices  16.4 us (28%)
  Pallas kernels  14.2 us (24%)
  waiting for transfers between devices  6.8 us (12%)
  between operations  0.76 us (1%)
    all_to_all x1, blocking collectives, per_device(): lax.all_to_all(sent, ('band', 'mem'), split_axis=0, concat_axis=0, axis_i...  20.2 us
    ppermute x9, starting transfers between devices, over(): return lax.ppermute(x, 'band', [(i, i ^ bit) for i in range(4)])  8.59 us
    all_to_all x1, starting transfers between devices, per_device(): lax.all_to_all(payload, 'mem', split_axis=0, concat_axis=0, tiled=True)  7.79 us
    pallas_call x1, Pallas kernels, per_device(): call(obs_body, [VM] * 7 + [HB], [(shape((16, 1024), F32), VM), (pltpu.VME...  5.52 us
    all_to_all x1, waiting for transfers between devices, per_device(): lax.all_to_all(payload, 'mem', split_axis=0, concat_axis=0, tiled=True)  3.67 us
    ppermute x9, waiting for transfers between devices, over(): return lax.ppermute(x, 'band', [(i, i ^ bit) for i in range(4)])  3.13 us
    pallas_call x1, Pallas kernels, per_device(): call(prep_body, [HB] * 3 + [ANY] + [HB] * 2 + [ANY], [(pltpu.VMEM(d, t),...  2.48 us
    pallas_call x1, Pallas kernels, per_device(): call(split_body, [HB] * 4, [(pltpu.VMEM((16, 8, 1024), BF), VM)] * 2 + [(...  1.55 us
  transfers between devices with their start and end apart: 10, of which 4 were waited for; matrix products, arithmetic and copies ran while one was open for 0% of the time, Pallas kernels for 19%

profile of v8, /device:TPU:0, one launch (start us, length us, event | category | flops | bytes accessed | tf_op | source)
XLA Modules:
  0.0 58.3 jit_solution(11079287313988853379)
XLA Ops:
  0.6 1.5 %shard_map.95 = (bf16[16,8,1024]{2,1,0:T(8,128)(2,1)S(1)}, bf16[16,8,1024]{2,1,0:T(8,128)(2,1)S(1)}, bf16[28,8,1024]{2,1,0:T(8,128)(2,1)S(1)}, bf16[28,8,1024]{2,1,0:T(8,128)(2,1)S(1)}, f32[2,256,256]{2,1,0:T(8,128)S(1)}) custom-call(bf16[16,16,1024]{2,1,0:T(8,128)(2,1)} %mem.1, bf16[28,16,1024]{2,1,0:T(8,128)(2,1)} %eig.1, f32[1,256,512]{2,1,0:T(8,128)} %innovation.3, ...), custom_call_target="tpu_custom_call" | custom-call | tf_op jit(solution)/shard_map/pallas_call | solution.py:313
  2.2 0.1 collective-permute-start.1
  2.3 0.5 collective-permute-start
  2.8 4.0 %collective-permute-start.2 = (bf16[128,1024]{1,0:T(8,128)(2,1)S(1)}, bf16[128,1024]{1,0:T(8,128)(2,1)S(1)}, u32[]{:S(2)}, u32[]{:S(2)}) collective-permute-start(bf16[128,1024]{1,0:T(8,128)(2,1)S(1)} %bitcast.12), channel_id=1, source_target_pairs={{0,64},{32,96},{64,0},{96,32},{1,65},{33,97},{65,1},{97,33},{2,66}... | collective-permute-start | bytes 786440 | tf_op jit(solution)/shard_map/ppermute | solution.py:310
  6.7 0.7 %shard_map.98 = bf16[32,16,256]{2,1,0:T(8,128)(2,1)} custom-call(f32[2,256,256]{2,1,0:T(8,128)S(1)} %get-tuple-element.28.iv, bf16[128,1024]{1,0:T(8,128)(2,1)S(1)} %bitcast.13), custom_call_target="tpu_custom_call" | custom-call | tf_op jit(solution)/shard_map/pallas_call | solution.py:322
  7.5 7.8 %all-to-all-start = ((bf16[32,16,256]{2,1,0:T(8,128)(2,1)}), bf16[32,16,256]{2,1,0:T(8,128)(2,1)S(1)}, u32[]{:S(2)}, u32[]{:S(2)}) async-start(bf16[32,16,256]{2,1,0:T(8,128)(2,1)} %shard_map.98), calls=%async_computation | async-start | bytes 524288 | tf_op jit(solution)/shard_map/all_to_all | solution.py:325
  15.3 0.5 collective-permute-start.8
  15.7 1.4 %shard_map.96 = (f32[8,1024]{1,0:T(8,128)S(1)}, bf16[448,256]{1,0:T(8,128)(2,1)S(1)}) custom-call(f32[64,112]{1,0:T(8,128)} %bitcast.21, bf16[128,1024]{1,0:T(8,128)(2,1)S(1)} %bitcast.14, bf16[128,1024]{1,0:T(8,128)(2,1)S(1)} %collective-permute-done.refs_2_, bf16[224,1024]{1,0:T(8,128)(2,1)S(1)} %bitcast.9, ...), custom_call_target="tpu_custom_call" | custom-call | flops 250000000 | bytes 2000000 | tf_op jit(solution)/shard_map/pallas_call | solution.py:329
  17.2 1.3 %collective-permute-done.3.refs_3_.x = bf16[128,1024]{1,0:T(8,128)(2,1)S(1)} collective-permute-done((bf16[128,1024]{1,0:T(8,128)(2,1)S(1)}, bf16[128,1024]{1,0:T(8,128)(2,1)S(1)}, u32[]{:S(2)}, u32[]{:S(2)}) %collective-permute-start.3) | collective-permute-done | bytes 262176 | tf_op jit(solution)/shard_map/ppermute | solution.py:310
  18.5 0.4 shard_map.97._.a
  18.9 2.9 %collective-permute-start.4 = (f32[8,1024]{1,0:T(8,128)S(1)}, f32[8,1024]{1,0:T(8,128)S(1)}, u32[]{:S(2)}, u32[]{:S(2)}) collective-permute-start(f32[8,1024]{1,0:T(8,128)S(1)} %shard_map.97._.a), channel_id=1, source_target_pairs={{0,64},{32,96},{64,0},{96,32},{1,65},{33,97},{65,1},{97,33},{2,66}... | collective-permute-start | bytes 98312 | tf_op jit(solution)/shard_map/ppermute | solution.py:310
  21.8 3.7 %all-to-all-done.got_in = bf16[32,16,256]{2,1,0:T(8,128)(2,1)S(1)} async-done(((bf16[32,16,256]{2,1,0:T(8,128)(2,1)}), bf16[32,16,256]{2,1,0:T(8,128)(2,1)S(1)}, u32[]{:S(2)}, u32[]{:S(2)}) %all-to-all-start) | async-done | bytes 262176 | tf_op jit(solution)/shard_map/all_to_all | solution.py:325
  25.5 2.5 %shard_map.99 = (bf16[1024,1024]{1,0:T(8,128)(2,1)S(1)}, bf16[1024,1024]{1,0:T(8,128)(2,1)S(1)}, bf16[64,256]{1,0:T(8,128)(2,1)S(1)}, bf16[64,256]{1,0:T(8,128)(...) custom-call(s32[16,64]{1,0:T(8,128)} %bitcast.23, ...), custom_call_target="tpu_custom_call" | custom-call | flops 100000000 | bytes 12000000 | tf_op jit(solution)/shard_map/pallas_call | solution.py:339
  28.0 0.1 collective-permute-start.5
  28.1 1.2 %collective-permute-done.5.inc_mt._ = bf16[8,1024]{1,0:T(8,128)(2,1)S(1)} collective-permute-done((bf16[8,1024]{1,0:T(8,128)(2,1)S(1)}, bf16[8,1024]{1,0:T(8,128)(2,1)S(1)}, u32[]{:S(2)}, u32[]{:S(2)}) %collective-permute-start.5) | collective-permute-done | bytes 16416 | tf_op jit(solution)/shard_map/ppermute | solution.py:310
  29.3 0.2 collective-permute-start.7
  29.4 5.5 %shard_map.101 = (f32[16,1024]{1,0:T(8,128)S(1)}, f32[64,256]{1,0:T(8,128)S(1)}) custom-call(bf16[8,1024]{1,0:T(8,128)(2,1)S(1)} %shard_map.100.inc_my, bf16[8,1024]{1,0:T(8,128)(2,1)S(1)} %collective-permute-done.5.inc_mt._, bf16[1024,1024]{1,0:T(8,128)(2,1)S(1)} %get-tuple-element.30.onehot, bf16[1024,1024]{1,0:T(8,128)(2,1)S(1)} %get-tuple-element.31.onehot_t, ...), custom_call_target="tpu_custom_call" | custom-call | flops 1000000000 | bytes 12000000 | tf_op jit(solution)/shard_map/pallas_call | solution.py:357
  35.0 0.4 collective-permute-start.6
  35.4 0.2 shard_map.104.slots
  35.7 0.6 %collective-permute-done.6.came = f32[16,1024]{1,0:T(8,128)S(1)} collective-permute-done((f32[16,1024]{1,0:T(8,128)S(1)}, f32[16,1024]{1,0:T(8,128)S(1)}, u32[]{:S(2)}, u32[]{:S(2)}) %collective-permute-start.6) | collective-permute-done | bytes 65568 | tf_op jit(solution)/shard_map/ppermute | solution.py:310
  36.3 0.9 %shard_map.103.mine = f32[32,56]{1,0:T(8,128)S(1)} custom-call(f32[16,1024]{1,0:T(8,128)S(1)} %get-tuple-element.35.adj, f32[16,1024]{1,0:T(8,128)S(1)} %collective-permute-done.6.came, bf16[128,1024]{1,0:T(8,128)(2,1)S(1)} %bitcast.15, bf16[128,1024]{1,0:T(8,128)(2,1)S(1)} %bitcast.20, bf16[128,1024]{1,0:T(8,128)(2,1)S(1)} %collective-permute-done.2.refs_2_.o_my, ...), custom_call_target="tpu_custom_call" | custom-call | flops 500000000 | bytes 2000000 | tf_op jit(solution)/shard_map/pallas_call | solution.py:370
  37.2 0.1 shard_map.105
  37.3 20.2 %all_to_all.10.refs_0_ = bf16[64,16,128]{2,1,0:T(8,128)(2,1)S(1)} all-to-all(bf16[64,16,128]{2,1,0:T(8,128)(2,1)S(1)} %shard_map.105), channel_id=1, replica_groups={{0,1,2,3,4,5,6,7,8,9,10,11,12,13,14,15,16,17,18,19,20,21,22,23,24,25,26..., dimensions={0} | all-to-all | bytes 524288 | tf_op jit(solution)/shard_map/all_to_all | solution.py:378
  57.5 0.8 %shard_map.106 = (f32[16,112]{1,0:T(8,128)}, f32[1,256,128]{2,1,0:T(8,128)}) custom-call(bf16[64,16,128]{2,1,0:T(8,128)(2,1)S(1)} %all_to_all.10.refs_0_, f32[64,112]{1,0:T(8,128)S(1)} %bitcast.22, f32[256,128]{1,0:T(8,128)S(1)} %get-tuple-element.38.refs_2_, f32[256,128]{1,0:T(8,128)S(1)} %get-tuple-element.39.refs_3_), custom_call_target="tpu_custom_call" | custom-call | flops 1000000 | bytes 600000 | tf_op jit(solution)/shard_map/pallas_call | solution.py:380
  (11 shorter events, 0.0 us)
Async XLA Ops:
  2.2 13.5 %collective-permute-start.1 = (bf16[224,1024]{1,0:T(8,128)(2,1)S(1)}, bf16[224,1024]{1,0:T(8,128)(2,1)S(1)}, u32[]{:S(2)}, u32[]{:S(2)}) collective-permute-start(bf16[224,1024]{1,0:T(8,128)(2,1)S(1)} %bitcast.16), channel_id=1, source_target_pairs={{0,32},{32,0},{64,96},{96,64},{1,33},{33,1},{65,97},{97,65},{2,34}... | collective-permute-start | bytes 1376264 | tf_op jit(solution)/shard_map/ppermute | solution.py:310
  2.3 13.4 %collective-permute-start = (bf16[128,1024]{1,0:T(8,128)(2,1)S(1)}, bf16[128,1024]{1,0:T(8,128)(2,1)S(1)}, u32[]{:S(2)}, u32[]{:S(2)}) collective-permute-start(bf16[128,1024]{1,0:T(8,128)(2,1)S(1)} %bitcast.18), channel_id=1, source_target_pairs={{0,32},{32,0},{64,96},{96,64},{1,33},{33,1},{65,97},{97,65},{2,34}... | collective-permute-start | bytes 786440 | tf_op jit(solution)/shard_map/ppermute | solution.py:310
  2.8 14.4 %collective-permute-start.2 = (bf16[128,1024]{1,0:T(8,128)(2,1)S(1)}, bf16[128,1024]{1,0:T(8,128)(2,1)S(1)}, u32[]{:S(2)}, u32[]{:S(2)}) collective-permute-start(bf16[128,1024]{1,0:T(8,128)(2,1)S(1)} %bitcast.12), channel_id=1, source_target_pairs={{0,64},{32,96},{64,0},{96,32},{1,65},{33,97},{65,1},{97,33},{2,66}... | collective-permute-start | bytes 786440 | tf_op jit(solution)/shard_map/ppermute | solution.py:310
  6.7 11.7 %collective-permute-start.3 = (bf16[128,1024]{1,0:T(8,128)(2,1)S(1)}, bf16[128,1024]{1,0:T(8,128)(2,1)S(1)}, u32[]{:S(2)}, u32[]{:S(2)}) collective-permute-start(bf16[128,1024]{1,0:T(8,128)(2,1)S(1)} %bitcast.19), channel_id=1, source_target_pairs={{0,96},{32,64},{64,32},{96,0},{1,97},{33,65},{65,33},{97,1},{2,98}... | collective-permute-start | bytes 786440 | tf_op jit(solution)/shard_map/ppermute | solution.py:310
  7.5 18.0 %all-to-all-start = ((bf16[32,16,256]{2,1,0:T(8,128)(2,1)}), bf16[32,16,256]{2,1,0:T(8,128)(2,1)S(1)}, u32[]{:S(2)}, u32[]{:S(2)}) async-start(bf16[32,16,256]{2,1,0:T(8,128)(2,1)} %shard_map.98), calls=%async_computation | async-start | bytes 524288 | tf_op jit(solution)/shard_map/all_to_all | solution.py:325
  15.3 20.4 %collective-permute-start.8 = (bf16[224,1024]{1,0:T(8,128)(2,1)S(1)}, bf16[224,1024]{1,0:T(8,128)(2,1)S(1)}, u32[]{:S(2)}, u32[]{:S(2)}) collective-permute-start(bf16[224,1024]{1,0:T(8,128)(2,1)S(1)} %bitcast.8), channel_id=1, source_target_pairs={{0,32},{32,0},{64,96},{96,64},{1,33},{33,1},{65,97},{97,65},{2,34}... | collective-permute-start | bytes 1376264 | tf_op jit(solution)/shard_map/ppermute | solution.py:310
  18.9 9.1 %collective-permute-start.4 = (f32[8,1024]{1,0:T(8,128)S(1)}, f32[8,1024]{1,0:T(8,128)S(1)}, u32[]{:S(2)}, u32[]{:S(2)}) collective-permute-start(f32[8,1024]{1,0:T(8,128)S(1)} %shard_map.97._.a), channel_id=1, source_target_pairs={{0,64},{32,96},{64,0},{96,32},{1,65},{33,97},{65,1},{97,33},{2,66}... | collective-permute-start | bytes 98312 | tf_op jit(solution)/shard_map/ppermute | solution.py:310
  28.0 1.3 %collective-permute-start.5 = (bf16[8,1024]{1,0:T(8,128)(2,1)S(1)}, bf16[8,1024]{1,0:T(8,128)(2,1)S(1)}, u32[]{:S(2)}, u32[]{:S(2)}) collective-permute-start(bf16[8,1024]{1,0:T(8,128)(2,1)S(1)} %shard_map.100.inc_my), channel_id=1, source_target_pairs={{0,32},{32,0},{64,96},{96,64},{1,33},{33,1},{65,97},{97,65},{2,34}... | collective-permute-start | bytes 49160 | tf_op jit(solution)/shard_map/ppermute | solution.py:310
  29.3 7.0 %collective-permute-start.7 = (bf16[128,1024]{1,0:T(8,128)(2,1)S(1)}, bf16[128,1024]{1,0:T(8,128)(2,1)S(1)}, u32[]{:S(2)}, u32[]{:S(2)}) collective-permute-start(bf16[128,1024]{1,0:T(8,128)(2,1)S(1)} %shard_map.102), channel_id=1, source_target_pairs={{0,32},{32,0},{64,96},{96,64},{1,33},{33,1},{65,97},{97,65},{2,34}... | collective-permute-start | bytes 786440 | tf_op jit(solution)/shard_map/ppermute | solution.py:310
  35.0 22.5 %copy-start = (f32[112,64]{0,1:T(8,128)S(1)}, f32[112,64]{0,1:T(8,128)}, u32[]{:S(2)}) copy-start(f32[112,64]{0,1:T(8,128)} %param.10) | copy-start | bytes 86020
  35.0 1.3 %collective-permute-start.6 = (f32[16,1024]{1,0:T(8,128)S(1)}, f32[16,1024]{1,0:T(8,128)S(1)}, u32[]{:S(2)}, u32[]{:S(2)}) collective-permute-start(f32[16,1024]{1,0:T(8,128)S(1)} %get-tuple-element.35.adj), channel_id=1, source_target_pairs={{0,32},{32,0},{64,96},{96,64},{1,33},{33,1},{65,97},{97,65},{2,34}... | collective-permute-start | bytes 196616 | tf_op jit(solution)/shard_map/ppermute | solution.py:310

commit v9 on v8

--- a/solution.py
+++ b/solution.py
@@ -181,15 +181,11 @@
     wait_all(copies[5:])
 
 
-def add_body(a, b, _, out):
-    out[...] = (a[...] + b[...]).astype(BF)
-
-
-def pass_body(_, x, same_x):
-    del x, same_x
-
-
-def obs_body(inc_my, inc_mt, onehot, onehot_t, innov, weight, near, interpolation,
+def pass_body(*refs):
+    del refs
+
+
+def obs_body(p0, p1, p2, p3, onehot, onehot_t, innov, weight, near, interpolation,
              adj_all, image_out, picked, depb, spread, far, sem):
     fetch = [
         start_all([
@@ -205,8 +201,8 @@
 
     band = lax.axis_index("band")
     first = (band & 1) == 0
-    mine = inc_my[...].astype(F32)
-    mate = inc_mt[...].astype(F32)
+    mine = p0[...] + p2[...]
+    mate = p1[...] + p3[...]
     inc = jnp.concatenate([jnp.where(first, mine, mate), jnp.where(first, mate, mine)], axis=0).astype(BF)
     r0 = iota((256, 256), 0)
     r1 = iota((256, 256), 1)
@@ -347,20 +343,19 @@
     )(in_hbm(columns.T), in_hbm(owners), in_hbm(interpolation), got, in_hbm(innovation), in_hbm(obs_weight), part)
     onehot, onehot_t, place_hi, place_lo, interp, innov, weight, innov_own, live_own = [in_vmem(a) for a in kept]
 
-    (inc_my,) = call(
-        add_body, [VM, VM, ANY], [(shape((8, 1024), BF), VM)], 10 ** 4, 10 ** 5,
-    )(part, over(part, 2), place_hi)
-    inc_mt = over(inc_my, 1)
+    p3 = over(part, 3)
+    p2 = over(part, 2)
+    p1 = over(part, 1)
     (m3,) = call(
-        pass_body, [ANY, VM], [(pltpu.VMEM((128, 1024), BF), VM)], 0, 0, aliases={1: 0}
-    )(inc_mt, m3)
+        pass_body, [ANY] * 4 + [VM], [(pltpu.VMEM((128, 1024), BF), VM)], 0, 0, aliases={4: 0}
+    )(p1, p2, p3, place_hi, m3)
     adj, image = call(
-        obs_body, [VM] * 7 + [HB],
+        obs_body, [VM] * 9 + [HB],
         [(shape((16, 1024), F32), VM), (pltpu.VMEM((64, 256), F32), VM)],
         10 ** 9, 12 * 10 ** 6,
         [pltpu.VMEM((64, 256), BF), pltpu.VMEM((64, 256), BF), pltpu.VMEM((64, 256), F32),
          pltpu.VMEM((32, 256, 256), BF), dma((8,))],
-    )(inc_my, inc_mt, onehot, onehot_t, innov, weight, interp, in_hbm(interpolation))
+    )(part, p1, p2, p3, onehot, onehot_t, innov, weight, interp, in_hbm(interpolation))
 
     (slots,) = call(
         slots_body, [VM] * 3, [(pltpu.VMEM((256, 256), F32), VM)], 10 ** 7, 5 * 10 ** 5

time: 58.6 us -> 58.7 us (level)
  waiting for transfers between devices: 6.8 us -> 4.72 us
  blocking collectives: 20.2 us -> 21.3 us
  starting transfers between devices: 16.4 us -> 17.4 us
    all_to_all x1, blocking collectives: 20.2 us -> 21.3 us  [per_device(): lax.all_to_all(sent, ('band', 'mem'), split_axis=0, concat_axis=0, axis_i...]
    all_to_all x1, waiting for transfers between devices: 3.67 us -> 2.55 us  [per_device(): lax.all_to_all(payload, 'mem', split_axis=0, concat_axis=0, tiled=True)]
    ppermute x9 -> x10, starting transfers between devices: 8.59 us -> 9.62 us  [over(): return lax.ppermute(x, 'band', [(i, i ^ bit) for i in range(4)])]
    ppermute x9 -> x10, waiting for transfers between devices: 3.13 us -> 2.17 us  [over(): return lax.ppermute(x, 'band', [(i, i ^ bit) for i in range(4)])]
    pallas_call x3 -> x2, Pallas kernels: 5.53 us -> 5.55 us  [the longest x1 5.55 us: per_device(): call(obs_body, [VM] * 9 + [HB], [(shape((16, 1024), F32), VM), (pltpu.VME...]
  transfers between devices with their start and end apart: 10 -> 11, of which waited for: 4 -> 4; matrix products, arithmetic and copies ran while one was open for 0% -> 0% of each run, Pallas kernels for 19% -> 19%
where the time goes in v9:
time: 58.7 us; the launch traced here: 58.3 us
  blocking collectives  21.3 us (36%)
  starting transfers between devices  17.4 us (30%)
  Pallas kernels  14.2 us (24%)
  waiting for transfers between devices  4.72 us (8%)
  between operations  0.75 us (1%)
    all_to_all x1, blocking collectives, per_device(): lax.all_to_all(sent, ('band', 'mem'), split_axis=0, concat_axis=0, axis_i...  21.3 us
    ppermute x10, starting transfers between devices, over(): return lax.ppermute(x, 'band', [(i, i ^ bit) for i in range(4)])  9.62 us
    all_to_all x1, starting transfers between devices, per_device(): lax.all_to_all(payload, 'mem', split_axis=0, concat_axis=0, tiled=True)  7.79 us
    pallas_call x1, Pallas kernels, per_device(): call(obs_body, [VM] * 9 + [HB], [(shape((16, 1024), F32), VM), (pltpu.VME...  5.55 us
    all_to_all x1, waiting for transfers between devices, per_device(): lax.all_to_all(payload, 'mem', split_axis=0, concat_axis=0, tiled=True)  2.55 us
    pallas_call x1, Pallas kernels, per_device(): call(prep_body, [HB] * 3 + [ANY] + [HB] * 2 + [ANY], [(pltpu.VMEM(d, t),...  2.48 us
    ppermute x10, waiting for transfers between devices, over(): return lax.ppermute(x, 'band', [(i, i ^ bit) for i in range(4)])  2.17 us
    pallas_call x1, Pallas kernels, per_device(): call(split_body, [HB] * 4, [(pltpu.VMEM((16, 8, 1024), BF), VM)] * 2 + [(...  1.55 us
  transfers between devices with their start and end apart: 11, of which 4 were waited for; matrix products, arithmetic and copies ran while one was open for 0% of the time, Pallas kernels for 19%

profile of v9, /device:TPU:0, one launch (start us, length us, event | category | flops | bytes accessed | tf_op | source)
XLA Modules:
  0.0 58.3 jit_solution(5706994013714184033)
XLA Ops:
  0.6 1.5 %shard_map.95 = (bf16[16,8,1024]{2,1,0:T(8,128)(2,1)S(1)}, bf16[16,8,1024]{2,1,0:T(8,128)(2,1)S(1)}, bf16[28,8,1024]{2,1,0:T(8,128)(2,1)S(1)}, bf16[28,8,1024]{2,1,0:T(8,128)(2,1)S(1)}, f32[2,256,256]{2,1,0:T(8,128)S(1)}) custom-call(bf16[16,16,1024]{2,1,0:T(8,128)(2,1)} %mem.1, bf16[28,16,1024]{2,1,0:T(8,128)(2,1)} %eig.1, f32[1,256,512]{2,1,0:T(8,128)} %innovation.3, ...), custom_call_target="tpu_custom_call" | custom-call | tf_op jit(solution)/shard_map/pallas_call | solution.py:309
  2.2 0.1 collective-permute-start.1
  2.3 0.5 collective-permute-start
  2.8 4.0 %collective-permute-start.2 = (bf16[128,1024]{1,0:T(8,128)(2,1)S(1)}, bf16[128,1024]{1,0:T(8,128)(2,1)S(1)}, u32[]{:S(2)}, u32[]{:S(2)}) collective-permute-start(bf16[128,1024]{1,0:T(8,128)(2,1)S(1)} %bitcast.12), channel_id=1, source_target_pairs={{0,64},{32,96},{64,0},{96,32},{1,65},{33,97},{65,1},{97,33},{2,66}... | collective-permute-start | bytes 786440 | tf_op jit(solution)/shard_map/ppermute | solution.py:306
  6.7 0.7 %shard_map.98 = bf16[32,16,256]{2,1,0:T(8,128)(2,1)} custom-call(f32[2,256,256]{2,1,0:T(8,128)S(1)} %get-tuple-element.28.iv, bf16[128,1024]{1,0:T(8,128)(2,1)S(1)} %bitcast.13), custom_call_target="tpu_custom_call" | custom-call | tf_op jit(solution)/shard_map/pallas_call | solution.py:318
  7.5 7.8 %all-to-all-start = ((bf16[32,16,256]{2,1,0:T(8,128)(2,1)}), bf16[32,16,256]{2,1,0:T(8,128)(2,1)S(1)}, u32[]{:S(2)}, u32[]{:S(2)}) async-start(bf16[32,16,256]{2,1,0:T(8,128)(2,1)} %shard_map.98), calls=%async_computation | async-start | bytes 524288 | tf_op jit(solution)/shard_map/all_to_all | solution.py:321
  15.3 0.5 collective-permute-start.9
  15.7 1.4 %shard_map.96 = (f32[8,1024]{1,0:T(8,128)S(1)}, bf16[448,256]{1,0:T(8,128)(2,1)S(1)}) custom-call(f32[64,112]{1,0:T(8,128)} %bitcast.21, bf16[128,1024]{1,0:T(8,128)(2,1)S(1)} %bitcast.14, bf16[128,1024]{1,0:T(8,128)(2,1)S(1)} %collective-permute-done.refs_2_, bf16[224,1024]{1,0:T(8,128)(2,1)S(1)} %bitcast.9, ...), custom_call_target="tpu_custom_call" | custom-call | flops 250000000 | bytes 2000000 | tf_op jit(solution)/shard_map/pallas_call | solution.py:325
  17.2 1.3 %collective-permute-done.3.refs_3_.refs_4_ = bf16[128,1024]{1,0:T(8,128)(2,1)S(1)} collective-permute-done((bf16[128,1024]{1,0:T(8,128)(2,1)S(1)}, bf16[128,1024]{1,0:T(8,128)(2,1)S(1)}, u32[]{:S(2)}, u32[]{:S(2)}) %collective-permute-start.3) | collective-permute-done | bytes 262176 | tf_op jit(solution)/shard_map/ppermute | solution.py:306
  18.5 0.4 shard_map.97._.p0
  18.9 0.3 collective-permute-start.4
  19.2 3.7 %collective-permute-start.5 = (f32[8,1024]{1,0:T(8,128)S(1)}, f32[8,1024]{1,0:T(8,128)S(1)}, u32[]{:S(2)}, u32[]{:S(2)}) collective-permute-start(f32[8,1024]{1,0:T(8,128)S(1)} %shard_map.97._.p0), channel_id=1, source_target_pairs={{0,64},{32,96},{64,0},{96,32},{1,65},{33,97},{65,1},{97,33},{2,66}... | collective-permute-start | bytes 98312 | tf_op jit(solution)/shard_map/ppermute | solution.py:306
  22.9 2.5 %all-to-all-done.got_in = bf16[32,16,256]{2,1,0:T(8,128)(2,1)S(1)} async-done(((bf16[32,16,256]{2,1,0:T(8,128)(2,1)}), bf16[32,16,256]{2,1,0:T(8,128)(2,1)S(1)}, u32[]{:S(2)}, u32[]{:S(2)}) %all-to-all-start) | async-done | bytes 262176 | tf_op jit(solution)/shard_map/all_to_all | solution.py:321
  25.5 2.5 %shard_map.99 = (bf16[1024,1024]{1,0:T(8,128)(2,1)S(1)}, bf16[1024,1024]{1,0:T(8,128)(2,1)S(1)}, bf16[64,256]{1,0:T(8,128)(2,1)S(1)}, bf16[64,256]{1,0:T(8,128)(...) custom-call(s32[16,64]{1,0:T(8,128)} %bitcast.23, ...), custom_call_target="tpu_custom_call" | custom-call | flops 100000000 | bytes 12000000 | tf_op jit(solution)/shard_map/pallas_call | solution.py:335
  28.0 0.2 collective-permute-done.6.p3.refs_2_
  28.2 0.1 collective-permute-start.8
  28.3 5.5 %shard_map.100 = (f32[16,1024]{1,0:T(8,128)S(1)}, f32[64,256]{1,0:T(8,128)S(1)}) custom-call(f32[8,1024]{1,0:T(8,128)S(1)} %shard_map.97._.p0, f32[8,1024]{1,0:T(8,128)S(1)} %collective-permute-done.4.p1.refs_0_, f32[8,1024]{1,0:T(8,128)S(1)} %collective-permute-done.5.p2.refs_1_, f32[8,1024]{1,0:T(8,128)S(1)} %collective-permute-done.6.p3.refs_2_, ...), custom_call_target="tpu_custom_call" | custom-call | flops 1000000000 | bytes 12000000 | tf_op jit(solution)/shard_map/pallas_call | solution.py:352
  33.9 0.5 collective-permute-start.7
  34.4 0.2 shard_map.103.slots
  34.6 0.6 %collective-permute-done.7.came = f32[16,1024]{1,0:T(8,128)S(1)} collective-permute-done((f32[16,1024]{1,0:T(8,128)S(1)}, f32[16,1024]{1,0:T(8,128)S(1)}, u32[]{:S(2)}, u32[]{:S(2)}) %collective-permute-start.7) | collective-permute-done | bytes 65568 | tf_op jit(solution)/shard_map/ppermute | solution.py:306
  35.3 0.9 %shard_map.102.mine = f32[32,56]{1,0:T(8,128)S(1)} custom-call(f32[16,1024]{1,0:T(8,128)S(1)} %get-tuple-element.34.adj, f32[16,1024]{1,0:T(8,128)S(1)} %collective-permute-done.7.came, bf16[128,1024]{1,0:T(8,128)(2,1)S(1)} %bitcast.15, bf16[128,1024]{1,0:T(8,128)(2,1)S(1)} %bitcast.20, bf16[128,1024]{1,0:T(8,128)(2,1)S(1)} %collective-permute-done.2.refs_2_.o_my, ...), custom_call_target="tpu_custom_call" | custom-call | flops 500000000 | bytes 2000000 | tf_op jit(solution)/shard_map/pallas_call | solution.py:365
  36.2 0.1 shard_map.104
  36.3 21.3 %all_to_all.10.refs_0_ = bf16[64,16,128]{2,1,0:T(8,128)(2,1)S(1)} all-to-all(bf16[64,16,128]{2,1,0:T(8,128)(2,1)S(1)} %shard_map.104), channel_id=1, replica_groups={{0,1,2,3,4,5,6,7,8,9,10,11,12,13,14,15,16,17,18,19,20,21,22,23,24,25,26..., dimensions={0} | all-to-all | bytes 524288 | tf_op jit(solution)/shard_map/all_to_all | solution.py:373
  57.6 0.8 %shard_map.105 = (f32[16,112]{1,0:T(8,128)}, f32[1,256,128]{2,1,0:T(8,128)}) custom-call(bf16[64,16,128]{2,1,0:T(8,128)(2,1)S(1)} %all_to_all.10.refs_0_, f32[64,112]{1,0:T(8,128)S(1)} %bitcast.22, f32[256,128]{1,0:T(8,128)S(1)} %get-tuple-element.38.refs_2_, f32[256,128]{1,0:T(8,128)S(1)} %get-tuple-element.39.refs_3_), custom_call_target="tpu_custom_call" | custom-call | flops 1000000 | bytes 600000 | tf_op jit(solution)/shard_map/pallas_call | solution.py:375
  (12 shorter events, 0.0 us)
Async XLA Ops:
  2.2 13.5 %collective-permute-start.1 = (bf16[224,1024]{1,0:T(8,128)(2,1)S(1)}, bf16[224,1024]{1,0:T(8,128)(2,1)S(1)}, u32[]{:S(2)}, u32[]{:S(2)}) collective-permute-start(bf16[224,1024]{1,0:T(8,128)(2,1)S(1)} %bitcast.16), channel_id=1, source_target_pairs={{0,32},{32,0},{64,96},{96,64},{1,33},{33,1},{65,97},{97,65},{2,34}... | collective-permute-start | bytes 1376264 | tf_op jit(solution)/shard_map/ppermute | solution.py:306
  2.3 13.4 %collective-permute-start = (bf16[128,1024]{1,0:T(8,128)(2,1)S(1)}, bf16[128,1024]{1,0:T(8,128)(2,1)S(1)}, u32[]{:S(2)}, u32[]{:S(2)}) collective-permute-start(bf16[128,1024]{1,0:T(8,128)(2,1)S(1)} %bitcast.18), channel_id=1, source_target_pairs={{0,32},{32,0},{64,96},{96,64},{1,33},{33,1},{65,97},{97,65},{2,34}... | collective-permute-start | bytes 786440 | tf_op jit(solution)/shard_map/ppermute | solution.py:306
  2.8 14.4 %collective-permute-start.2 = (bf16[128,1024]{1,0:T(8,128)(2,1)S(1)}, bf16[128,1024]{1,0:T(8,128)(2,1)S(1)}, u32[]{:S(2)}, u32[]{:S(2)}) collective-permute-start(bf16[128,1024]{1,0:T(8,128)(2,1)S(1)} %bitcast.12), channel_id=1, source_target_pairs={{0,64},{32,96},{64,0},{96,32},{1,65},{33,97},{65,1},{97,33},{2,66}... | collective-permute-start | bytes 786440 | tf_op jit(solution)/shard_map/ppermute | solution.py:306
  6.7 11.7 %collective-permute-start.3 = (bf16[128,1024]{1,0:T(8,128)(2,1)S(1)}, bf16[128,1024]{1,0:T(8,128)(2,1)S(1)}, u32[]{:S(2)}, u32[]{:S(2)}) collective-permute-start(bf16[128,1024]{1,0:T(8,128)(2,1)S(1)} %bitcast.19), channel_id=1, source_target_pairs={{0,96},{32,64},{64,32},{96,0},{1,97},{33,65},{65,33},{97,1},{2,98}... | collective-permute-start | bytes 786440 | tf_op jit(solution)/shard_map/ppermute | solution.py:306
  7.5 18.0 %all-to-all-start = ((bf16[32,16,256]{2,1,0:T(8,128)(2,1)}), bf16[32,16,256]{2,1,0:T(8,128)(2,1)S(1)}, u32[]{:S(2)}, u32[]{:S(2)}) async-start(bf16[32,16,256]{2,1,0:T(8,128)(2,1)} %shard_map.98), calls=%async_computation | async-start | bytes 524288 | tf_op jit(solution)/shard_map/all_to_all | solution.py:321
  15.3 19.4 %collective-permute-start.9 = (bf16[224,1024]{1,0:T(8,128)(2,1)S(1)}, bf16[224,1024]{1,0:T(8,128)(2,1)S(1)}, u32[]{:S(2)}, u32[]{:S(2)}) collective-permute-start(bf16[224,1024]{1,0:T(8,128)(2,1)S(1)} %bitcast.8), channel_id=1, source_target_pairs={{0,32},{32,0},{64,96},{96,64},{1,33},{33,1},{65,97},{97,65},{2,34}... | collective-permute-start | bytes 1376264 | tf_op jit(solution)/shard_map/ppermute | solution.py:306
  18.9 9.1 %collective-permute-start.4 = (f32[8,1024]{1,0:T(8,128)S(1)}, f32[8,1024]{1,0:T(8,128)S(1)}, u32[]{:S(2)}, u32[]{:S(2)}) collective-permute-start(f32[8,1024]{1,0:T(8,128)S(1)} %shard_map.97._.p0), channel_id=1, source_target_pairs={{0,32},{32,0},{64,96},{96,64},{1,33},{33,1},{65,97},{97,65},{2,34}... | collective-permute-start | bytes 98312 | tf_op jit(solution)/shard_map/ppermute | solution.py:306
  19.2 8.8 %collective-permute-start.5 = (f32[8,1024]{1,0:T(8,128)S(1)}, f32[8,1024]{1,0:T(8,128)S(1)}, u32[]{:S(2)}, u32[]{:S(2)}) collective-permute-start(f32[8,1024]{1,0:T(8,128)S(1)} %shard_map.97._.p0), channel_id=1, source_target_pairs={{0,64},{32,96},{64,0},{96,32},{1,65},{33,97},{65,1},{97,33},{2,66}... | collective-permute-start | bytes 98312 | tf_op jit(solution)/shard_map/ppermute | solution.py:306
  22.9 5.3 %collective-permute-start.6 = (f32[8,1024]{1,0:T(8,128)S(1)}, f32[8,1024]{1,0:T(8,128)S(1)}, u32[]{:S(2)}, u32[]{:S(2)}) collective-permute-start(f32[8,1024]{1,0:T(8,128)S(1)} %shard_map.97._.p0), channel_id=1, source_target_pairs={{0,96},{32,64},{64,32},{96,0},{1,97},{33,65},{65,33},{97,1},{2,98}... | collective-permute-start | bytes 98312 | tf_op jit(solution)/shard_map/ppermute | solution.py:306
  28.2 7.1 %collective-permute-start.8 = (bf16[128,1024]{1,0:T(8,128)(2,1)S(1)}, bf16[128,1024]{1,0:T(8,128)(2,1)S(1)}, u32[]{:S(2)}, u32[]{:S(2)}) collective-permute-start(bf16[128,1024]{1,0:T(8,128)(2,1)S(1)} %shard_map.101), channel_id=1, source_target_pairs={{0,32},{32,0},{64,96},{96,64},{1,33},{33,1},{65,97},{97,65},{2,34}... | collective-permute-start | bytes 786440 | tf_op jit(solution)/shard_map/ppermute | solution.py:306
  33.9 23.7 %copy-start = (f32[112,64]{0,1:T(8,128)S(1)}, f32[112,64]{0,1:T(8,128)}, u32[]{:S(2)}) copy-start(f32[112,64]{0,1:T(8,128)} %param.10) | copy-start | bytes 86020
  33.9 1.4 %collective-permute-start.7 = (f32[16,1024]{1,0:T(8,128)S(1)}, f32[16,1024]{1,0:T(8,128)S(1)}, u32[]{:S(2)}, u32[]{:S(2)}) collective-permute-start(f32[16,1024]{1,0:T(8,128)S(1)} %get-tuple-element.34.adj), channel_id=1, source_target_pairs={{0,32},{32,0},{64,96},{96,64},{1,33},{33,1},{65,97},{97,65},{2,34}... | collective-permute-start | bytes 196616 | tf_op jit(solution)/shard_map/ppermute | solution.py:306

commit v10 on v8

--- a/solution.py
+++ b/solution.py
@@ -89,17 +89,18 @@
     return pl.ds(pl.multiple_of((core + 2 * side) * 128, 128), 128)
 
 
-def split_body(mem, eig, innovation, obs_weight, m_mine, m_mate, e_mine, e_mate, iv, sem):
-    copies = halves_copies(mem, m_mine, m_mate, sem, 0) + halves_copies(eig, e_mine, e_mate, sem, 2) + [
+def split_body(mem, eig, m_mine, m_mate, e_mine, e_mate, sem):
+    wait_all(start_all(halves_copies(mem, m_mine, m_mate, sem, 0) + halves_copies(eig, e_mine, e_mate, sem, 2)))
+
+
+def load_body(innovation, obs_weight, _, payload, iv, sem):
+    copies = start_all([
         pltpu.make_async_copy(
-            a.at[0, :, quarter_at(side)], iv.at[n, :, side * 128:(side + 1) * 128], sem.at[4 + 2 * n + side])
+            a.at[0, :, quarter_at(side)], iv.at[n, :, side * 128:(side + 1) * 128], sem.at[2 * n + side])
         for n, a in enumerate((innovation, obs_weight)) for side in range(2)
-    ]
-    wait_all(start_all(copies))
-
-
-def load_body(iv, _, payload):
+    ])
     for n in range(2):
+        wait_all(copies[2 * n:2 * n + 2])
         payload[:, n * 8:(n + 1) * 8, :] = iv[n].reshape(32, 8, 256).astype(BF)
 
 
@@ -227,19 +228,27 @@
         image.append(acc)
     image = jnp.concatenate(image, axis=0)
     image_out[...] = image
-    depb[...] = (weight[...] * (innov[...] - image)).astype(BF)
+    dep = weight[...] * (innov[...] - image)
+    depb[...] = dep.astype(BF)
+    dep_t = dep.T.astype(BF)
+    column = iota((256, 64), 1)
+    odd = jnp.zeros((256, 64), F32)
     for b in range(4):
         lhs = depb[b * 16:(b + 1) * 16, :]
         acc = jnp.zeros((16, 256), F32)
         for i in range(16):
-            acc = jnp.where(rows == i, dot(lhs, block(b * 16 + i), NT), acc)
+            j = b * 16 + i
+            if j % 2:
+                odd = jnp.where(column == j, dot(block(j), dep_t), odd)
+            else:
+                acc = jnp.where(rows == i, dot(lhs, block(j), NT), acc)
         spread[b * 16:(b + 1) * 16, :] = acc
     x = spread[...]
-    hi = x.astype(BF)
-    lo = (x - hi.astype(F32)).astype(BF)
+    hi, lo, _ = parts3(x)
+    odd_hi, odd_lo, _ = parts3(odd)
     terms = []
-    for part in (hi, lo):
-        turned = dot(swap, part, NT)
+    for part, odd_part in ((hi, odd_hi), (lo, odd_lo)):
+        turned = dot(swap, part, NT) + dot(swap, odd_part)
         terms.append(jnp.concatenate([turned[c * 16:(c + 1) * 16] for c in range(16)], axis=1))
     both = dot(jnp.concatenate(terms, axis=0).astype(BF), onehot[...])
     adj = both[:16] + both[16:]
@@ -310,18 +319,18 @@
         return lax.ppermute(x, "band", [(i, i ^ bit) for i in range(4)])
 
     dma = pltpu.SemaphoreType.DMA
-    m_my, m_mt, e_my, e_mt, iv = call(
-        split_body, [HB] * 4,
-        [(pltpu.VMEM((16, 8, 1024), BF), VM)] * 2 + [(pltpu.VMEM((28, 8, 1024), BF), VM)] * 2
-        + [(pltpu.VMEM((2, 256, 256), F32), VM)], 0, 0, [dma((8,))],
-    )(in_hbm(members), in_hbm(eigvecs), in_hbm(innovation), in_hbm(obs_weight))
+    m_my, m_mt, e_my, e_mt = call(
+        split_body, [HB] * 2,
+        [(pltpu.VMEM((16, 8, 1024), BF), VM)] * 2 + [(pltpu.VMEM((28, 8, 1024), BF), VM)] * 2, 0, 0, [dma((4,))],
+    )(in_hbm(members), in_hbm(eigvecs))
     m_my, m_mt, e0, e_mt = [in_vmem(a.reshape(-1, 1024)) for a in (m_my, m_mt, e_my, e_mt)]
     m3 = over(m_mt, 3)
     m2 = over(m_my, 2)
     m1 = over(m_mt, 1)
     (payload,) = call(
-        load_body, [VM, ANY], [(pltpu.VMEM((32, 16, 256), BF), VM)], 0, 0,
-    )(in_vmem(iv), m_my)
+        load_body, [HB] * 2 + [ANY], [(pltpu.HBM((32, 16, 256), BF), VM)],
+        0, 0, [pltpu.VMEM((2, 256, 256), F32), dma((4,))],
+    )(in_hbm(innovation), in_hbm(obs_weight), m_my)
     got = lax.all_to_all(payload, "mem", split_axis=0, concat_axis=0, tiled=True)
     e1 = over(e_mt, 1)
     m1, m2, m3, e1 = [in_vmem(a) for a in (m1, m2, m3, e1)]

time: 58.6 us -> 57.5 us (0.981)
  blocking collectives: 20.2 us -> 18.3 us
  starting transfers between devices: 16.4 us -> 17.1 us
  Pallas kernels: 14.2 us -> 14.9 us
  waiting for transfers between devices: 6.8 us -> 6.11 us
    all_to_all x1, blocking collectives: 20.2 us -> 18.3 us  [per_device(): lax.all_to_all(sent, ('band', 'mem'), split_axis=0, concat_axis=0, axis_i...]
    ppermute x9, waiting for transfers between devices: 3.13 us -> 1.9 us  [over(): return lax.ppermute(x, 'band', [(i, i ^ bit) for i in range(4)])]
    pallas_call x2, Pallas kernels: 2.27 us -> 3.2 us  [the longest x1 1.84 us: per_device(): call(load_body, [HB] * 2 + [ANY], [(pltpu.HBM((32, 16, 256), BF), VM)], 0...]
    ppermute x9, starting transfers between devices: 8.59 us -> 9.29 us  [over(): return lax.ppermute(x, 'band', [(i, i ^ bit) for i in range(4)])]
  transfers between devices with their start and end apart: 10 -> 10, of which waited for: 4 -> 4; matrix products, arithmetic and copies ran while one was open for 0% -> 0% of each run, Pallas kernels for 19% -> 21%
where the time goes in v10:
time: 57.5 us; the launch traced here: 57.1 us
  blocking collectives  18.3 us (32%)
  starting transfers between devices  17.1 us (30%)
  Pallas kernels  14.9 us (26%)
  waiting for transfers between devices  6.11 us (11%)
  between operations  0.76 us (1%)
    all_to_all x1, blocking collectives, per_device(): lax.all_to_all(sent, ('band', 'mem'), split_axis=0, concat_axis=0, axis_i...  18.3 us
    ppermute x9, starting transfers between devices, over(): return lax.ppermute(x, 'band', [(i, i ^ bit) for i in range(4)])  9.29 us
    all_to_all x1, starting transfers between devices, per_device(): lax.all_to_all(payload, 'mem', split_axis=0, concat_axis=0, tiled=True)  7.8 us
    pallas_call x1, Pallas kernels, per_device(): call(obs_body, [VM] * 7 + [HB], [(shape((16, 1024), F32), VM), (pltpu.VME...  5.3 us
    all_to_all x1, waiting for transfers between devices, per_device(): lax.all_to_all(payload, 'mem', split_axis=0, concat_axis=0, tiled=True)  4.21 us
    pallas_call x1, Pallas kernels, per_device(): call(prep_body, [HB] * 3 + [ANY] + [HB] * 2 + [ANY], [(pltpu.VMEM(d, t),...  2.48 us
    ppermute x9, waiting for transfers between devices, over(): return lax.ppermute(x, 'band', [(i, i ^ bit) for i in range(4)])  1.9 us
    pallas_call x1, Pallas kernels, per_device(): call(load_body, [HB] * 2 + [ANY], [(pltpu.HBM((32, 16, 256), BF), VM)], 0...  1.84 us
  transfers between devices with their start and end apart: 10, of which 4 were waited for; matrix products, arithmetic and copies ran while one was open for 0% of the time, Pallas kernels for 21%

profile of v10, /device:TPU:0, one launch (start us, length us, event | category | flops | bytes accessed | tf_op | source)
XLA Modules:
  0.0 57.1 jit_solution(11459230795489897316)
XLA Ops:
  0.6 1.4 %shard_map.95 = (bf16[16,8,1024]{2,1,0:T(8,128)(2,1)S(1)}, bf16[16,8,1024]{2,1,0:T(8,128)(2,1)S(1)}, bf16[28,8,1024]{2,1,0:T(8,128)(2,1)S(1)}, bf16[28,8,1024]{2,1,0:T(8,128)(2,1)S(1)}) custom-call(bf16[16,16,1024]{2,1,0:T(8,128)(2,1)} %mem.1, bf16[28,16,1024]{2,1,0:T(8,128)(2,1)} %eig.1), custom_call_target="tpu_custom_call" | custom-call | tf_op jit(solution)/shard_map/pallas_call | solution.py:322
  2.0 0.1 collective-permute-start.1
  2.1 0.5 collective-permute-start
  2.6 4.0 %collective-permute-start.2 = (bf16[128,1024]{1,0:T(8,128)(2,1)S(1)}, bf16[128,1024]{1,0:T(8,128)(2,1)S(1)}, u32[]{:S(2)}, u32[]{:S(2)}) collective-permute-start(bf16[128,1024]{1,0:T(8,128)(2,1)S(1)} %bitcast.12), channel_id=1, source_target_pairs={{0,64},{32,96},{64,0},{96,32},{1,65},{33,97},{65,1},{97,33},{2,66}... | collective-permute-start | bytes 786440 | tf_op jit(solution)/shard_map/ppermute | solution.py:319
  6.6 1.8 %shard_map.98 = bf16[32,16,256]{2,1,0:T(8,128)(2,1)} custom-call(f32[1,256,512]{2,1,0:T(8,128)} %innovation.3, f32[1,256,512]{2,1,0:T(8,128)} %obs_weight.3, bf16[128,1024]{1,0:T(8,128)(2,1)S(1)} %bitcast.13), custom_call_target="tpu_custom_call" | custom-call | tf_op jit(solution)/shard_map/pallas_call | solution.py:330
  8.4 7.8 %all-to-all-start = ((bf16[32,16,256]{2,1,0:T(8,128)(2,1)}), bf16[32,16,256]{2,1,0:T(8,128)(2,1)S(1)}, u32[]{:S(2)}, u32[]{:S(2)}) async-start(bf16[32,16,256]{2,1,0:T(8,128)(2,1)} %shard_map.98), calls=%async_computation | async-start | bytes 524288 | tf_op jit(solution)/shard_map/all_to_all | solution.py:334
  16.2 0.5 collective-permute-start.8
  16.7 1.4 %shard_map.96 = (f32[8,1024]{1,0:T(8,128)S(1)}, bf16[448,256]{1,0:T(8,128)(2,1)S(1)}) custom-call(f32[64,112]{1,0:T(8,128)} %bitcast.21, bf16[128,1024]{1,0:T(8,128)(2,1)S(1)} %bitcast.14, bf16[128,1024]{1,0:T(8,128)(2,1)S(1)} %collective-permute-done.refs_2_, bf16[224,1024]{1,0:T(8,128)(2,1)S(1)} %bitcast.9, ...), custom_call_target="tpu_custom_call" | custom-call | flops 250000000 | bytes 2000000 | tf_op jit(solution)/shard_map/pallas_call | solution.py:338
  18.1 0.1 collective-permute-done.3.refs_3_.x
  18.2 0.4 shard_map.97._.a
  18.6 3.6 %collective-permute-start.4 = (f32[8,1024]{1,0:T(8,128)S(1)}, f32[8,1024]{1,0:T(8,128)S(1)}, u32[]{:S(2)}, u32[]{:S(2)}) collective-permute-start(f32[8,1024]{1,0:T(8,128)S(1)} %shard_map.97._.a), channel_id=1, source_target_pairs={{0,64},{32,96},{64,0},{96,32},{1,65},{33,97},{65,1},{97,33},{2,66}... | collective-permute-start | bytes 98312 | tf_op jit(solution)/shard_map/ppermute | solution.py:319
  22.2 4.2 %all-to-all-done.got_in = bf16[32,16,256]{2,1,0:T(8,128)(2,1)S(1)} async-done(((bf16[32,16,256]{2,1,0:T(8,128)(2,1)}), bf16[32,16,256]{2,1,0:T(8,128)(2,1)S(1)}, u32[]{:S(2)}, u32[]{:S(2)}) %all-to-all-start) | async-done | bytes 262176 | tf_op jit(solution)/shard_map/all_to_all | solution.py:334
  26.4 2.5 %shard_map.99 = (bf16[1024,1024]{1,0:T(8,128)(2,1)S(1)}, bf16[1024,1024]{1,0:T(8,128)(2,1)S(1)}, bf16[64,256]{1,0:T(8,128)(2,1)S(1)}, bf16[64,256]{1,0:T(8,128)(...) custom-call(s32[16,64]{1,0:T(8,128)} %bitcast.23, ...), custom_call_target="tpu_custom_call" | custom-call | flops 100000000 | bytes 12000000 | tf_op jit(solution)/shard_map/pallas_call | solution.py:348
  29.0 0.1 collective-permute-start.5
  29.0 1.2 %collective-permute-done.5.inc_mt._ = bf16[8,1024]{1,0:T(8,128)(2,1)S(1)} collective-permute-done((bf16[8,1024]{1,0:T(8,128)(2,1)S(1)}, bf16[8,1024]{1,0:T(8,128)(2,1)S(1)}, u32[]{:S(2)}, u32[]{:S(2)}) %collective-permute-start.5) | collective-permute-done | bytes 16416 | tf_op jit(solution)/shard_map/ppermute | solution.py:319
  30.2 0.2 collective-permute-start.7
  30.4 5.3 %shard_map.101 = (f32[16,1024]{1,0:T(8,128)S(1)}, f32[64,256]{1,0:T(8,128)S(1)}) custom-call(bf16[8,1024]{1,0:T(8,128)(2,1)S(1)} %shard_map.100.inc_my, bf16[8,1024]{1,0:T(8,128)(2,1)S(1)} %collective-permute-done.5.inc_mt._, bf16[1024,1024]{1,0:T(8,128)(2,1)S(1)} %get-tuple-element.28.onehot, bf16[1024,1024]{1,0:T(8,128)(2,1)S(1)} %get-tuple-element.29.onehot_t, ...), custom_call_target="tpu_custom_call" | custom-call | flops 1000000000 | bytes 12000000 | tf_op jit(solution)/shard_map/pallas_call | solution.py:366
  35.7 0.4 collective-permute-start.6
  36.1 0.2 shard_map.104.slots
  36.4 0.6 %collective-permute-done.6.came = f32[16,1024]{1,0:T(8,128)S(1)} collective-permute-done((f32[16,1024]{1,0:T(8,128)S(1)}, f32[16,1024]{1,0:T(8,128)S(1)}, u32[]{:S(2)}, u32[]{:S(2)}) %collective-permute-start.6) | collective-permute-done | bytes 65568 | tf_op jit(solution)/shard_map/ppermute | solution.py:319
  37.0 0.9 %shard_map.103.mine = f32[32,56]{1,0:T(8,128)S(1)} custom-call(f32[16,1024]{1,0:T(8,128)S(1)} %get-tuple-element.33.adj, f32[16,1024]{1,0:T(8,128)S(1)} %collective-permute-done.6.came, bf16[128,1024]{1,0:T(8,128)(2,1)S(1)} %bitcast.15, bf16[128,1024]{1,0:T(8,128)(2,1)S(1)} %bitcast.20, bf16[128,1024]{1,0:T(8,128)(2,1)S(1)} %collective-permute-done.2.refs_2_.o_my, ...), custom_call_target="tpu_custom_call" | custom-call | flops 500000000 | bytes 2000000 | tf_op jit(solution)/shard_map/pallas_call | solution.py:379
  37.9 0.1 shard_map.105
  38.1 18.3 %all_to_all.10.refs_0_ = bf16[64,16,128]{2,1,0:T(8,128)(2,1)S(1)} all-to-all(bf16[64,16,128]{2,1,0:T(8,128)(2,1)S(1)} %shard_map.105), channel_id=1, replica_groups={{0,1,2,3,4,5,6,7,8,9,10,11,12,13,14,15,16,17,18,19,20,21,22,23,24,25,26..., dimensions={0} | all-to-all | bytes 524288 | tf_op jit(solution)/shard_map/all_to_all | solution.py:387
  56.3 0.8 %shard_map.106 = (f32[16,112]{1,0:T(8,128)}, f32[1,256,128]{2,1,0:T(8,128)}) custom-call(bf16[64,16,128]{2,1,0:T(8,128)(2,1)S(1)} %all_to_all.10.refs_0_, f32[64,112]{1,0:T(8,128)S(1)} %bitcast.22, f32[256,128]{1,0:T(8,128)S(1)} %get-tuple-element.36.refs_2_, f32[256,128]{1,0:T(8,128)S(1)} %get-tuple-element.37.refs_3_), custom_call_target="tpu_custom_call" | custom-call | flops 1000000 | bytes 600000 | tf_op jit(solution)/shard_map/pallas_call | solution.py:389
  (11 shorter events, 0.0 us)
Async XLA Ops:
  2.0 14.7 %collective-permute-start.1 = (bf16[224,1024]{1,0:T(8,128)(2,1)S(1)}, bf16[224,1024]{1,0:T(8,128)(2,1)S(1)}, u32[]{:S(2)}, u32[]{:S(2)}) collective-permute-start(bf16[224,1024]{1,0:T(8,128)(2,1)S(1)} %bitcast.16), channel_id=1, source_target_pairs={{0,32},{32,0},{64,96},{96,64},{1,33},{33,1},{65,97},{97,65},{2,34}... | collective-permute-start | bytes 1376264 | tf_op jit(solution)/shard_map/ppermute | solution.py:319
  2.1 14.6 %collective-permute-start = (bf16[128,1024]{1,0:T(8,128)(2,1)S(1)}, bf16[128,1024]{1,0:T(8,128)(2,1)S(1)}, u32[]{:S(2)}, u32[]{:S(2)}) collective-permute-start(bf16[128,1024]{1,0:T(8,128)(2,1)S(1)} %bitcast.18), channel_id=1, source_target_pairs={{0,32},{32,0},{64,96},{96,64},{1,33},{33,1},{65,97},{97,65},{2,34}... | collective-permute-start | bytes 786440 | tf_op jit(solution)/shard_map/ppermute | solution.py:319
  2.6 15.5 %collective-permute-start.2 = (bf16[128,1024]{1,0:T(8,128)(2,1)S(1)}, bf16[128,1024]{1,0:T(8,128)(2,1)S(1)}, u32[]{:S(2)}, u32[]{:S(2)}) collective-permute-start(bf16[128,1024]{1,0:T(8,128)(2,1)S(1)} %bitcast.12), channel_id=1, source_target_pairs={{0,64},{32,96},{64,0},{96,32},{1,65},{33,97},{65,1},{97,33},{2,66}... | collective-permute-start | bytes 786440 | tf_op jit(solution)/shard_map/ppermute | solution.py:319
  6.6 11.6 %collective-permute-start.3 = (bf16[128,1024]{1,0:T(8,128)(2,1)S(1)}, bf16[128,1024]{1,0:T(8,128)(2,1)S(1)}, u32[]{:S(2)}, u32[]{:S(2)}) collective-permute-start(bf16[128,1024]{1,0:T(8,128)(2,1)S(1)} %bitcast.19), channel_id=1, source_target_pairs={{0,96},{32,64},{64,32},{96,0},{1,97},{33,65},{65,33},{97,1},{2,98}... | collective-permute-start | bytes 786440 | tf_op jit(solution)/shard_map/ppermute | solution.py:319
  8.4 18.0 %all-to-all-start = ((bf16[32,16,256]{2,1,0:T(8,128)(2,1)}), bf16[32,16,256]{2,1,0:T(8,128)(2,1)S(1)}, u32[]{:S(2)}, u32[]{:S(2)}) async-start(bf16[32,16,256]{2,1,0:T(8,128)(2,1)} %shard_map.98), calls=%async_computation | async-start | bytes 524288 | tf_op jit(solution)/shard_map/all_to_all | solution.py:334
  16.2 20.2 %collective-permute-start.8 = (bf16[224,1024]{1,0:T(8,128)(2,1)S(1)}, bf16[224,1024]{1,0:T(8,128)(2,1)S(1)}, u32[]{:S(2)}, u32[]{:S(2)}) collective-permute-start(bf16[224,1024]{1,0:T(8,128)(2,1)S(1)} %bitcast.8), channel_id=1, source_target_pairs={{0,32},{32,0},{64,96},{96,64},{1,33},{33,1},{65,97},{97,65},{2,34}... | collective-permute-start | bytes 1376264 | tf_op jit(solution)/shard_map/ppermute | solution.py:319
  18.6 10.3 %collective-permute-start.4 = (f32[8,1024]{1,0:T(8,128)S(1)}, f32[8,1024]{1,0:T(8,128)S(1)}, u32[]{:S(2)}, u32[]{:S(2)}) collective-permute-start(f32[8,1024]{1,0:T(8,128)S(1)} %shard_map.97._.a), channel_id=1, source_target_pairs={{0,64},{32,96},{64,0},{96,32},{1,65},{33,97},{65,1},{97,33},{2,66}... | collective-permute-start | bytes 98312 | tf_op jit(solution)/shard_map/ppermute | solution.py:319
  29.0 1.3 %collective-permute-start.5 = (bf16[8,1024]{1,0:T(8,128)(2,1)S(1)}, bf16[8,1024]{1,0:T(8,128)(2,1)S(1)}, u32[]{:S(2)}, u32[]{:S(2)}) collective-permute-start(bf16[8,1024]{1,0:T(8,128)(2,1)S(1)} %shard_map.100.inc_my), channel_id=1, source_target_pairs={{0,32},{32,0},{64,96},{96,64},{1,33},{33,1},{65,97},{97,65},{2,34}... | collective-permute-start | bytes 49160 | tf_op jit(solution)/shard_map/ppermute | solution.py:319
  30.2 6.8 %collective-permute-start.7 = (bf16[128,1024]{1,0:T(8,128)(2,1)S(1)}, bf16[128,1024]{1,0:T(8,128)(2,1)S(1)}, u32[]{:S(2)}, u32[]{:S(2)}) collective-permute-start(bf16[128,1024]{1,0:T(8,128)(2,1)S(1)} %shard_map.102), channel_id=1, source_target_pairs={{0,32},{32,0},{64,96},{96,64},{1,33},{33,1},{65,97},{97,65},{2,34}... | collective-permute-start | bytes 786440 | tf_op jit(solution)/shard_map/ppermute | solution.py:319
  35.7 20.7 %copy-start = (f32[112,64]{0,1:T(8,128)S(1)}, f32[112,64]{0,1:T(8,128)}, u32[]{:S(2)}) copy-start(f32[112,64]{0,1:T(8,128)} %param.10) | copy-start | bytes 86020
  35.7 1.3 %collective-permute-start.6 = (f32[16,1024]{1,0:T(8,128)S(1)}, f32[16,1024]{1,0:T(8,128)S(1)}, u32[]{:S(2)}, u32[]{:S(2)}) collective-permute-start(f32[16,1024]{1,0:T(8,128)S(1)} %get-tuple-element.33.adj), channel_id=1, source_target_pairs={{0,32},{32,0},{64,96},{96,64},{1,33},{33,1},{65,97},{97,65},{2,34}... | collective-permute-start | bytes 196616 | tf_op jit(solution)/shard_map/ppermute | solution.py:319

commit v11 on v10

--- a/solution.py
+++ b/solution.py
@@ -111,9 +111,11 @@
     return scale * total
 
 
-def increment_own(scale, control_t, ma, mb, ea, eb, out, kron, ct, sem):
-    get = pltpu.make_async_copy(control_t, ct, sem)
-    get.start()
+def increment_own(scale, control_t, columns_t, owners, ma, mb, ea, eb, out, kron, columns_out, owners_out, ct, sem):
+    get, *small = start_all([
+        pltpu.make_async_copy(a, b, sem.at[n])
+        for n, (a, b) in enumerate(((control_t, ct), (columns_t, columns_out), (owners, owners_out)))
+    ])
     band = lax.axis_index("band")
     row = iota((448, 112), 0)
     second = (row >= 224).astype(jnp.int32)
@@ -130,6 +132,7 @@
     for g in range(0, 1024, 256):
         cut = slice(g, g + 256)
         out[:, cut] = increment_of(scale, full[:, :256], ma, mb, ea, eb, cut)
+    wait_all(small)
 
 
 def increment_other(scale, kron, before, ma, mb, ea, eb, out):
@@ -138,17 +141,14 @@
         out[:, cut] = before[:, cut] + increment_of(scale, kron[...], ma, mb, ea, eb, cut)
 
 
-def prep_body(columns_t, owners_in, interpolation, got_in, innovation, obs_weight, _,
-              onehot, onehot_t, place_hi, place_lo, interp, innov, weight, innov_own, live_own,
-              cols_s, own_s, got, sem):
+def prep_body(cols_s, own_s, interpolation, got, innovation, obs_weight, _,
+              onehot, onehot_t, place_hi, place_lo, interp, innov, weight, innov_own, live_own, sem):
     band = lax.axis_index("band")
     tile = lax.axis_index("mem")
     quarter = pl.ds(pl.multiple_of(band * 128, 128), 128)
-    small = [(columns_t, cols_s), (owners_in, own_s), (got_in, got)]
     mid = [(innovation.at[0, :, quarter], innov_own), (obs_weight.at[0, :, quarter], live_own)]
     big = [(interpolation.at[:32, :, quarter_at(side)], interp.at[:, :, side * 128:(side + 1) * 128]) for side in range(2)]
-    copies = start_all([pltpu.make_async_copy(a, b, sem.at[n]) for n, (a, b) in enumerate(small + mid + big)])
-    wait_all(copies[:3])
+    copies = start_all([pltpu.make_async_copy(a, b, sem.at[n]) for n, (a, b) in enumerate(mid + big)])
     t = iota((64, 1024), 1)
     cols = cols_s[...].astype(F32).T.astype(jnp.int32)
     for c in range(16):
@@ -177,9 +177,9 @@
     side = jnp.where((iota((256, 128), 1) >> 6) == odd, dot(pair, hit), 0.0)
     count = jnp.sum(side, axis=1, keepdims=True)
     live = jnp.where((iota((256, 1), 0) & 7).astype(F32) < count, 1.0, 0.0)
-    wait_all(copies[3:5])
+    wait_all(copies[:2])
     live_own[...] = live * live_own[...]
-    wait_all(copies[5:])
+    wait_all(copies[2:])
 
 
 def add_body(a, b, _, out):
@@ -335,11 +335,12 @@
     e1 = over(e_mt, 1)
     m1, m2, m3, e1 = [in_vmem(a) for a in (m1, m2, m3, e1)]
 
-    part, kron = call(
-        lambda *refs: increment_own(scale, *refs), [HB] + [VM] * 4,
-        [(pltpu.VMEM((8, 1024), F32), VM), (pltpu.VMEM((448, 256), BF), VM)],
-        25 * 10 ** 7, 2 * 10 ** 6, [pltpu.VMEM((64, 112), F32), dma(())],
-    )(in_hbm(control.T), m_my, m1, e0, e1)
+    part, kron, columns_v, owners_v = call(
+        lambda *refs: increment_own(scale, *refs), [HB] * 3 + [VM] * 4,
+        [(pltpu.VMEM((8, 1024), F32), VM), (pltpu.VMEM((448, 256), BF), VM),
+         (pltpu.VMEM((16, 64), jnp.int32), VM), (pltpu.VMEM((16, 128), jnp.int32), VM)],
+        25 * 10 ** 7, 2 * 10 ** 6, [pltpu.VMEM((64, 112), F32), dma((3,))],
+    )(in_hbm(control.T), in_hbm(columns.T), in_hbm(owners), m_my, m1, e0, e1)
     (part,) = call(
         lambda *refs: increment_other(scale, *refs), [VM] * 6, [(shape((8, 1024), F32), VM)],
         25 * 10 ** 7, 2 * 10 ** 6,
@@ -347,13 +348,13 @@
 
     kept = call(
         prep_body,
-        [HB] * 3 + [ANY] + [HB] * 2 + [ANY],
+        [VM, VM, HB, VM, HB, HB, ANY],
         [(pltpu.VMEM(d, t), VM) for d, t in (
             ((1024, 1024), BF), ((1024, 1024), BF), ((64, 256), BF), ((64, 256), BF), ((32, 256, 256), BF), ((64, 256), F32), ((64, 256), F32),
             ((256, 128), F32), ((256, 128), F32))],
         10 ** 8, 12 * 10 ** 6,
-        [pltpu.VMEM((16, 64), jnp.int32), pltpu.VMEM((16, 128), jnp.int32), pltpu.VMEM((32, 16, 256), BF), dma((7,))],
-    )(in_hbm(columns.T), in_hbm(owners), in_hbm(interpolation), got, in_hbm(innovation), in_hbm(obs_weight), part)
+        [dma((4,))],
+    )(in_vmem(columns_v), in_vmem(owners_v), in_hbm(interpolation), in_vmem(got), in_hbm(innovation), in_hbm(obs_weight), part)
     onehot, onehot_t, place_hi, place_lo, interp, innov, weight, innov_own, live_own = [in_vmem(a) for a in kept]
 
     (inc_my,) = call(

time: 57.5 us -> 58.4 us (1.016)
  Pallas kernels: 14.9 us -> 16 us
    pallas_call x2, Pallas kernels: 3.92 us -> 5.1 us  [the longest x1 3.64 us: per_device(): call(prep_body, [VM, VM, HB, VM, HB, HB, ANY], [(pltpu.VMEM(d, t), VM) fo...]
  transfers between devices with their start and end apart: 10 -> 10, of which waited for: 4 -> 3; matrix products, arithmetic and copies ran while one was open for 0% -> 0% of each run, Pallas kernels for 21% -> 22%
where the time goes in v11:
time: 58.4 us; the launch traced here: 58 us
  blocking collectives  18 us (31%)
  starting transfers between devices  17.1 us (29%)
  Pallas kernels  16 us (27%)
  waiting for transfers between devices  6.06 us (10%)
  between operations  0.76 us (1%)
    all_to_all x1, blocking collectives, per_device(): lax.all_to_all(sent, ('band', 'mem'), split_axis=0, concat_axis=0, axis_i...  18 us
    ppermute x9, starting transfers between devices, over(): return lax.ppermute(x, 'band', [(i, i ^ bit) for i in range(4)])  9.32 us
    all_to_all x1, starting transfers between devices, per_device(): lax.all_to_all(payload, 'mem', split_axis=0, concat_axis=0, tiled=True)  7.8 us
    pallas_call x1, Pallas kernels, per_device(): call(obs_body, [VM] * 7 + [HB], [(shape((16, 1024), F32), VM), (pltpu.VME...  5.29 us
    all_to_all x1, waiting for transfers between devices, per_device(): lax.all_to_all(payload, 'mem', split_axis=0, concat_axis=0, tiled=True)  4.19 us
    pallas_call x1, Pallas kernels, per_device(): call(prep_body, [VM, VM, HB, VM, HB, HB, ANY], [(pltpu.VMEM(d, t), VM) fo...  3.64 us
    ppermute x9, waiting for transfers between devices, over(): return lax.ppermute(x, 'band', [(i, i ^ bit) for i in range(4)])  1.87 us
    pallas_call x1, Pallas kernels, per_device(): call(load_body, [HB] * 2 + [ANY], [(pltpu.HBM((32, 16, 256), BF), VM)], 0...  1.84 us
  transfers between devices with their start and end apart: 10, of which 3 were waited for; matrix products, arithmetic and copies ran while one was open for 0% of the time, Pallas kernels for 22%

profile of v11, /device:TPU:0, one launch (start us, length us, event | category | flops | bytes accessed | tf_op | source)
XLA Modules:
  0.0 58.0 jit_solution(4629532427888792785)
XLA Ops:
  0.6 1.4 %shard_map.95 = (bf16[16,8,1024]{2,1,0:T(8,128)(2,1)S(1)}, bf16[16,8,1024]{2,1,0:T(8,128)(2,1)S(1)}, bf16[28,8,1024]{2,1,0:T(8,128)(2,1)S(1)}, bf16[28,8,1024]{2,1,0:T(8,128)(2,1)S(1)}) custom-call(bf16[16,16,1024]{2,1,0:T(8,128)(2,1)} %mem.1, bf16[28,16,1024]{2,1,0:T(8,128)(2,1)} %eig.1), custom_call_target="tpu_custom_call" | custom-call | tf_op jit(solution)/shard_map/pallas_call | solution.py:322
  2.0 0.1 collective-permute-start.1
  2.1 0.5 collective-permute-start
  2.6 4.0 %collective-permute-start.2 = (bf16[128,1024]{1,0:T(8,128)(2,1)S(1)}, bf16[128,1024]{1,0:T(8,128)(2,1)S(1)}, u32[]{:S(2)}, u32[]{:S(2)}) collective-permute-start(bf16[128,1024]{1,0:T(8,128)(2,1)S(1)} %bitcast.12), channel_id=1, source_target_pairs={{0,64},{32,96},{64,0},{96,32},{1,65},{33,97},{65,1},{97,33},{2,66}... | collective-permute-start | bytes 786440 | tf_op jit(solution)/shard_map/ppermute | solution.py:319
  6.6 1.8 %shard_map.98 = bf16[32,16,256]{2,1,0:T(8,128)(2,1)} custom-call(f32[1,256,512]{2,1,0:T(8,128)} %innovation.3, f32[1,256,512]{2,1,0:T(8,128)} %obs_weight.3, bf16[128,1024]{1,0:T(8,128)(2,1)S(1)} %bitcast.13), custom_call_target="tpu_custom_call" | custom-call | tf_op jit(solution)/shard_map/pallas_call | solution.py:330
  8.4 7.8 %all-to-all-start = ((bf16[32,16,256]{2,1,0:T(8,128)(2,1)}), bf16[32,16,256]{2,1,0:T(8,128)(2,1)S(1)}, u32[]{:S(2)}, u32[]{:S(2)}) async-start(bf16[32,16,256]{2,1,0:T(8,128)(2,1)} %shard_map.98), calls=%async_computation | async-start | bytes 524288 | tf_op jit(solution)/shard_map/all_to_all | solution.py:334
  16.2 0.5 collective-permute-start.8
  16.7 1.5 %shard_map.96 = (f32[8,1024]{1,0:T(8,128)S(1)}, bf16[448,256]{1,0:T(8,128)(2,1)S(1)}, s32[16,64]{1,0:T(8,128)S(1)}, s32[16,128]{1,0:T(8,128)S(1)}) custom-call(f32[64,112]{1,0:T(8,128)} %bitcast.21, s32[16,64]{1,0:T(8,128)} %bitcast.23, s32[16,128]{1,0:T(8,128)} %bitcast.24, bf16[128,1024]{1,0:T(8,128)(2,1)S(1)} %bitcast.14, ...), custom_call_target="tpu_custom_call" | custom-call | flops 250000000 | bytes 2000000 | tf_op jit(solution)/shard_map/pallas_call | solution.py:338
  18.1 0.0 collective-permute-done.3.refs_3_.x
  18.2 0.4 shard_map.97._.a
  18.6 3.6 %collective-permute-start.4 = (f32[8,1024]{1,0:T(8,128)S(1)}, f32[8,1024]{1,0:T(8,128)S(1)}, u32[]{:S(2)}, u32[]{:S(2)}) collective-permute-start(f32[8,1024]{1,0:T(8,128)S(1)} %shard_map.97._.a), channel_id=1, source_target_pairs={{0,64},{32,96},{64,0},{96,32},{1,65},{33,97},{65,1},{97,33},{2,66}... | collective-permute-start | bytes 98312 | tf_op jit(solution)/shard_map/ppermute | solution.py:319
  22.2 4.2 %all-to-all-done.got = bf16[32,16,256]{2,1,0:T(8,128)(2,1)S(1)} async-done(((bf16[32,16,256]{2,1,0:T(8,128)(2,1)}), bf16[32,16,256]{2,1,0:T(8,128)(2,1)S(1)}, u32[]{:S(2)}, u32[]{:S(2)}) %all-to-all-start) | async-done | bytes 262176 | tf_op jit(solution)/shard_map/all_to_all | solution.py:334
  26.4 3.6 %shard_map.99 = (bf16[1024,1024]{1,0:T(8,128)(2,1)S(1)}, bf16[1024,1024]{1,0:T(8,128)(2,1)S(1)}, bf16[64,256]{1,0:T(8,128)(2,1)S(1)}, bf16[64,256]{1,0:T(8,128)(...) custom-call(s32[16,64]{1,0:T(8,128)S(1)} %get-tuple-element.29.cols_, ...), custom_call_target="tpu_custom_call" | custom-call | flops 100000000 | bytes 12000000 | tf_op jit(solution)/shard_map/pallas_call | solution.py:349
  30.1 0.1 collective-permute-start.5
  30.2 1.2 %collective-permute-done.5.inc_mt._ = bf16[8,1024]{1,0:T(8,128)(2,1)S(1)} collective-permute-done((bf16[8,1024]{1,0:T(8,128)(2,1)S(1)}, bf16[8,1024]{1,0:T(8,128)(2,1)S(1)}, u32[]{:S(2)}, u32[]{:S(2)}) %collective-permute-start.5) | collective-permute-done | bytes 16416 | tf_op jit(solution)/shard_map/ppermute | solution.py:319
  31.4 0.2 collective-permute-start.7
  31.5 5.3 %shard_map.101 = (f32[16,1024]{1,0:T(8,128)S(1)}, f32[64,256]{1,0:T(8,128)S(1)}) custom-call(bf16[8,1024]{1,0:T(8,128)(2,1)S(1)} %shard_map.100.inc_my, bf16[8,1024]{1,0:T(8,128)(2,1)S(1)} %collective-permute-done.5.inc_mt._, bf16[1024,1024]{1,0:T(8,128)(2,1)S(1)} %get-tuple-element.32.onehot, bf16[1024,1024]{1,0:T(8,128)(2,1)S(1)} %get-tuple-element.33.onehot_t, ...), custom_call_target="tpu_custom_call" | custom-call | flops 1000000000 | bytes 12000000 | tf_op jit(solution)/shard_map/pallas_call | solution.py:367
  36.9 0.4 collective-permute-start.6
  37.3 0.2 shard_map.104.slots
  37.6 0.6 %collective-permute-done.6.came = f32[16,1024]{1,0:T(8,128)S(1)} collective-permute-done((f32[16,1024]{1,0:T(8,128)S(1)}, f32[16,1024]{1,0:T(8,128)S(1)}, u32[]{:S(2)}, u32[]{:S(2)}) %collective-permute-start.6) | collective-permute-done | bytes 65568 | tf_op jit(solution)/shard_map/ppermute | solution.py:319
  38.2 0.9 %shard_map.103.mine = f32[32,56]{1,0:T(8,128)S(1)} custom-call(f32[16,1024]{1,0:T(8,128)S(1)} %get-tuple-element.37.adj, f32[16,1024]{1,0:T(8,128)S(1)} %collective-permute-done.6.came, bf16[128,1024]{1,0:T(8,128)(2,1)S(1)} %bitcast.15, bf16[128,1024]{1,0:T(8,128)(2,1)S(1)} %bitcast.20, bf16[128,1024]{1,0:T(8,128)(2,1)S(1)} %collective-permute-done.2.refs_2_.o_my, ...), custom_call_target="tpu_custom_call" | custom-call | flops 500000000 | bytes 2000000 | tf_op jit(solution)/shard_map/pallas_call | solution.py:380
  39.1 0.1 shard_map.105
  39.2 18.0 %all_to_all.10.refs_0_ = bf16[64,16,128]{2,1,0:T(8,128)(2,1)S(1)} all-to-all(bf16[64,16,128]{2,1,0:T(8,128)(2,1)S(1)} %shard_map.105), channel_id=1, replica_groups={{0,1,2,3,4,5,6,7,8,9,10,11,12,13,14,15,16,17,18,19,20,21,22,23,24,25,26..., dimensions={0} | all-to-all | bytes 524288 | tf_op jit(solution)/shard_map/all_to_all | solution.py:388
  57.3 0.8 %shard_map.106 = (f32[16,112]{1,0:T(8,128)}, f32[1,256,128]{2,1,0:T(8,128)}) custom-call(bf16[64,16,128]{2,1,0:T(8,128)(2,1)S(1)} %all_to_all.10.refs_0_, f32[64,112]{1,0:T(8,128)S(1)} %bitcast.22, f32[256,128]{1,0:T(8,128)S(1)} %get-tuple-element.40.refs_2_, f32[256,128]{1,0:T(8,128)S(1)} %get-tuple-element.41.refs_3_), custom_call_target="tpu_custom_call" | custom-call | flops 1000000 | bytes 600000 | tf_op jit(solution)/shard_map/pallas_call | solution.py:390
  (11 shorter events, 0.0 us)
Async XLA Ops:
  2.0 14.7 %collective-permute-start.1 = (bf16[224,1024]{1,0:T(8,128)(2,1)S(1)}, bf16[224,1024]{1,0:T(8,128)(2,1)S(1)}, u32[]{:S(2)}, u32[]{:S(2)}) collective-permute-start(bf16[224,1024]{1,0:T(8,128)(2,1)S(1)} %bitcast.16), channel_id=1, source_target_pairs={{0,32},{32,0},{64,96},{96,64},{1,33},{33,1},{65,97},{97,65},{2,34}... | collective-permute-start | bytes 1376264 | tf_op jit(solution)/shard_map/ppermute | solution.py:319
  2.1 14.6 %collective-permute-start = (bf16[128,1024]{1,0:T(8,128)(2,1)S(1)}, bf16[128,1024]{1,0:T(8,128)(2,1)S(1)}, u32[]{:S(2)}, u32[]{:S(2)}) collective-permute-start(bf16[128,1024]{1,0:T(8,128)(2,1)S(1)} %bitcast.18), channel_id=1, source_target_pairs={{0,32},{32,0},{64,96},{96,64},{1,33},{33,1},{65,97},{97,65},{2,34}... | collective-permute-start | bytes 786440 | tf_op jit(solution)/shard_map/ppermute | solution.py:319
  2.6 15.5 %collective-permute-start.2 = (bf16[128,1024]{1,0:T(8,128)(2,1)S(1)}, bf16[128,1024]{1,0:T(8,128)(2,1)S(1)}, u32[]{:S(2)}, u32[]{:S(2)}) collective-permute-start(bf16[128,1024]{1,0:T(8,128)(2,1)S(1)} %bitcast.12), channel_id=1, source_target_pairs={{0,64},{32,96},{64,0},{96,32},{1,65},{33,97},{65,1},{97,33},{2,66}... | collective-permute-start | bytes 786440 | tf_op jit(solution)/shard_map/ppermute | solution.py:319
  6.6 11.6 %collective-permute-start.3 = (bf16[128,1024]{1,0:T(8,128)(2,1)S(1)}, bf16[128,1024]{1,0:T(8,128)(2,1)S(1)}, u32[]{:S(2)}, u32[]{:S(2)}) collective-permute-start(bf16[128,1024]{1,0:T(8,128)(2,1)S(1)} %bitcast.19), channel_id=1, source_target_pairs={{0,96},{32,64},{64,32},{96,0},{1,97},{33,65},{65,33},{97,1},{2,98}... | collective-permute-start | bytes 786440 | tf_op jit(solution)/shard_map/ppermute | solution.py:319
  8.4 18.0 %all-to-all-start = ((bf16[32,16,256]{2,1,0:T(8,128)(2,1)}), bf16[32,16,256]{2,1,0:T(8,128)(2,1)S(1)}, u32[]{:S(2)}, u32[]{:S(2)}) async-start(bf16[32,16,256]{2,1,0:T(8,128)(2,1)} %shard_map.98), calls=%async_computation | async-start | bytes 524288 | tf_op jit(solution)/shard_map/all_to_all | solution.py:334
  16.2 21.3 %collective-permute-start.8 = (bf16[224,1024]{1,0:T(8,128)(2,1)S(1)}, bf16[224,1024]{1,0:T(8,128)(2,1)S(1)}, u32[]{:S(2)}, u32[]{:S(2)}) collective-permute-start(bf16[224,1024]{1,0:T(8,128)(2,1)S(1)} %bitcast.8), channel_id=1, source_target_pairs={{0,32},{32,0},{64,96},{96,64},{1,33},{33,1},{65,97},{97,65},{2,34}... | collective-permute-start | bytes 1376264 | tf_op jit(solution)/shard_map/ppermute | solution.py:319
  18.6 11.5 %collective-permute-start.4 = (f32[8,1024]{1,0:T(8,128)S(1)}, f32[8,1024]{1,0:T(8,128)S(1)}, u32[]{:S(2)}, u32[]{:S(2)}) collective-permute-start(f32[8,1024]{1,0:T(8,128)S(1)} %shard_map.97._.a), channel_id=1, source_target_pairs={{0,64},{32,96},{64,0},{96,32},{1,65},{33,97},{65,1},{97,33},{2,66}... | collective-permute-start | bytes 98312 | tf_op jit(solution)/shard_map/ppermute | solution.py:319
  30.1 1.3 %collective-permute-start.5 = (bf16[8,1024]{1,0:T(8,128)(2,1)S(1)}, bf16[8,1024]{1,0:T(8,128)(2,1)S(1)}, u32[]{:S(2)}, u32[]{:S(2)}) collective-permute-start(bf16[8,1024]{1,0:T(8,128)(2,1)S(1)} %shard_map.100.inc_my), channel_id=1, source_target_pairs={{0,32},{32,0},{64,96},{96,64},{1,33},{33,1},{65,97},{97,65},{2,34}... | collective-permute-start | bytes 49160 | tf_op jit(solution)/shard_map/ppermute | solution.py:319
  31.4 6.8 %collective-permute-start.7 = (bf16[128,1024]{1,0:T(8,128)(2,1)S(1)}, bf16[128,1024]{1,0:T(8,128)(2,1)S(1)}, u32[]{:S(2)}, u32[]{:S(2)}) collective-permute-start(bf16[128,1024]{1,0:T(8,128)(2,1)S(1)} %shard_map.102), channel_id=1, source_target_pairs={{0,32},{32,0},{64,96},{96,64},{1,33},{33,1},{65,97},{97,65},{2,34}... | collective-permute-start | bytes 786440 | tf_op jit(solution)/shard_map/ppermute | solution.py:319
  36.8 20.4 %copy-start = (f32[112,64]{0,1:T(8,128)S(1)}, f32[112,64]{0,1:T(8,128)}, u32[]{:S(2)}) copy-start(f32[112,64]{0,1:T(8,128)} %param.10) | copy-start | bytes 86020
  36.9 1.3 %collective-permute-start.6 = (f32[16,1024]{1,0:T(8,128)S(1)}, f32[16,1024]{1,0:T(8,128)S(1)}, u32[]{:S(2)}, u32[]{:S(2)}) collective-permute-start(f32[16,1024]{1,0:T(8,128)S(1)} %get-tuple-element.37.adj), channel_id=1, source_target_pairs={{0,32},{32,0},{64,96},{96,64},{1,33},{33,1},{65,97},{97,65},{2,34}... | collective-permute-start | bytes 196616 | tf_op jit(solution)/shard_map/ppermute | solution.py:319

commit v12 on v11

--- a/solution.py
+++ b/solution.py
@@ -141,14 +141,14 @@
         out[:, cut] = before[:, cut] + increment_of(scale, kron[...], ma, mb, ea, eb, cut)
 
 
-def prep_body(cols_s, own_s, interpolation, got, innovation, obs_weight, _,
-              onehot, onehot_t, place_hi, place_lo, interp, innov, weight, innov_own, live_own, sem):
+def prep_body(cols_s, own_s, interpolation, got_in, innovation, obs_weight, _,
+              onehot, onehot_t, place_hi, place_lo, interp, innov, weight, innov_own, live_own, got, sem):
     band = lax.axis_index("band")
     tile = lax.axis_index("mem")
     quarter = pl.ds(pl.multiple_of(band * 128, 128), 128)
     mid = [(innovation.at[0, :, quarter], innov_own), (obs_weight.at[0, :, quarter], live_own)]
     big = [(interpolation.at[:32, :, quarter_at(side)], interp.at[:, :, side * 128:(side + 1) * 128]) for side in range(2)]
-    copies = start_all([pltpu.make_async_copy(a, b, sem.at[n]) for n, (a, b) in enumerate(mid + big)])
+    copies = start_all([pltpu.make_async_copy(a, b, sem.at[n]) for n, (a, b) in enumerate([(got_in, got)] + mid + big)])
     t = iota((64, 1024), 1)
     cols = cols_s[...].astype(F32).T.astype(jnp.int32)
     for c in range(16):
@@ -168,6 +168,7 @@
     half = 4 * (band >> 1)
     place_hi[...] = ones_where((target == slot + half) & ((slot & 7) < 4))
     place_lo[...] = ones_where((target == slot + half - 4) & ((slot & 7) >= 4))
+    copies[0].wait()
     x = got[...].astype(F32)
     innov[...] = dot(sel, x[:, :8].reshape(256, 256).astype(BF))
     weight[...] = dot(sel, x[:, 8:].reshape(256, 256).astype(BF))
@@ -177,9 +178,9 @@
     side = jnp.where((iota((256, 128), 1) >> 6) == odd, dot(pair, hit), 0.0)
     count = jnp.sum(side, axis=1, keepdims=True)
     live = jnp.where((iota((256, 1), 0) & 7).astype(F32) < count, 1.0, 0.0)
-    wait_all(copies[:2])
+    wait_all(copies[1:3])
     live_own[...] = live * live_own[...]
-    wait_all(copies[2:])
+    wait_all(copies[3:])
 
 
 def add_body(a, b, _, out):
@@ -348,13 +349,13 @@
 
     kept = call(
         prep_body,
-        [VM, VM, HB, VM, HB, HB, ANY],
+        [VM, VM, HB, ANY, HB, HB, ANY],
         [(pltpu.VMEM(d, t), VM) for d, t in (
             ((1024, 1024), BF), ((1024, 1024), BF), ((64, 256), BF), ((64, 256), BF), ((32, 256, 256), BF), ((64, 256), F32), ((64, 256), F32),
             ((256, 128), F32), ((256, 128), F32))],
         10 ** 8, 12 * 10 ** 6,
-        [dma((4,))],
-    )(in_vmem(columns_v), in_vmem(owners_v), in_hbm(interpolation), in_vmem(got), in_hbm(innovation), in_hbm(obs_weight), part)
+        [pltpu.VMEM((32, 16, 256), BF), dma((5,))],
+    )(in_vmem(columns_v), in_vmem(owners_v), in_hbm(interpolation), got, in_hbm(innovation), in_hbm(obs_weight), part)
     onehot, onehot_t, place_hi, place_lo, interp, innov, weight, innov_own, live_own = [in_vmem(a) for a in kept]
 
     (inc_my,) = call(

time: 58.4 us -> 57.8 us (0.990)
  transfers between devices with their start and end apart: 10 -> 10, of which waited for: 3 -> 3; matrix products, arithmetic and copies ran while one was open for 0% -> 0% of each run, Pallas kernels for 22% -> 21%
where the time goes in v12:
time: 57.8 us; the launch traced here: 57.5 us
  blocking collectives  18 us (31%)
  starting transfers between devices  17.1 us (30%)
  Pallas kernels  15.5 us (27%)
  waiting for transfers between devices  6.07 us (11%)
  between operations  0.76 us (1%)
    all_to_all x1, blocking collectives, per_device(): lax.all_to_all(sent, ('band', 'mem'), split_axis=0, concat_axis=0, axis_i...  18 us
    ppermute x9, starting transfers between devices, over(): return lax.ppermute(x, 'band', [(i, i ^ bit) for i in range(4)])  9.31 us
    all_to_all x1, starting transfers between devices, per_device(): lax.all_to_all(payload, 'mem', split_axis=0, concat_axis=0, tiled=True)  7.8 us
    pallas_call x1, Pallas kernels, per_device(): call(obs_body, [VM] * 7 + [HB], [(shape((16, 1024), F32), VM), (pltpu.VME...  5.3 us
    all_to_all x1, waiting for transfers between devices, per_device(): lax.all_to_all(payload, 'mem', split_axis=0, concat_axis=0, tiled=True)  4.19 us
    pallas_call x1, Pallas kernels, per_device(): call(prep_body, [VM, VM, HB, ANY, HB, HB, ANY], [(pltpu.VMEM(d, t), VM) f...  3.09 us
    ppermute x9, waiting for transfers between devices, over(): return lax.ppermute(x, 'band', [(i, i ^ bit) for i in range(4)])  1.88 us
    pallas_call x1, Pallas kernels, per_device(): call(load_body, [HB] * 2 + [ANY], [(pltpu.HBM((32, 16, 256), BF), VM)], 0...  1.84 us
  transfers between devices with their start and end apart: 10, of which 3 were waited for; matrix products, arithmetic and copies ran while one was open for 0% of the time, Pallas kernels for 21%

profile of v12, /device:TPU:0, one launch (start us, length us, event | category | flops | bytes accessed | tf_op | source)
XLA Modules:
  0.0 57.5 jit_solution(6674457082302015535)
XLA Ops:
  0.6 1.4 %shard_map.95 = (bf16[16,8,1024]{2,1,0:T(8,128)(2,1)S(1)}, bf16[16,8,1024]{2,1,0:T(8,128)(2,1)S(1)}, bf16[28,8,1024]{2,1,0:T(8,128)(2,1)S(1)}, bf16[28,8,1024]{2,1,0:T(8,128)(2,1)S(1)}) custom-call(bf16[16,16,1024]{2,1,0:T(8,128)(2,1)} %mem.1, bf16[28,16,1024]{2,1,0:T(8,128)(2,1)} %eig.1), custom_call_target="tpu_custom_call" | custom-call | tf_op jit(solution)/shard_map/pallas_call | solution.py:323
  2.0 0.1 collective-permute-start.1
  2.1 0.5 collective-permute-start
  2.6 4.0 %collective-permute-start.2 = (bf16[128,1024]{1,0:T(8,128)(2,1)S(1)}, bf16[128,1024]{1,0:T(8,128)(2,1)S(1)}, u32[]{:S(2)}, u32[]{:S(2)}) collective-permute-start(bf16[128,1024]{1,0:T(8,128)(2,1)S(1)} %bitcast.12), channel_id=1, source_target_pairs={{0,64},{32,96},{64,0},{96,32},{1,65},{33,97},{65,1},{97,33},{2,66}... | collective-permute-start | bytes 786440 | tf_op jit(solution)/shard_map/ppermute | solution.py:320
  6.6 1.8 %shard_map.98 = bf16[32,16,256]{2,1,0:T(8,128)(2,1)} custom-call(f32[1,256,512]{2,1,0:T(8,128)} %innovation.3, f32[1,256,512]{2,1,0:T(8,128)} %obs_weight.3, bf16[128,1024]{1,0:T(8,128)(2,1)S(1)} %bitcast.13), custom_call_target="tpu_custom_call" | custom-call | tf_op jit(solution)/shard_map/pallas_call | solution.py:331
  8.4 7.8 %all-to-all-start = ((bf16[32,16,256]{2,1,0:T(8,128)(2,1)}), bf16[32,16,256]{2,1,0:T(8,128)(2,1)S(1)}, u32[]{:S(2)}, u32[]{:S(2)}) async-start(bf16[32,16,256]{2,1,0:T(8,128)(2,1)} %shard_map.98), calls=%async_computation | async-start | bytes 524288 | tf_op jit(solution)/shard_map/all_to_all | solution.py:335
  16.2 0.5 collective-permute-start.8
  16.7 1.5 %shard_map.96 = (f32[8,1024]{1,0:T(8,128)S(1)}, bf16[448,256]{1,0:T(8,128)(2,1)S(1)}, s32[16,64]{1,0:T(8,128)S(1)}, s32[16,128]{1,0:T(8,128)S(1)}) custom-call(f32[64,112]{1,0:T(8,128)} %bitcast.21, s32[16,64]{1,0:T(8,128)} %bitcast.23, s32[16,128]{1,0:T(8,128)} %bitcast.24, bf16[128,1024]{1,0:T(8,128)(2,1)S(1)} %bitcast.14, ...), custom_call_target="tpu_custom_call" | custom-call | flops 250000000 | bytes 2000000 | tf_op jit(solution)/shard_map/pallas_call | solution.py:339
  18.1 0.0 collective-permute-done.3.refs_3_.x
  18.2 0.4 shard_map.97._.a
  18.6 3.6 %collective-permute-start.4 = (f32[8,1024]{1,0:T(8,128)S(1)}, f32[8,1024]{1,0:T(8,128)S(1)}, u32[]{:S(2)}, u32[]{:S(2)}) collective-permute-start(f32[8,1024]{1,0:T(8,128)S(1)} %shard_map.97._.a), channel_id=1, source_target_pairs={{0,64},{32,96},{64,0},{96,32},{1,65},{33,97},{65,1},{97,33},{2,66}... | collective-permute-start | bytes 98312 | tf_op jit(solution)/shard_map/ppermute | solution.py:320
  22.2 4.2 %all-to-all-done.got_in = bf16[32,16,256]{2,1,0:T(8,128)(2,1)S(1)} async-done(((bf16[32,16,256]{2,1,0:T(8,128)(2,1)}), bf16[32,16,256]{2,1,0:T(8,128)(2,1)S(1)}, u32[]{:S(2)}, u32[]{:S(2)}) %all-to-all-start) | async-done | bytes 262176 | tf_op jit(solution)/shard_map/all_to_all | solution.py:335
  26.4 3.1 %shard_map.99 = (bf16[1024,1024]{1,0:T(8,128)(2,1)S(1)}, bf16[1024,1024]{1,0:T(8,128)(2,1)S(1)}, bf16[64,256]{1,0:T(8,128)(2,1)S(1)}, bf16[64,256]{1,0:T(8,128)(...) custom-call(s32[16,64]{1,0:T(8,128)S(1)} %get-tuple-element.29.cols_, ...), custom_call_target="tpu_custom_call" | custom-call | flops 100000000 | bytes 12000000 | tf_op jit(solution)/shard_map/pallas_call | solution.py:350
  29.6 0.1 collective-permute-start.5
  29.7 1.2 %collective-permute-done.5.inc_mt._ = bf16[8,1024]{1,0:T(8,128)(2,1)S(1)} collective-permute-done((bf16[8,1024]{1,0:T(8,128)(2,1)S(1)}, bf16[8,1024]{1,0:T(8,128)(2,1)S(1)}, u32[]{:S(2)}, u32[]{:S(2)}) %collective-permute-start.5) | collective-permute-done | bytes 16416 | tf_op jit(solution)/shard_map/ppermute | solution.py:320
  30.8 0.2 collective-permute-start.7
  31.0 5.3 %shard_map.101 = (f32[16,1024]{1,0:T(8,128)S(1)}, f32[64,256]{1,0:T(8,128)S(1)}) custom-call(bf16[8,1024]{1,0:T(8,128)(2,1)S(1)} %shard_map.100.inc_my, bf16[8,1024]{1,0:T(8,128)(2,1)S(1)} %collective-permute-done.5.inc_mt._, bf16[1024,1024]{1,0:T(8,128)(2,1)S(1)} %get-tuple-element.32.onehot, bf16[1024,1024]{1,0:T(8,128)(2,1)S(1)} %get-tuple-element.33.onehot_t, ...), custom_call_target="tpu_custom_call" | custom-call | flops 1000000000 | bytes 12000000 | tf_op jit(solution)/shard_map/pallas_call | solution.py:368
  36.3 0.4 collective-permute-start.6
  36.7 0.2 shard_map.104.slots
  37.0 0.6 %collective-permute-done.6.came = f32[16,1024]{1,0:T(8,128)S(1)} collective-permute-done((f32[16,1024]{1,0:T(8,128)S(1)}, f32[16,1024]{1,0:T(8,128)S(1)}, u32[]{:S(2)}, u32[]{:S(2)}) %collective-permute-start.6) | collective-permute-done | bytes 65568 | tf_op jit(solution)/shard_map/ppermute | solution.py:320
  37.6 0.9 %shard_map.103.mine = f32[32,56]{1,0:T(8,128)S(1)} custom-call(f32[16,1024]{1,0:T(8,128)S(1)} %get-tuple-element.37.adj, f32[16,1024]{1,0:T(8,128)S(1)} %collective-permute-done.6.came, bf16[128,1024]{1,0:T(8,128)(2,1)S(1)} %bitcast.15, bf16[128,1024]{1,0:T(8,128)(2,1)S(1)} %bitcast.20, bf16[128,1024]{1,0:T(8,128)(2,1)S(1)} %collective-permute-done.2.refs_2_.o_my, ...), custom_call_target="tpu_custom_call" | custom-call | flops 500000000 | bytes 2000000 | tf_op jit(solution)/shard_map/pallas_call | solution.py:381
  38.5 0.1 shard_map.105
  38.7 18.0 %all_to_all.10.refs_0_ = bf16[64,16,128]{2,1,0:T(8,128)(2,1)S(1)} all-to-all(bf16[64,16,128]{2,1,0:T(8,128)(2,1)S(1)} %shard_map.105), channel_id=1, replica_groups={{0,1,2,3,4,5,6,7,8,9,10,11,12,13,14,15,16,17,18,19,20,21,22,23,24,25,26..., dimensions={0} | all-to-all | bytes 524288 | tf_op jit(solution)/shard_map/all_to_all | solution.py:389
  56.7 0.8 %shard_map.106 = (f32[16,112]{1,0:T(8,128)}, f32[1,256,128]{2,1,0:T(8,128)}) custom-call(bf16[64,16,128]{2,1,0:T(8,128)(2,1)S(1)} %all_to_all.10.refs_0_, f32[64,112]{1,0:T(8,128)S(1)} %bitcast.22, f32[256,128]{1,0:T(8,128)S(1)} %get-tuple-element.40.refs_2_, f32[256,128]{1,0:T(8,128)S(1)} %get-tuple-element.41.refs_3_), custom_call_target="tpu_custom_call" | custom-call | flops 1000000 | bytes 600000 | tf_op jit(solution)/shard_map/pallas_call | solution.py:391
  (11 shorter events, 0.0 us)
Async XLA Ops:
  2.0 14.7 %collective-permute-start.1 = (bf16[224,1024]{1,0:T(8,128)(2,1)S(1)}, bf16[224,1024]{1,0:T(8,128)(2,1)S(1)}, u32[]{:S(2)}, u32[]{:S(2)}) collective-permute-start(bf16[224,1024]{1,0:T(8,128)(2,1)S(1)} %bitcast.16), channel_id=1, source_target_pairs={{0,32},{32,0},{64,96},{96,64},{1,33},{33,1},{65,97},{97,65},{2,34}... | collective-permute-start | bytes 1376264 | tf_op jit(solution)/shard_map/ppermute | solution.py:320
  2.1 14.6 %collective-permute-start = (bf16[128,1024]{1,0:T(8,128)(2,1)S(1)}, bf16[128,1024]{1,0:T(8,128)(2,1)S(1)}, u32[]{:S(2)}, u32[]{:S(2)}) collective-permute-start(bf16[128,1024]{1,0:T(8,128)(2,1)S(1)} %bitcast.18), channel_id=1, source_target_pairs={{0,32},{32,0},{64,96},{96,64},{1,33},{33,1},{65,97},{97,65},{2,34}... | collective-permute-start | bytes 786440 | tf_op jit(solution)/shard_map/ppermute | solution.py:320
  2.6 15.5 %collective-permute-start.2 = (bf16[128,1024]{1,0:T(8,128)(2,1)S(1)}, bf16[128,1024]{1,0:T(8,128)(2,1)S(1)}, u32[]{:S(2)}, u32[]{:S(2)}) collective-permute-start(bf16[128,1024]{1,0:T(8,128)(2,1)S(1)} %bitcast.12), channel_id=1, source_target_pairs={{0,64},{32,96},{64,0},{96,32},{1,65},{33,97},{65,1},{97,33},{2,66}... | collective-permute-start | bytes 786440 | tf_op jit(solution)/shard_map/ppermute | solution.py:320
  6.6 11.6 %collective-permute-start.3 = (bf16[128,1024]{1,0:T(8,128)(2,1)S(1)}, bf16[128,1024]{1,0:T(8,128)(2,1)S(1)}, u32[]{:S(2)}, u32[]{:S(2)}) collective-permute-start(bf16[128,1024]{1,0:T(8,128)(2,1)S(1)} %bitcast.19), channel_id=1, source_target_pairs={{0,96},{32,64},{64,32},{96,0},{1,97},{33,65},{65,33},{97,1},{2,98}... | collective-permute-start | bytes 786440 | tf_op jit(solution)/shard_map/ppermute | solution.py:320
  8.4 18.0 %all-to-all-start = ((bf16[32,16,256]{2,1,0:T(8,128)(2,1)}), bf16[32,16,256]{2,1,0:T(8,128)(2,1)S(1)}, u32[]{:S(2)}, u32[]{:S(2)}) async-start(bf16[32,16,256]{2,1,0:T(8,128)(2,1)} %shard_map.98), calls=%async_computation | async-start | bytes 524288 | tf_op jit(solution)/shard_map/all_to_all | solution.py:335
  16.2 20.8 %collective-permute-start.8 = (bf16[224,1024]{1,0:T(8,128)(2,1)S(1)}, bf16[224,1024]{1,0:T(8,128)(2,1)S(1)}, u32[]{:S(2)}, u32[]{:S(2)}) collective-permute-start(bf16[224,1024]{1,0:T(8,128)(2,1)S(1)} %bitcast.8), channel_id=1, source_target_pairs={{0,32},{32,0},{64,96},{96,64},{1,33},{33,1},{65,97},{97,65},{2,34}... | collective-permute-start | bytes 1376264 | tf_op jit(solution)/shard_map/ppermute | solution.py:320
  18.6 10.9 %collective-permute-start.4 = (f32[8,1024]{1,0:T(8,128)S(1)}, f32[8,1024]{1,0:T(8,128)S(1)}, u32[]{:S(2)}, u32[]{:S(2)}) collective-permute-start(f32[8,1024]{1,0:T(8,128)S(1)} %shard_map.97._.a), channel_id=1, source_target_pairs={{0,64},{32,96},{64,0},{96,32},{1,65},{33,97},{65,1},{97,33},{2,66}... | collective-permute-start | bytes 98312 | tf_op jit(solution)/shard_map/ppermute | solution.py:320
  29.6 1.3 %collective-permute-start.5 = (bf16[8,1024]{1,0:T(8,128)(2,1)S(1)}, bf16[8,1024]{1,0:T(8,128)(2,1)S(1)}, u32[]{:S(2)}, u32[]{:S(2)}) collective-permute-start(bf16[8,1024]{1,0:T(8,128)(2,1)S(1)} %shard_map.100.inc_my), channel_id=1, source_target_pairs={{0,32},{32,0},{64,96},{96,64},{1,33},{33,1},{65,97},{97,65},{2,34}... | collective-permute-start | bytes 49160 | tf_op jit(solution)/shard_map/ppermute | solution.py:320
  30.8 6.8 %collective-permute-start.7 = (bf16[128,1024]{1,0:T(8,128)(2,1)S(1)}, bf16[128,1024]{1,0:T(8,128)(2,1)S(1)}, u32[]{:S(2)}, u32[]{:S(2)}) collective-permute-start(bf16[128,1024]{1,0:T(8,128)(2,1)S(1)} %shard_map.102), channel_id=1, source_target_pairs={{0,32},{32,0},{64,96},{96,64},{1,33},{33,1},{65,97},{97,65},{2,34}... | collective-permute-start | bytes 786440 | tf_op jit(solution)/shard_map/ppermute | solution.py:320
  36.3 20.4 %copy-start = (f32[112,64]{0,1:T(8,128)S(1)}, f32[112,64]{0,1:T(8,128)}, u32[]{:S(2)}) copy-start(f32[112,64]{0,1:T(8,128)} %param.10) | copy-start | bytes 86020
  36.3 1.3 %collective-permute-start.6 = (f32[16,1024]{1,0:T(8,128)S(1)}, f32[16,1024]{1,0:T(8,128)S(1)}, u32[]{:S(2)}, u32[]{:S(2)}) collective-permute-start(f32[16,1024]{1,0:T(8,128)S(1)} %get-tuple-element.37.adj), channel_id=1, source_target_pairs={{0,32},{32,0},{64,96},{96,64},{1,33},{33,1},{65,97},{97,65},{2,34}... | collective-permute-start | bytes 196616 | tf_op jit(solution)/shard_map/ppermute | solution.py:320
